TPU v7x, 32 devices: a whole 2x2x4 slice. The times are simulated.
32 devices in a mesh: row: 8 (over z, x), col: 4 (over y, core).
Axes of the slice: x: 2, y: 2, z: 4, core: 2. Of those that a mesh axis runs over, the one named last changes fastest.
Arguments:
- iterate: float32 [3584, 9216], P('row', 'col'), may hold values from -0.09375 to 0.09375
Outputs:
- update: float32 [3584, 9216], P('row', 'col')
All inputs are finite; a program needn't handle non-finite values.
Results may differ from a plain program's by a relative error of at most 0.000068.
Values sent between devices are 32-bit elements; how exact they have to be, the bound alone decides.
A program may use at most 128 MiB of HBM per device.

v0:
```python
import math

import jax
import jax.numpy as jnp
from jax import lax
from jax.sharding import PartitionSpec as P

M = 3584
N = 9216


HIGHEST_PREC = lax.Precision.HIGHEST
COEF_A = 3.4445
COEF_B = -4.775
COEF_C = 2.0315


def matmul(left, right):
    return jnp.dot(left, right, precision=HIGHEST_PREC, preferred_element_type=jnp.float32)


def body(iterate):
    col_count = lax.axis_size("col")
    slab_all = lax.all_gather(iterate, "row", axis=0, tiled=True)
    partial_value = matmul(iterate, slab_all.T)
    gram_panel = lax.psum(partial_value, "col")
    tile_width = gram_panel.shape[1] // col_count
    my_col = lax.axis_index("col")
    gram_tile = lax.dynamic_slice_in_dim(gram_panel, my_col * tile_width, tile_width, 1)
    gram_column = lax.all_gather(gram_tile, "row", axis=0, tiled=True)
    square_tile = matmul(gram_panel, gram_column)
    poly_tile = COEF_B * gram_tile + COEF_C * square_tile
    poly_panel = lax.all_gather(poly_tile, "col", axis=1, tiled=True)
    applied = matmul(poly_panel, slab_all)
    return (COEF_A * iterate + applied) * (0.2 * math.sqrt(max(M, N)))


def solution(mesh):
    placed = (P("row", "col"),)
    return jax.shard_map(
        body, mesh=mesh, in_specs=placed, out_specs=P("row", "col"), check_vma=False
    )
```

profile of v0, /device:TPU:0, one launch (start us, length us, event | category | flops | bytes accessed | tf_op | source)
XLA Modules:
  0.0 1129.4 jit_solution(1441939671965194359)
XLA Ops:
  6.5 0.0 all-gather.4.cloned.1.call-start
  6.5 0.7 all-gather.4.cloned.1.call-update
  7.3 0.0 all-reduce.2.cloned.1.call-start
  7.3 632.2 %all-gather.4.cloned.1.call-done = f32[3584,2304]{1,0:T(8,128)} async-done(((f32[448,2304]{1,0:T(8,128)}), f32[3584,2304]{1,0:T(8,128)}) %all-gather.4.cloned.1.call-update) | async-done | bytes 33030160 | tf_op jit(solution)/shard_map/all_gather | solution.py:24
  639.5 52.2 %fusion.1 = f32[448,3584]{1,0:T(8,128)} fusion(f32[448,2304]{1,0:T(8,128)} %param.1, f32[3584,2304]{1,0:T(8,128)} %all-gather.4.cloned.1.call-done), kind=kOutput, calls=%fused_computation.4 | convolution fusion | flops 44392513536 | bytes 43581440 | tf_op jit(solution)/shard_map/dot_general | solution.py:19
  691.7 0.0 all-reduce.2.cloned.1.call-update
  691.8 0.0 all-gather.6.cloned.1.call-start
  691.8 121.8 %all-reduce.2.cloned.1.call-done = f32[448,3584]{1,0:T(8,128)} async-done(((f32[448,3584]{1,0:T(8,128)}), f32[448,3584]{1,0:T(8,128)}) %all-reduce.2.cloned.1.call-update) | async-done | bytes 6422544 | tf_op jit(solution)/shard_map/psum | solution.py:26
  813.6 2.7 constant_dynamic-slice_fusion
  816.3 0.0 all-gather.6.cloned.1.call-update
  816.3 0.2 all-gather.8.cloned.1.call-start
  816.5 179.8 %all-gather.6.cloned.1.call-done = f32[3584,896]{1,0:T(8,128)} async-done(((f32[448,896]{1,0:T(8,128)}), f32[3584,896]{1,0:T(8,128)}) %all-gather.6.cloned.1.call-update) | async-done | bytes 12845072 | tf_op jit(solution)/shard_map/all_gather | solution.py:30
  996.3 26.6 %multiply_add_fusion = f32[448,896]{1,0:T(8,128)} fusion(f32[448,896]{1,0:T(8,128)} %constant_dynamic-slice_fusion, f32[448,3584]{1,0:T(8,128)} %all-reduce.2.cloned.1.call-done, f32[3584,896]{1,0:T(8,128)} %all-gather.6.cloned.1.call-done), kind=kOutput, calls=%fused_computation.2 | convolution fusion | flops 17264959488 | bytes 22478848 | tf_op jit(solution)/shard_map/dot_general | solution.py:19
  1022.9 0.0 all-gather.8.cloned.1.call-update
  1022.9 45.5 %all-gather.8.cloned.1.call-done = f32[448,3584]{1,0:T(8,128)} async-done(((f32[448,896]{1,0:T(8,128)}), f32[448,3584]{1,0:T(8,128)}) %all-gather.8.cloned.1.call-update) | async-done | bytes 6422544 | tf_op jit(solution)/shard_map/all_gather | solution.py:33
  1068.4 54.5 %fusion = f32[448,2304]{1,0:T(8,128)} fusion(f32[448,3584]{1,0:T(8,128)} %all-gather.8.cloned.1.call-done, f32[3584,2304]{1,0:T(8,128)} %all-gather.4.cloned.1.call-done, f32[448,2304]{1,0:T(8,128)} %param.1), kind=kOutput, calls=%fused_computation.1 | convolution fusion | flops 44395610112 | bytes 47710208 | tf_op jit(solution)/shard_map/dot_general | solution.py:19
Async XLA Ops:
  6.5 633.0 %all-gather.4.cloned.1.call-start = ((), (), s32[]{:S(2)}) async-start(), calls=%async_computation | async-start | bytes 37158912 | tf_op jit(solution)/shard_map/all_gather | solution.py:24
  7.3 806.3 %all-reduce.2.cloned.1.call-start = ((), (), s32[]{:S(2)}) async-start(), calls=%async_computation.1 | async-start | bytes 12845056 | tf_op jit(solution)/shard_map/psum | solution.py:26
  691.8 304.5 %all-gather.6.cloned.1.call-start = ((), (), s32[]{:S(2)}) async-start(), calls=%async_computation.2 | async-start | bytes 14450688 | tf_op jit(solution)/shard_map/all_gather | solution.py:30
  816.3 252.1 %all-gather.8.cloned.1.call-start = ((), (), s32[]{:S(2)}) async-start(), calls=%async_computation.3 | async-start | bytes 8028160 | tf_op jit(solution)/shard_map/all_gather | solution.py:33
Sparse Core Ops, SparseCore 0:
  8.9 630.5 all-gather.3
  691.9 121.6 all-reduce.1
  816.4 179.8 all-gather.5
  1023.0 45.3 all-gather.7
where the time goes:
time: 1130 us
  waiting for transfers between devices  980 us (87%)
  matrix products  133 us (12%)
  between operations  13.1 us (1%)
    all_gather x1, waiting for transfers between devices, body(): slab_all = lax.all_gather(iterate, 'row', axis=0, tiled=True)  632 us
    all_gather x1, waiting for transfers between devices, body(): gram_column = lax.all_gather(gram_tile, 'row', axis=0, tiled=True)  180 us
    dot_general x3, matrix products, matmul(): jnp.dot(left, right, precision=HIGHEST_PREC, preferred_element_type=jnp.f...  133 us
    psum x1, waiting for transfers between devices, body(): gram_panel = lax.psum(partial_value, 'col')  122 us
    all_gather x1, waiting for transfers between devices, body(): poly_panel = lax.all_gather(poly_tile, 'col', axis=1, tiled=True)  45.5 us
  transfers between devices with their start and end apart: 4, of which 4 were waited for; matrix products, arithmetic and copies ran while one was open for 0% of the time, Pallas kernels for 0%

commit v1 on v0

v1 whole, which is shorter than its diff:
```python
import math

import jax
import jax.numpy as jnp
from jax import lax
from jax.sharding import PartitionSpec as P

PREC = lax.Precision.HIGH
COEF_A = 3.4445
COEF_B = -4.775
COEF_C = 2.0315
CHUNKS = 3


def matmul(left, right):
    return jnp.dot(left, right, precision=PREC, preferred_element_type=jnp.float32)


def body(scale, iterate):
    col_count = lax.axis_size("col")
    width = iterate.shape[1] // CHUNKS
    pieces = [iterate[:, k * width : (k + 1) * width] for k in range(CHUNKS)]
    slabs = [lax.all_gather(piece, "row", axis=0, tiled=True) for piece in pieces]
    partial_value = None
    for piece, slab in zip(pieces, slabs):
        term = matmul(piece, slab.T)
        partial_value = term if partial_value is None else partial_value + term
    gram_panel = lax.psum(partial_value, "col")
    tile_width = gram_panel.shape[1] // col_count
    my_col = lax.axis_index("col")
    gram_tile = lax.dynamic_slice_in_dim(gram_panel, my_col * tile_width, tile_width, 1)
    gram_column = lax.all_gather(gram_tile, "row", axis=0, tiled=True)
    square_tile = matmul(gram_panel, gram_column)
    poly_tile = COEF_B * gram_tile + COEF_C * square_tile
    poly_panel = lax.all_gather(poly_tile, "col", axis=1, tiled=True)
    outs = [
        (COEF_A * piece + matmul(poly_panel, slab)) * scale
        for piece, slab in zip(pieces, slabs)
    ]
    return jnp.concatenate(outs, axis=1)


def solution(mesh):
    placed = P("row", "col")

    def run(iterate):
        scale = 0.2 * math.sqrt(max(iterate.shape))
        return jax.shard_map(
            lambda block: body(scale, block),
            mesh=mesh,
            in_specs=(placed,),
            out_specs=placed,
            check_vma=False,
        )(iterate)

    return run
```

time: 1130 us -> 908 us (0.80)
  waiting for transfers between devices: 980 us -> 795 us
  matrix products: 133 us -> 89.7 us
    all_gather x1 -> x3, waiting for transfers between devices: 632 us -> 448 us  [body(): lax.all_gather(piece, 'row', axis=0, tiled=True)]
    dot_general x3 -> x7, matrix products: 133 us -> 89.7 us  [matmul(): jnp.dot(left, right, precision=PREC, preferred_element_type=jnp.float32)]
  transfers between devices with their start and end apart: 4 -> 6, of which waited for: 4 -> 6; matrix products, arithmetic and copies ran while one was open for 0% -> 3% of each run, Pallas kernels for 0% -> 0%
where the time goes in v1:
time: 908 us
  waiting for transfers between devices  795 us (88%)
  matrix products  89.7 us (10%)
  between operations  13.6 us (1%)
    all_gather x3, waiting for transfers between devices, body(): lax.all_gather(piece, 'row', axis=0, tiled=True)  448 us
    all_gather x1, waiting for transfers between devices, body(): gram_column = lax.all_gather(gram_tile, 'row', axis=0, tiled=True)  180 us
    psum x1, waiting for transfers between devices, body(): gram_panel = lax.psum(partial_value, 'col')  120 us
    dot_general x7, matrix products, matmul(): jnp.dot(left, right, precision=PREC, preferred_element_type=jnp.float32)  89.7 us
    all_gather x1, waiting for transfers between devices, body(): poly_panel = lax.all_gather(poly_tile, 'col', axis=1, tiled=True)  45.5 us
  transfers between devices with their start and end apart: 6, of which 6 were waited for; matrix products, arithmetic and copies ran while one was open for 3% of the time, Pallas kernels for 0%

profile of v1, /device:TPU:0, one launch (start us, length us, event | category | flops | bytes accessed | tf_op | source)
XLA Modules:
  0.0 907.9 jit_solution(12267081114841490817)
XLA Ops:
  6.5 0.0 all-gather.8.cloned.1.call-start
  6.5 4.3 fusion.5
  10.9 0.0 all-gather.8.cloned.1.call-update
  10.9 0.0 all-gather.6.cloned.1.call-start
  11.0 0.7 all-gather.6.cloned.1.call-update
  11.7 0.0 all-gather.10.cloned.1.call-start
  11.7 0.7 all-gather.10.cloned.1.call-update
  12.4 0.0 all-reduce.2.cloned.1.call-start
  12.4 158.6 %all-gather.8.cloned.1.call-done = f32[3584,768]{1,0:T(8,128)} async-done(((f32[448,768]{1,0:T(8,128)}), f32[3584,768]{1,0:T(8,128)}) %all-gather.8.cloned.1.call-update) | async-done | bytes 11010064 | tf_op jit(solution)/shard_map/all_gather | solution.py:23
  171.0 12.7 %fusion.1 = f32[448,3584]{1,0:T(8,128)} fusion(f32[3584,768]{1,0:T(8,128)} %all-gather.8.cloned.1.call-done, f32[448,2304]{1,0:T(8,128)} %param.1), kind=kOutput, calls=%fused_computation.8 | convolution fusion | flops 7398752256 | bytes 18808832 | tf_op jit(solution)/shard_map/dot_general | solution.py:16
  183.8 144.9 %all-gather.6.cloned.1.call-done = f32[3584,768]{1,0:T(8,128)} async-done(((f32[448,768]{1,0:T(8,128)}), f32[3584,768]{1,0:T(8,128)}) %all-gather.6.cloned.1.call-update) | async-done | bytes 11010064 | tf_op jit(solution)/shard_map/all_gather | solution.py:23
  328.7 12.8 %fusion.3 = f32[448,3584]{1,0:T(8,128)} fusion(f32[3584,768]{1,0:T(8,128)} %all-gather.6.cloned.1.call-done, f32[448,2304]{1,0:T(8,128)} %param.1), kind=kOutput, calls=%fused_computation.10 | convolution fusion | flops 7398752256 | bytes 18808832 | tf_op jit(solution)/shard_map/dot_general | solution.py:16
  341.4 144.9 %all-gather.10.cloned.1.call-done = f32[3584,768]{1,0:T(8,128)} async-done(((f32[448,768]{1,0:T(8,128)}), f32[3584,768]{1,0:T(8,128)}) %all-gather.10.cloned.1.call-update) | async-done | bytes 11010064 | tf_op jit(solution)/shard_map/all_gather | solution.py:23
  486.3 15.5 %add_add_fusion = f32[448,3584]{1,0:T(8,128)} fusion(f32[448,3584]{1,0:T(8,128)} %fusion.3, f32[448,3584]{1,0:T(8,128)} %fusion.1, f32[3584,768]{1,0:T(8,128)} %all-gather.10.cloned.1.call-done, f32[448,2304]{1,0:T(8,128)} %param.1), kind=kOutput, calls=%fused_computation | convolution fusion | flops 7401963520 | bytes 31653888 | tf_op jit(solution)/shard_map/dot_general | solution.py:16
  501.8 0.0 all-reduce.2.cloned.1.call-update
  501.9 0.0 all-gather.12.cloned.1.call-start
  501.9 120.0 %all-reduce.2.cloned.1.call-done = f32[448,3584]{1,0:T(8,128)} async-done(((f32[448,3584]{1,0:T(8,128)}), f32[448,3584]{1,0:T(8,128)}) %all-reduce.2.cloned.1.call-update) | async-done | bytes 6422544 | tf_op jit(solution)/shard_map/psum | solution.py:28
  621.9 2.7 constant_dynamic-slice_fusion
  624.6 0.0 all-gather.12.cloned.1.call-update
  624.6 0.0 all-gather.14.cloned.1.call-start
  624.7 179.9 %all-gather.12.cloned.1.call-done = f32[3584,896]{1,0:T(8,128)} async-done(((f32[448,896]{1,0:T(8,128)}), f32[3584,896]{1,0:T(8,128)}) %all-gather.12.cloned.1.call-update) | async-done | bytes 12845072 | tf_op jit(solution)/shard_map/all_gather | solution.py:32
  804.6 16.3 %multiply_add_fusion = f32[448,896]{1,0:T(8,128)} fusion(f32[448,896]{1,0:T(8,128)} %constant_dynamic-slice_fusion, f32[448,3584]{1,0:T(8,128)} %all-reduce.2.cloned.1.call-done, f32[3584,896]{1,0:T(8,128)} %all-gather.12.cloned.1.call-done), kind=kOutput, calls=%fused_computation.2 | convolution fusion | flops 8633081856 | bytes 22478848 | tf_op jit(solution)/shard_map/dot_general | solution.py:16
  821.0 0.0 all-gather.14.cloned.1.call-update
  821.0 45.5 %all-gather.14.cloned.1.call-done = f32[448,3584]{1,0:T(8,128)} async-done(((f32[448,896]{1,0:T(8,128)}), f32[448,3584]{1,0:T(8,128)}) %all-gather.14.cloned.1.call-update) | async-done | bytes 6422544 | tf_op jit(solution)/shard_map/all_gather | solution.py:35
  866.5 0.0 copy-start
  866.5 0.0 copy-start.1
  866.5 0.0 slice-start
  866.5 0.0 slice-start.1
  866.5 12.6 %add_multiply_fusion = f32[448,768]{1,0:T(8,128)S(1)} fusion(f32[448,3584]{1,0:T(8,128)} %all-gather.14.cloned.1.call-done, f32[3584,768]{1,0:T(8,128)} %all-gather.10.cloned.1.call-done, f32[448,2304]{1,0:T(8,128)} %param.1), kind=kOutput, calls=%fused_computation.3 | convolution fusion | flops 7399784448 | bytes 20185088 | tf_op jit(solution)/shard_map/dot_general | solution.py:16
  879.1 0.0 copy-done
  879.1 0.0 copy-done.1
  879.1 0.0 slice-start.2
  879.1 11.2 %add_multiply_fusion.1 = f32[448,768]{1,0:T(8,128)S(1)} fusion(f32[448,3584]{1,0:T(8,128)S(1)} %copy-done, f32[3584,768]{1,0:T(8,128)} %all-gather.8.cloned.1.call-done, f32[448,2304]{1,0:T(8,128)S(1)} %copy-done.1), kind=kOutput, calls=%fused_computation.4 | convolution fusion | flops 7399784448 | bytes 20185088 | tf_op jit(solution)/shard_map/dot_general | solution.py:16
  890.4 0.0 slice-done
  890.4 0.0 slice-done.1
  890.4 0.0 slice-done.2
  890.4 8.4 add_multiply_fusion.2
  898.8 2.3 pad_maximum_fusion
  (1 shorter events, 0.0 us)
Async XLA Ops:
  6.5 164.5 %all-gather.8.cloned.1.call-start = ((), (), s32[]{:S(2)}) async-start(), calls=%async_computation.1 | async-start | bytes 12386304 | tf_op jit(solution)/shard_map/all_gather | solution.py:23
  10.9 317.7 %all-gather.6.cloned.1.call-start = ((), (), s32[]{:S(2)}) async-start(), calls=%async_computation | async-start | bytes 12386304 | tf_op jit(solution)/shard_map/all_gather | solution.py:23
  11.7 474.6 %all-gather.10.cloned.1.call-start = ((), (), s32[]{:S(2)}) async-start(), calls=%async_computation.2 | async-start | bytes 12386304 | tf_op jit(solution)/shard_map/all_gather | solution.py:23
  12.4 609.5 %all-reduce.2.cloned.1.call-start = ((), (), s32[]{:S(2)}) async-start(), calls=%async_computation.3 | async-start | bytes 12845056 | tf_op jit(solution)/shard_map/psum | solution.py:28
  501.9 302.7 %all-gather.12.cloned.1.call-start = ((), (), s32[]{:S(2)}) async-start(), calls=%async_computation.4 | async-start | bytes 14450688 | tf_op jit(solution)/shard_map/all_gather | solution.py:32
  624.6 241.8 %all-gather.14.cloned.1.call-start = ((), (), s32[]{:S(2)}) async-start(), calls=%async_computation.5 | async-start | bytes 8028160 | tf_op jit(solution)/shard_map/all_gather | solution.py:35
  866.5 12.7 %copy-start = (f32[448,3584]{1,0:T(8,128)S(1)}, f32[448,3584]{1,0:T(8,128)}, u32[]{:S(2)}) copy-start(f32[448,3584]{1,0:T(8,128)} %all-gather.14.cloned.1.call-done) | copy-start | bytes 19267588
  866.5 12.7 %copy-start.1 = (f32[448,2304]{1,0:T(8,128)S(1)}, f32[448,2304]{1,0:T(8,128)}, u32[]{:S(2)}) copy-start(f32[448,2304]{1,0:T(8,128)} %param.1) | copy-start | bytes 12386308
  866.5 23.9 %slice-start = ((s8[11010048]{0:T(1024)(128)(4,1)}), s8[4194304]{0:T(1024)(128)(4,1)S(1)}, s32[]{:S(2)}) async-start(s8[11010048]{0:T(1024)(128)(4,1)} %bitcast.11), calls=%async_computation.6 | async-start | bytes 8388608
  866.5 23.9 %slice-start.1 = ((s8[11010048]{0:T(1024)(128)(4,1)}), s8[4194304]{0:T(1024)(128)(4,1)S(1)}, s32[]{:S(2)}) async-start(s8[11010048]{0:T(1024)(128)(4,1)} %bitcast.11), calls=%async_computation.7 | async-start | bytes 8388608
  879.1 11.3 %slice-start.2 = ((s8[11010048]{0:T(1024)(128)(4,1)}), s8[2621440]{0:T(1024)(128)(4,1)S(1)}, s32[]{:S(2)}) async-start(s8[11010048]{0:T(1024)(128)(4,1)} %bitcast.11), calls=%async_computation.8 | async-start | bytes 5242880
Sparse Core Ops, SparseCore 0:
  11.0 159.9 all-gather.7
  173.2 155.4 all-gather.5
  330.8 155.4 all-gather.9
  502.0 119.8 all-reduce.1
  624.7 179.8 all-gather.11
  821.1 45.3 all-gather.13

commit v2 on v1

v2 whole, which is shorter than its diff:
```python
import math

import jax
import jax.numpy as jnp
from jax import lax
from jax.sharding import PartitionSpec as P

PREC = lax.Precision.HIGH
COEF_A = 3.4445
COEF_B = -4.775
COEF_C = 2.0315


def product(left, right, dims):
    return lax.dot_general(
        left, right, (dims, ((), ())), precision=PREC, preferred_element_type=jnp.float32
    )


def ring_order(count):
    return list(range(0, count, 2)) + list(range(1, count, 2))[::-1]


def shift(value, order, step):
    count = len(order)
    pairs = [(order[k], order[(k + step) % count]) for k in range(count)]
    return lax.ppermute(value, "row", pairs)


def swap(value, bit):
    count = lax.axis_size("col")
    return lax.ppermute(value, "col", [(k, k ^ bit) for k in range(count)])


def ring_gather(up, down, order, visit):
    count = len(order)
    table = jnp.array(order, jnp.int32)
    place = jnp.array([order.index(k) for k in range(count)], jnp.int32)
    me = lax.axis_index("row")
    mine = place[me]
    visit(0, up, me)
    visit(1, down, me)
    for step in range(1, count):
        up = shift(up, order, 1)
        down = shift(down, order, -1)
        visit(0, up, table[(mine - step) % count])
        visit(1, down, table[(mine + step) % count])


def body(scale, iterate):
    rows, cols = iterate.shape
    row_count, col_count = lax.axis_size("row"), lax.axis_size("col")
    total = rows * row_count
    order = ring_order(row_count)
    me, my_col = lax.axis_index("row"), lax.axis_index("col")
    half = cols // 2
    own = [iterate[:, :half], iterate[:, half:]]

    slabs = [jnp.zeros((total, half), jnp.float32) for _ in range(2)]
    panels = [jnp.zeros((total, rows), jnp.float32) for _ in range(2)]

    def take_rows(which, value, owner):
        slabs[which] = lax.dynamic_update_slice(slabs[which], value, (owner * rows, 0))
        block = product(value, own[which], ((1,), (1,)))
        panels[which] = lax.dynamic_update_slice(panels[which], block, (owner * rows, 0))

    ring_gather(own[0], own[1], order, take_rows)
    partial_value = panels[0] + panels[1]

    tile = partial_value
    bit = 1
    while bit < col_count:
        size = tile.shape[0] // 2
        upper = (my_col & bit) != 0
        low, high = tile[:size], tile[size:]
        tile = jnp.where(upper, high, low) + swap(jnp.where(upper, low, high), bit)
        bit *= 2

    def double(value, axis):
        bit = col_count // 2
        while bit:
            other = swap(value, bit)
            upper = (my_col & bit) != 0
            value = jnp.concatenate(
                [jnp.where(upper, other, value), jnp.where(upper, value, other)], axis
            )
            bit //= 2
        return value

    gram_tile = tile.T
    width = gram_tile.shape[1]
    column = [jnp.zeros((total, width), jnp.float32)]
    near = rows // 16 * 8

    def take_tile(which, value, owner):
        column[0] = lax.dynamic_update_slice(
            column[0], value, (owner * rows + (near if which else 0), 0)
        )

    ring_gather(gram_tile[:near], gram_tile[near:], order, take_tile)
    panel = double(tile, 0)
    square_tile = product(panel, column[0], ((0,), (0,)))
    poly_panel = double(COEF_B * gram_tile + COEF_C * square_tile, 1)
    outs = [
        (COEF_A * piece + product(poly_panel, slab, ((1,), (0,)))) * scale
        for piece, slab in zip(own, slabs)
    ]
    return jnp.concatenate(outs, axis=1)


def solution(mesh):
    placed = P("row", "col")

    def run(iterate):
        scale = 0.2 * math.sqrt(max(iterate.shape))
        return jax.shard_map(
            lambda block: body(scale, block),
            mesh=mesh,
            in_specs=(placed,),
            out_specs=placed,
            check_vma=False,
        )(iterate)

    return run
```

time: 908 us -> 718 us (0.79); the launches traced: 908 us -> 707 us
  waiting for transfers between devices: 795 us -> 316 us
  local copies, waits for them, and re-layouts: 7.04 us -> 183 us
  starting transfers between devices: 0.2 us -> 46.2 us
  matrix products: 89.7 us -> 120 us
  other arithmetic: 2.25 us -> 22.4 us
    all_gather x5 -> x0, waiting for transfers between devices: 674 us -> none  [the longest x3 448 us: body(): lax.all_gather(piece, 'row', axis=0, tiled=True)]
    ppermute x0 -> x34, waiting for transfers between devices: none -> 316 us  [the longest x28 259 us: shift(): return lax.ppermute(value, 'row', pairs)]
    dynamic_update_slice x0 -> x47, local copies, waits for them, and re-layouts: none -> 150 us  [the longest x16 94.9 us: take_rows(): lax.dynamic_update_slice(panels[which], block, (owner * rows, 0))]
    psum x1 -> x0, waiting for transfers between devices: 120 us -> none  [body(): gram_panel = lax.psum(partial_value, 'col')]
    ppermute x0 -> x34, starting transfers between devices: none -> 46.2 us  [the longest x28 41.4 us: shift(): return lax.ppermute(value, 'row', pairs)]
    dot_general x7 -> x19, matrix products: 89.7 us -> 120 us  [product(): lax.dot_general(left, right, (dims, ((), ())), precision=PREC, preferred_...]
    another operation x0 -> x4, local copies, waits for them, and re-layouts: none -> 20.3 us  [run(): jax.shard_map(lambda block: body(scale, block), mesh=mesh, in_specs=(plac...]
    add x0 -> x3, other arithmetic: none -> 9.43 us  [the longest x1 5.75 us: body(): partial_value = panels[0] + panels[1]]
  transfers between devices with their start and end apart: 6 -> 34, of which waited for: 6 -> 14; matrix products, arithmetic and copies ran while one was open for 3% -> 31% of each run, Pallas kernels for 0% -> 0%
where the time goes in v2:
time: 718 us; the launch traced here: 707 us
  waiting for transfers between devices  316 us (44%)
  local copies, waits for them, and re-layouts  183 us (25%)
  matrix products  120 us (17%)
  starting transfers between devices  46.2 us (6%)
  other arithmetic  22.4 us (3%)
  between operations  19 us (3%)
    ppermute x28, waiting for transfers between devices, shift(): return lax.ppermute(value, 'row', pairs)  259 us
    dot_general x19, matrix products, product(): lax.dot_general(left, right, (dims, ((), ())), precision=PREC, preferred_...  120 us
    dynamic_update_slice x16, local copies, waits for them, and re-layouts, take_rows(): lax.dynamic_update_slice(panels[which], block, (owner * rows, 0))  94.9 us
    ppermute x6, waiting for transfers between devices, swap(): return lax.ppermute(value, 'col', [(k, k ^ bit) for k in range(count)])  56.8 us
    ppermute x28, starting transfers between devices, shift(): return lax.ppermute(value, 'row', pairs)  41.4 us
    dynamic_update_slice x16, local copies, waits for them, and re-layouts, take_rows(): lax.dynamic_update_slice(slabs[which], value, (owner * rows, 0))  34.9 us
    another operation x4, local copies, waits for them, and re-layouts, run(): jax.shard_map(lambda block: body(scale, block), mesh=mesh, in_specs=(plac...  20.3 us
    dynamic_update_slice x15, local copies, waits for them, and re-layouts, take_tile(): lax.dynamic_update_slice(column[0], value, (owner * rows + (near if which...  20.2 us
  transfers between devices with their start and end apart: 34, of which 14 were waited for; matrix products, arithmetic and copies ran while one was open for 31% of the time, Pallas kernels for 0%

profile of v2, /device:TPU:0, one launch (start us, length us, event | category | flops | bytes accessed | tf_op | source)
XLA Modules:
  0.0 707.3 jit_solution(18358152626233353509)
XLA Ops:
  0.0 6.8 broadcast.42.clone.1
  11.6 44.9 %collective-permute-done.7 = f32[448,1152]{1,0:T(8,128)S(1)} collective-permute-done((f32[448,1152]{1,0:T(8,128)S(1)}, f32[448,1152]{1,0:T(8,128)S(1)}, u32[]{:S(2)}, u32[]{:S(2)}) %collective-permute-start.7) | collective-permute-done | bytes 2064416 | tf_op jit(solution)/shard_map/ppermute | solution.py:27
  58.5 44.1 %collective-permute-done.8 = f32[448,1152]{1,0:T(8,128)S(1)} collective-permute-done((f32[448,1152]{1,0:T(8,128)S(1)}, f32[448,1152]{1,0:T(8,128)S(1)}, u32[]{:S(2)}, u32[]{:S(2)}) %collective-permute-start.8) | collective-permute-done | bytes 2064416 | tf_op jit(solution)/shard_map/ppermute | solution.py:27
  104.6 43.2 %collective-permute-done.9 = f32[448,1152]{1,0:T(8,128)S(1)} collective-permute-done((f32[448,1152]{1,0:T(8,128)S(1)}, f32[448,1152]{1,0:T(8,128)S(1)}, u32[]{:S(2)}, u32[]{:S(2)}) %collective-permute-start.9) | collective-permute-done | bytes 2064416 | tf_op jit(solution)/shard_map/ppermute | solution.py:27
  151.1 42.8 %collective-permute-done.10 = f32[448,1152]{1,0:T(8,128)} collective-permute-done((f32[448,1152]{1,0:T(8,128)S(1)}, f32[448,1152]{1,0:T(8,128)}, u32[]{:S(2)}, u32[]{:S(2)}) %collective-permute-start.10) | collective-permute-done | bytes 2064416 | tf_op jit(solution)/shard_map/ppermute | solution.py:27
  215.6 4.2 fusion.29
  223.2 5.7 dynamic_update_slice.152
  236.5 5.7 dynamic_update_slice.144
  248.5 5.8 dynamic_update_slice.153
  254.5 4.2 fusion.43
  258.7 6.3 dynamic_update_slice.145
  268.5 5.7 dynamic_update_slice.154
  274.2 4.3 fusion.41
  278.5 6.3 dynamic_update_slice.146
  288.3 5.7 dynamic_update_slice.155
  298.1 6.3 dynamic_update_slice.147
  304.4 12.9 %collective-permute-start.13 = (f32[448,1152]{1,0:T(8,128)}, f32[448,1152]{1,0:T(8,128)S(1)}, u32[]{:S(2)}, u32[]{:S(2)}) collective-permute-start(f32[448,1152]{1,0:T(8,128)} %collective-permute-done.12), channel_id=1, source_target_pairs={{0,4},{8,0},{16,8},{24,16},{28,24},{20,28},{12,20},{4,12},{1,5},{9... | collective-permute-start | bytes 6193160 | tf_op jit(solution)/shard_map/ppermute | solution.py:27
  317.3 4.1 fusion.21
  321.4 5.6 dynamic_update_slice.156
  332.4 5.6 dynamic_update_slice.148
  338.0 4.1 fusion.19
  342.2 6.2 dynamic_update_slice.157
  348.4 4.1 fusion.35
  352.6 5.7 dynamic_update_slice.149
  358.2 4.1 fusion.17
  362.4 6.3 dynamic_update_slice.158
  372.8 5.7 dynamic_update_slice.150
  378.5 4.3 fusion.15
  382.8 6.7 dynamic_update_slice.159
  389.5 4.2 fusion.31
  393.7 5.7 dynamic_update_slice.151
  399.4 5.7 add.551
  408.7 6.0 collective-permute-done.14
  419.9 35.6 %collective-permute-done.15 = f32[896,448]{0,1:T(8,128)S(1)} collective-permute-done((f32[896,448]{0,1:T(8,128)S(1)}, f32[896,448]{0,1:T(8,128)S(1)}, u32[]{:S(2)}, u32[]{:S(2)}) %collective-permute-start.15) | collective-permute-done | bytes 1605664 | tf_op jit(solution)/shard_map/ppermute | solution.py:32
  455.7 5.4 broadcast_in_dim.3
  465.8 15.6 %collective-permute-done.18 = f32[224,896]{1,0:T(8,128)S(1)} collective-permute-done((f32[224,896]{1,0:T(8,128)S(1)}, f32[224,896]{1,0:T(8,128)S(1)}, u32[]{:S(2)}, u32[]{:S(2)}) %collective-permute-start.18) | collective-permute-done | bytes 802848 | tf_op jit(solution)/shard_map/ppermute | solution.py:27
  483.4 16.2 %collective-permute-done.20 = f32[224,896]{1,0:T(8,128)S(1)} collective-permute-done((f32[224,896]{1,0:T(8,128)S(1)}, f32[224,896]{1,0:T(8,128)S(1)}, u32[]{:S(2)}, u32[]{:S(2)}) %collective-permute-start.20) | collective-permute-done | bytes 802848 | tf_op jit(solution)/shard_map/ppermute | solution.py:27
  504.2 13.4 %collective-permute-done.22 = f32[224,896]{1,0:T(8,128)S(1)} collective-permute-done((f32[224,896]{1,0:T(8,128)S(1)}, f32[224,896]{1,0:T(8,128)S(1)}, u32[]{:S(2)}, u32[]{:S(2)}) %collective-permute-start.22) | collective-permute-done | bytes 802848 | tf_op jit(solution)/shard_map/ppermute | solution.py:27
  519.7 15.8 %collective-permute-done.24 = f32[224,896]{1,0:T(8,128)} collective-permute-done((f32[224,896]{1,0:T(8,128)S(1)}, f32[224,896]{1,0:T(8,128)}, u32[]{:S(2)}, u32[]{:S(2)}) %collective-permute-start.24) | collective-permute-done | bytes 802848 | tf_op jit(solution)/shard_map/ppermute | solution.py:27
  542.6 10.9 %collective-permute-done.26 = f32[224,896]{1,0:T(8,128)} collective-permute-done((f32[224,896]{1,0:T(8,128)}, f32[224,896]{1,0:T(8,128)}, u32[]{:S(2)}, u32[]{:S(2)}) %collective-permute-start.26) | collective-permute-done | bytes 802848 | tf_op jit(solution)/shard_map/ppermute | solution.py:27
  566.9 4.9 collective-permute-done.28
  578.2 7.4 %collective-permute-done.30 = f32[224,896]{1,0:T(8,128)S(1)} collective-permute-done((f32[224,896]{1,0:T(8,128)S(1)}, f32[224,896]{1,0:T(8,128)S(1)}, u32[]{:S(2)}, u32[]{:S(2)}) %collective-permute-start.30) | collective-permute-done | bytes 802848 | tf_op jit(solution)/shard_map/ppermute | solution.py:27
  587.5 17.6 %multiply_add_fusion = f32[448,896]{1,0:T(8,128)S(1)} fusion(f32[3584,896]{1,0:T(8,128)} %constant_dynamic-update-slice_fusion.10, f32[1792,448]{0,1:T(8,128)S(1)} %get-tuple-element.8, f32[1792,448]{0,1:T(8,128)S(1)} %get-tuple-element.7, f32[896,448]{0,1:T(8,128)S(1)} %select_add_fusion.1), kind=kOutput, calls=%fused_computation.16 | convolution fusion | flops 8634687488 | bytes 22478848 | tf_op jit(solution)/shard_map/dot_general | solution.py:15
  606.8 6.7 broadcast.42.clone
  620.2 15.2 %collective-permute-done.32 = f32[448,896]{1,0:T(8,128)S(1)} collective-permute-done((f32[448,896]{1,0:T(8,128)S(1)}, f32[448,896]{1,0:T(8,128)S(1)}, u32[]{:S(2)}, u32[]{:S(2)}) %collective-permute-start.32) | collective-permute-done | bytes 1605664 | tf_op jit(solution)/shard_map/ppermute | solution.py:32
  665.1 18.6 %fusion.7 = f32[448,1152]{1,0:T(8,128)} fusion(f32[3584,1152]{1,0:T(8,128)} %constant_dynamic-update-slice_fusion.20, f32[448,1792]{1,0:T(8,128)S(1)} %get-tuple-element.6, f32[448,1792]{1,0:T(8,128)S(1)} %get-tuple-element.5, f32[448,2304]{1,0:T(8,128)S(1)} %copy-done.1), kind=kOutput, calls=%fused_computation.12 | convolution fusion | flops 11101282304 | bytes 27066368 | tf_op jit(solution)/shard_map/dot_general | solution.py:15
  683.8 18.7 %fusion.9 = f32[448,1152]{1,0:T(8,128)} fusion(f32[3584,1152]{1,0:T(8,128)} %constant_dynamic-update-slice_fusion.29, f32[448,1792]{1,0:T(8,128)S(1)} %get-tuple-element.6, f32[448,1792]{1,0:T(8,128)S(1)} %get-tuple-element.5, f32[448,2304]{1,0:T(8,128)S(1)} %copy-done.1), kind=kOutput, calls=%fused_computation.14 | convolution fusion | flops 11101282304 | bytes 27066368 | tf_op jit(solution)/shard_map/dot_general | solution.py:15
  702.4 4.5 pad_maximum_fusion.3
  (172 shorter events, 143.0 us)
Async XLA Ops:
  6.8 189.3 %copy-start.32 = (s32[8]{0:T(128)S(1)}, s32[8]{0:T(128)}, u32[]{:S(2)}) copy-start(s32[8]{0:T(128)} %constant.273.clone) | copy-start | bytes 100
  6.8 199.2 %copy-start.31 = (s32[8]{0:T(128)S(1)}, s32[8]{0:T(128)}, u32[]{:S(2)}) copy-start(s32[8]{0:T(128)} %constant.272.clone) | copy-start | bytes 100
  8.5 48.0 %collective-permute-start.7 = (f32[448,1152]{1,0:T(8,128)S(1)}, f32[448,1152]{1,0:T(8,128)S(1)}, u32[]{:S(2)}, u32[]{:S(2)}) collective-permute-start(f32[448,1152]{1,0:T(8,128)S(1)} %get-tuple-element.10), channel_id=1, source_target_pairs={{0,4},{8,0},{16,8},{24,16},{28,24},{20,28},{12,20},{4,12},{1,5},{9... | collective-permute-start | bytes 6193160 | tf_op jit(solution)/shard_map/ppermute | solution.py:27
  11.5 46.7 %collective-permute-start = (f32[448,1152]{1,0:T(8,128)S(1)}, f32[448,1152]{1,0:T(8,128)S(1)}, u32[]{:S(2)}, u32[]{:S(2)}) collective-permute-start(f32[448,1152]{1,0:T(8,128)S(1)} %get-tuple-element.11), channel_id=1, source_target_pairs={{0,8},{8,16},{16,24},{24,28},{28,20},{20,12},{12,4},{4,0},{1,9},{9... | collective-permute-start | bytes 6193160 | tf_op jit(solution)/shard_map/ppermute | solution.py:27
  56.5 46.1 %collective-permute-start.8 = (f32[448,1152]{1,0:T(8,128)S(1)}, f32[448,1152]{1,0:T(8,128)S(1)}, u32[]{:S(2)}, u32[]{:S(2)}) collective-permute-start(f32[448,1152]{1,0:T(8,128)S(1)} %collective-permute-done.7), channel_id=1, source_target_pairs={{0,4},{8,0},{16,8},{24,16},{28,24},{20,28},{12,20},{4,12},{1,5},{9... | collective-permute-start | bytes 6193160 | tf_op jit(solution)/shard_map/ppermute | solution.py:27
  58.1 135.8 %copy-start.12 = (f32[448,1152]{1,0:T(8,128)}, f32[448,1152]{1,0:T(8,128)S(1)}, u32[]{:S(2)}) copy-start(f32[448,1152]{1,0:T(8,128)S(1)} %collective-permute-done) | copy-start | bytes 6193156
  58.1 45.8 %collective-permute-start.1 = (f32[448,1152]{1,0:T(8,128)S(1)}, f32[448,1152]{1,0:T(8,128)S(1)}, u32[]{:S(2)}, u32[]{:S(2)}) collective-permute-start(f32[448,1152]{1,0:T(8,128)S(1)} %collective-permute-done), channel_id=1, source_target_pairs={{0,8},{8,16},{16,24},{24,28},{28,20},{20,12},{12,4},{4,0},{1,9},{9... | collective-permute-start | bytes 6193160 | tf_op jit(solution)/shard_map/ppermute | solution.py:27
  102.6 162.4 %copy-start.5 = (f32[448,1152]{1,0:T(8,128)}, f32[448,1152]{1,0:T(8,128)S(1)}, u32[]{:S(2)}) copy-start(f32[448,1152]{1,0:T(8,128)S(1)} %collective-permute-done.8) | copy-start | bytes 6193156
  102.6 45.2 %collective-permute-start.9 = (f32[448,1152]{1,0:T(8,128)S(1)}, f32[448,1152]{1,0:T(8,128)S(1)}, u32[]{:S(2)}, u32[]{:S(2)}) collective-permute-start(f32[448,1152]{1,0:T(8,128)S(1)} %collective-permute-done.8), channel_id=1, source_target_pairs={{0,4},{8,0},{16,8},{24,16},{28,24},{20,28},{12,20},{4,12},{1,5},{9... | collective-permute-start | bytes 6193160 | tf_op jit(solution)/shard_map/ppermute | solution.py:27
  103.9 91.1 %copy-start.16 = (f32[448,1152]{1,0:T(8,128)}, f32[448,1152]{1,0:T(8,128)S(1)}, u32[]{:S(2)}) copy-start(f32[448,1152]{1,0:T(8,128)S(1)} %collective-permute-done.1) | copy-start | bytes 6193156
  103.9 46.2 %collective-permute-start.2 = (f32[448,1152]{1,0:T(8,128)S(1)}, f32[448,1152]{1,0:T(8,128)S(1)}, u32[]{:S(2)}, u32[]{:S(2)}) collective-permute-start(f32[448,1152]{1,0:T(8,128)S(1)} %collective-permute-done.1), channel_id=1, source_target_pairs={{0,8},{8,16},{16,24},{24,28},{28,20},{20,12},{12,4},{4,0},{1,9},{9... | collective-permute-start | bytes 6193160 | tf_op jit(solution)/shard_map/ppermute | solution.py:27
  149.1 44.9 %collective-permute-start.10 = (f32[448,1152]{1,0:T(8,128)S(1)}, f32[448,1152]{1,0:T(8,128)}, u32[]{:S(2)}, u32[]{:S(2)}) collective-permute-start(f32[448,1152]{1,0:T(8,128)S(1)} %collective-permute-done.9), channel_id=1, source_target_pairs={{0,4},{8,0},{16,8},{24,16},{28,24},{20,28},{12,20},{4,12},{1,5},{9... | collective-permute-start | bytes 6193160 | tf_op jit(solution)/shard_map/ppermute | solution.py:27
  150.1 44.9 %copy-start.14 = (f32[448,1152]{1,0:T(8,128)}, f32[448,1152]{1,0:T(8,128)S(1)}, u32[]{:S(2)}) copy-start(f32[448,1152]{1,0:T(8,128)S(1)} %collective-permute-done.2) | copy-start | bytes 6193156
  150.1 44.9 %collective-permute-start.3 = (f32[448,1152]{1,0:T(8,128)S(1)}, f32[448,1152]{1,0:T(8,128)}, u32[]{:S(2)}, u32[]{:S(2)}) collective-permute-start(f32[448,1152]{1,0:T(8,128)S(1)} %collective-permute-done.2), channel_id=1, source_target_pairs={{0,8},{8,16},{16,24},{24,28},{28,20},{20,12},{12,4},{4,0},{1,9},{9... | collective-permute-start | bytes 6193160 | tf_op jit(solution)/shard_map/ppermute | solution.py:27
  194.0 48.3 %collective-permute-start.11 = (f32[448,1152]{1,0:T(8,128)}, f32[448,1152]{1,0:T(8,128)}, u32[]{:S(2)}, u32[]{:S(2)}) collective-permute-start(f32[448,1152]{1,0:T(8,128)} %collective-permute-done.10), channel_id=1, source_target_pairs={{0,4},{8,0},{16,8},{24,16},{28,24},{20,28},{12,20},{4,12},{1,5},{9... | collective-permute-start | bytes 6193160 | tf_op jit(solution)/shard_map/ppermute | solution.py:27
  195.0 59.3 %collective-permute-start.4 = (f32[448,1152]{1,0:T(8,128)}, f32[448,1152]{1,0:T(8,128)}, u32[]{:S(2)}, u32[]{:S(2)}) collective-permute-start(f32[448,1152]{1,0:T(8,128)} %collective-permute-done.3), channel_id=1, source_target_pairs={{0,8},{8,16},{16,24},{24,28},{28,20},{20,12},{12,4},{4,0},{1,9},{9... | collective-permute-start | bytes 6193160 | tf_op jit(solution)/shard_map/ppermute | solution.py:27
  242.3 62.1 %collective-permute-start.12 = (f32[448,1152]{1,0:T(8,128)}, f32[448,1152]{1,0:T(8,128)}, u32[]{:S(2)}, u32[]{:S(2)}) collective-permute-start(f32[448,1152]{1,0:T(8,128)} %collective-permute-done.11), channel_id=1, source_target_pairs={{0,4},{8,0},{16,8},{24,16},{28,24},{20,28},{12,20},{4,12},{1,5},{9... | collective-permute-start | bytes 6193160 | tf_op jit(solution)/shard_map/ppermute | solution.py:27
  254.3 72.8 %collective-permute-start.5 = (f32[448,1152]{1,0:T(8,128)}, f32[448,1152]{1,0:T(8,128)}, u32[]{:S(2)}, u32[]{:S(2)}) collective-permute-start(f32[448,1152]{1,0:T(8,128)} %collective-permute-done.4), channel_id=1, source_target_pairs={{0,8},{8,16},{16,24},{24,28},{28,20},{20,12},{12,4},{4,0},{1,9},{9... | collective-permute-start | bytes 6193160 | tf_op jit(solution)/shard_map/ppermute | solution.py:27
  304.4 74.1 %collective-permute-start.13 = (f32[448,1152]{1,0:T(8,128)}, f32[448,1152]{1,0:T(8,128)S(1)}, u32[]{:S(2)}, u32[]{:S(2)}) collective-permute-start(f32[448,1152]{1,0:T(8,128)} %collective-permute-done.12), channel_id=1, source_target_pairs={{0,4},{8,0},{16,8},{24,16},{28,24},{20,28},{12,20},{4,12},{1,5},{9... | collective-permute-start | bytes 6193160 | tf_op jit(solution)/shard_map/ppermute | solution.py:27
  327.1 62.4 %collective-permute-start.6 = (f32[448,1152]{1,0:T(8,128)}, f32[448,1152]{1,0:T(8,128)}, u32[]{:S(2)}, u32[]{:S(2)}) collective-permute-start(f32[448,1152]{1,0:T(8,128)} %collective-permute-done.5), channel_id=1, source_target_pairs={{0,8},{8,16},{16,24},{24,28},{28,20},{20,12},{12,4},{4,0},{1,9},{9... | collective-permute-start | bytes 6193160 | tf_op jit(solution)/shard_map/ppermute | solution.py:27
  378.5 11.0 %copy-start.18 = (f32[448,1152]{1,0:T(8,128)}, f32[448,1152]{1,0:T(8,128)S(1)}, u32[]{:S(2)}) copy-start(f32[448,1152]{1,0:T(8,128)S(1)} %collective-permute-done.13) | copy-start | bytes 6193156
  408.7 6.0 collective-permute-start.14
  418.3 37.2 %collective-permute-start.15 = (f32[896,448]{0,1:T(8,128)S(1)}, f32[896,448]{0,1:T(8,128)S(1)}, u32[]{:S(2)}, u32[]{:S(2)}) collective-permute-start(f32[896,448]{0,1:T(8,128)S(1)} %slice_select_fusion.1), channel_id=1, source_target_pairs={{0,2},{1,3},{2,0},{3,1},{4,6},{5,7},{6,4},{7,5},{8,10},{9,11},{10,... | collective-permute-start | bytes 4816904 | tf_op jit(solution)/shard_map/ppermute | solution.py:32
  462.2 19.1 %collective-permute-start.18 = (f32[224,896]{1,0:T(8,128)S(1)}, f32[224,896]{1,0:T(8,128)S(1)}, u32[]{:S(2)}, u32[]{:S(2)}) collective-permute-start(f32[224,896]{1,0:T(8,128)S(1)} %get-tuple-element.18), channel_id=1, source_target_pairs={{0,8},{8,16},{16,24},{24,28},{28,20},{20,12},{12,4},{4,0},{1,9},{9... | collective-permute-start | bytes 2408456 | tf_op jit(solution)/shard_map/ppermute | solution.py:27
  462.6 19.1 %collective-permute-start.19 = (f32[224,896]{1,0:T(8,128)S(1)}, f32[224,896]{1,0:T(8,128)S(1)}, u32[]{:S(2)}, u32[]{:S(2)}) collective-permute-start(f32[224,896]{1,0:T(8,128)S(1)} %get-tuple-element.16), channel_id=1, source_target_pairs={{0,4},{8,0},{16,8},{24,16},{28,24},{20,28},{12,20},{4,12},{1,5},{9... | collective-permute-start | bytes 2408456 | tf_op jit(solution)/shard_map/ppermute | solution.py:27
  464.2 37.3 %collective-permute-start.16 = (f32[896,448]{0,1:T(8,128)S(1)}, f32[896,448]{0,1:T(8,128)S(1)}, u32[]{:S(2)}, u32[]{:S(2)}) collective-permute-start(f32[896,448]{0,1:T(8,128)S(1)} %select_add_fusion.1), channel_id=1, source_target_pairs={{0,2},{1,3},{2,0},{3,1},{4,6},{5,7},{6,4},{7,5},{8,10},{9,11},{10,... | collective-permute-start | bytes 4816904 | tf_op jit(solution)/shard_map/ppermute | solution.py:32
  481.3 20.2 %copy-start.20 = (f32[224,896]{1,0:T(8,128)}, f32[224,896]{1,0:T(8,128)S(1)}, u32[]{:S(2)}) copy-start(f32[224,896]{1,0:T(8,128)S(1)} %collective-permute-done.18) | copy-start | bytes 2408452
  481.3 18.2 %collective-permute-start.20 = (f32[224,896]{1,0:T(8,128)S(1)}, f32[224,896]{1,0:T(8,128)S(1)}, u32[]{:S(2)}, u32[]{:S(2)}) collective-permute-start(f32[224,896]{1,0:T(8,128)S(1)} %collective-permute-done.18), channel_id=1, source_target_pairs={{0,8},{8,16},{16,24},{24,28},{28,20},{20,12},{12,4},{4,0},{1,9},{9... | collective-permute-start | bytes 2408456 | tf_op jit(solution)/shard_map/ppermute | solution.py:27
  481.8 20.2 %copy-start.23 = (f32[224,896]{1,0:T(8,128)}, f32[224,896]{1,0:T(8,128)S(1)}, u32[]{:S(2)}) copy-start(f32[224,896]{1,0:T(8,128)S(1)} %collective-permute-done.19) | copy-start | bytes 2408452
  481.8 18.2 %collective-permute-start.21 = (f32[224,896]{1,0:T(8,128)S(1)}, f32[224,896]{1,0:T(8,128)S(1)}, u32[]{:S(2)}, u32[]{:S(2)}) collective-permute-start(f32[224,896]{1,0:T(8,128)S(1)} %collective-permute-done.19), channel_id=1, source_target_pairs={{0,4},{8,0},{16,8},{24,16},{28,24},{20,28},{12,20},{4,12},{1,5},{9... | collective-permute-start | bytes 2408456 | tf_op jit(solution)/shard_map/ppermute | solution.py:27
  499.5 18.1 %collective-permute-start.22 = (f32[224,896]{1,0:T(8,128)S(1)}, f32[224,896]{1,0:T(8,128)S(1)}, u32[]{:S(2)}, u32[]{:S(2)}) collective-permute-start(f32[224,896]{1,0:T(8,128)S(1)} %collective-permute-done.20), channel_id=1, source_target_pairs={{0,8},{8,16},{16,24},{24,28},{28,20},{20,12},{12,4},{4,0},{1,9},{9... | collective-permute-start | bytes 2408456 | tf_op jit(solution)/shard_map/ppermute | solution.py:27
  499.9 18.1 %collective-permute-start.23 = (f32[224,896]{1,0:T(8,128)S(1)}, f32[224,896]{1,0:T(8,128)S(1)}, u32[]{:S(2)}, u32[]{:S(2)}) collective-permute-start(f32[224,896]{1,0:T(8,128)S(1)} %collective-permute-done.21), channel_id=1, source_target_pairs={{0,4},{8,0},{16,8},{24,16},{28,24},{20,28},{12,20},{4,12},{1,5},{9... | collective-permute-start | bytes 2408456 | tf_op jit(solution)/shard_map/ppermute | solution.py:27
  504.2 71.5 %collective-permute-start.17 = (f32[1792,448]{0,1:T(8,128)}, f32[1792,448]{0,1:T(8,128)}, u32[]{:S(2)}, u32[]{:S(2)}) collective-permute-start(f32[1792,448]{0,1:T(8,128)} %pad_maximum_fusion.4), channel_id=1, source_target_pairs={{0,1},{1,0},{2,3},{3,2},{4,5},{5,4},{6,7},{7,6},{8,9},{9,8},{10,11... | collective-permute-start | bytes 9633800 | tf_op jit(solution)/shard_map/ppermute | solution.py:32
  517.6 17.8 %collective-permute-start.24 = (f32[224,896]{1,0:T(8,128)S(1)}, f32[224,896]{1,0:T(8,128)}, u32[]{:S(2)}, u32[]{:S(2)}) collective-permute-start(f32[224,896]{1,0:T(8,128)S(1)} %collective-permute-done.22), channel_id=1, source_target_pairs={{0,8},{8,16},{16,24},{24,28},{28,20},{20,12},{12,4},{4,0},{1,9},{9... | collective-permute-start | bytes 2408456 | tf_op jit(solution)/shard_map/ppermute | solution.py:27
  518.5 17.0 %copy-start.27 = (f32[224,896]{1,0:T(8,128)}, f32[224,896]{1,0:T(8,128)S(1)}, u32[]{:S(2)}) copy-start(f32[224,896]{1,0:T(8,128)S(1)} %collective-permute-done.23) | copy-start | bytes 2408452
  518.5 17.4 %collective-permute-start.25 = (f32[224,896]{1,0:T(8,128)S(1)}, f32[224,896]{1,0:T(8,128)}, u32[]{:S(2)}, u32[]{:S(2)}) collective-permute-start(f32[224,896]{1,0:T(8,128)S(1)} %collective-permute-done.23), channel_id=1, source_target_pairs={{0,4},{8,0},{16,8},{24,16},{28,24},{20,28},{12,20},{4,12},{1,5},{9... | collective-permute-start | bytes 2408456 | tf_op jit(solution)/shard_map/ppermute | solution.py:27
  535.4 18.1 %collective-permute-start.26 = (f32[224,896]{1,0:T(8,128)}, f32[224,896]{1,0:T(8,128)}, u32[]{:S(2)}, u32[]{:S(2)}) collective-permute-start(f32[224,896]{1,0:T(8,128)} %collective-permute-done.24), channel_id=1, source_target_pairs={{0,8},{8,16},{16,24},{24,28},{28,20},{20,12},{12,4},{4,0},{1,9},{9... | collective-permute-start | bytes 2408456 | tf_op jit(solution)/shard_map/ppermute | solution.py:27
  535.8 18.1 %collective-permute-start.27 = (f32[224,896]{1,0:T(8,128)}, f32[224,896]{1,0:T(8,128)}, u32[]{:S(2)}, u32[]{:S(2)}) collective-permute-start(f32[224,896]{1,0:T(8,128)} %collective-permute-done.25), channel_id=1, source_target_pairs={{0,4},{8,0},{16,8},{24,16},{28,24},{20,28},{12,20},{4,12},{1,5},{9... | collective-permute-start | bytes 2408456 | tf_op jit(solution)/shard_map/ppermute | solution.py:27
  537.5 18.1 %copy-start.22 = (f32[224,896]{1,0:T(8,128)S(1)}, f32[224,896]{1,0:T(8,128)}, u32[]{:S(2)}) copy-start(f32[224,896]{1,0:T(8,128)} %copy-done.21) | copy-start | bytes 2408452
  538.4 18.1 %copy-start.26 = (f32[224,896]{1,0:T(8,128)S(1)}, f32[224,896]{1,0:T(8,128)}, u32[]{:S(2)}) copy-start(f32[224,896]{1,0:T(8,128)} %copy-done.25) | copy-start | bytes 2408452
  540.6 16.8 %copy-start.28 = (f32[224,896]{1,0:T(8,128)S(1)}, f32[224,896]{1,0:T(8,128)}, u32[]{:S(2)}) copy-start(f32[224,896]{1,0:T(8,128)} %copy-done.27) | copy-start | bytes 2408452
  553.5 18.3 %collective-permute-start.28 = (f32[224,896]{1,0:T(8,128)}, f32[224,896]{1,0:T(8,128)S(1)}, u32[]{:S(2)}, u32[]{:S(2)}) collective-permute-start(f32[224,896]{1,0:T(8,128)} %collective-permute-done.26), channel_id=1, source_target_pairs={{0,8},{8,16},{16,24},{24,28},{28,20},{20,12},{12,4},{4,0},{1,9},{9... | collective-permute-start | bytes 2408456 | tf_op jit(solution)/shard_map/ppermute | solution.py:27
  553.9 18.3 %collective-permute-start.29 = (f32[224,896]{1,0:T(8,128)}, f32[224,896]{1,0:T(8,128)S(1)}, u32[]{:S(2)}, u32[]{:S(2)}) collective-permute-start(f32[224,896]{1,0:T(8,128)} %collective-permute-done.27), channel_id=1, source_target_pairs={{0,4},{8,0},{16,8},{24,16},{28,24},{20,28},{12,20},{4,12},{1,5},{9... | collective-permute-start | bytes 2408456 | tf_op jit(solution)/shard_map/ppermute | solution.py:27
  562.5 13.1 %copy-start.4 = (f32[896,448]{0,1:T(8,128)S(1)}, f32[896,448]{0,1:T(8,128)}, u32[]{:S(2)}) copy-start(f32[896,448]{0,1:T(8,128)} %copy-done.3) | copy-start | bytes 4816900
  571.8 13.8 %collective-permute-start.30 = (f32[224,896]{1,0:T(8,128)S(1)}, f32[224,896]{1,0:T(8,128)S(1)}, u32[]{:S(2)}, u32[]{:S(2)}) collective-permute-start(f32[224,896]{1,0:T(8,128)S(1)} %collective-permute-done.28), channel_id=1, source_target_pairs={{0,8},{8,16},{16,24},{24,28},{28,20},{20,12},{12,4},{4,0},{1,9},{9... | collective-permute-start | bytes 2408456 | tf_op jit(solution)/shard_map/ppermute | solution.py:27
  572.2 14.4 %collective-permute-start.31 = (f32[224,896]{1,0:T(8,128)S(1)}, f32[224,896]{1,0:T(8,128)S(1)}, u32[]{:S(2)}, u32[]{:S(2)}) collective-permute-start(f32[224,896]{1,0:T(8,128)S(1)} %collective-permute-done.29), channel_id=1, source_target_pairs={{0,4},{8,0},{16,8},{24,16},{28,24},{20,28},{12,20},{4,12},{1,5},{9... | collective-permute-start | bytes 2408456 | tf_op jit(solution)/shard_map/ppermute | solution.py:27
  605.2 30.2 %collective-permute-start.32 = (f32[448,896]{1,0:T(8,128)S(1)}, f32[448,896]{1,0:T(8,128)S(1)}, u32[]{:S(2)}, u32[]{:S(2)}) collective-permute-start(f32[448,896]{1,0:T(8,128)S(1)} %multiply_add_fusion), channel_id=1, source_target_pairs={{0,2},{1,3},{2,0},{3,1},{4,6},{5,7},{6,4},{7,5},{8,10},{9,11},{10,... | collective-permute-start | bytes 4816904 | tf_op jit(solution)/shard_map/ppermute | solution.py:32
  636.0 28.6 %collective-permute-start.33 = (f32[448,1792]{1,0:T(8,128)S(1)}, f32[448,1792]{1,0:T(8,128)S(1)}, u32[]{:S(2)}, u32[]{:S(2)}) collective-permute-start(f32[448,1792]{1,0:T(8,128)S(1)} %pad_maximum_fusion.5), channel_id=1, source_target_pairs={{0,1},{1,0},{2,3},{3,2},{4,5},{5,4},{6,7},{7,6},{8,9},{9,8},{10,11... | collective-permute-start | bytes 9633800 | tf_op jit(solution)/shard_map/ppermute | solution.py:32
  (19 other events, 71.3 us)

commit v3 on v1

v3 whole, which is shorter than its diff:
```python
import math

import jax
import jax.numpy as jnp
from jax import lax
from jax.sharding import PartitionSpec as P

PREC = lax.Precision.HIGH
COEF_A = 3.4445
COEF_B = -4.775
COEF_C = 2.0315


def product(left, right, dims):
    return lax.dot_general(
        left, right, (dims, ((), ())), precision=PREC, preferred_element_type=jnp.float32
    )


def ring_order(count):
    return list(range(0, count, 2)) + list(range(1, count, 2))[::-1]


def shift(value, order, step):
    count = len(order)
    pairs = [(order[k], order[(k + step) % count]) for k in range(count)]
    return lax.ppermute(value, "row", pairs)


def swap(value, bit):
    count = lax.axis_size("col")
    return lax.ppermute(value, "col", [(k, k ^ bit) for k in range(count)])


def sum_over_col(low, high, upper):
    mine = jnp.where(upper, high, low) + swap(jnp.where(upper, low, high), 1)
    bit = 2
    while bit < lax.axis_size("col"):
        mine = mine + swap(mine, bit)
        bit *= 2
    other = swap(mine, 1)
    return jnp.where(upper, other, mine), jnp.where(upper, mine, other)


def body(scale, iterate):
    rows, cols = iterate.shape
    row_count, col_count = lax.axis_size("row"), lax.axis_size("col")
    total = rows * row_count
    near = rows // 2
    per = row_count // col_count
    width = per * rows
    order = ring_order(row_count)
    place = jnp.array([order.index(k) for k in range(row_count)], jnp.int32)
    mine = place[lax.axis_index("row")]
    my_col = lax.axis_index("col")
    upper = (my_col & 1) != 0

    up, down = iterate[:near], iterate[near:]
    near_blocks, far_blocks = [], []
    slab = None
    for step in range(row_count):
        last = step == row_count - 1
        if not last:
            next_up, next_down = shift(up, order, 1), shift(down, order, -1)
        near_at = (mine - step) % row_count * rows
        far_at = (mine + step) % row_count * rows + near
        if step == 1:
            slab = jnp.broadcast_to(up[:1], (total, cols))
            own_at = mine * rows
            slab = lax.dynamic_update_slice(slab, iterate, (own_at, 0))
        if step >= 1:
            slab = lax.dynamic_update_slice(slab, up, (near_at, 0))
            slab = lax.dynamic_update_slice(slab, down, (far_at, 0))
        near_part = product(up, iterate, ((1,), (1,)))
        far_part = product(down, iterate, ((1,), (1,)))
        near_part, far_part = sum_over_col(near_part, far_part, upper)
        if not last:
            held = (next_up, next_down, near_part, far_part)
            if slab is None:
                next_up, next_down, near_part, far_part = lax.optimization_barrier(held)
            else:
                next_up, next_down, near_part, far_part, slab = lax.optimization_barrier(
                    held + (slab,)
                )
            up, down = next_up, next_down
        near_blocks.append(near_part)
        far_blocks.append(far_part)

    near_all = jnp.stack(near_blocks)
    far_all = jnp.stack(far_blocks)
    parts = []
    for k in range(per):
        at = my_col * per + k
        parts.append(lax.dynamic_index_in_dim(near_all, (mine - at) % row_count, 0, False))
        parts.append(lax.dynamic_index_in_dim(far_all, (at - mine) % row_count, 0, False))
    gram_tile = jnp.concatenate(parts, axis=0).T

    up, down = gram_tile[:near], gram_tile[near:]
    square_tile = None
    for step in range(row_count):
        last = step == row_count - 1
        if not last:
            next_up, next_down = shift(up, order, 1), shift(down, order, -1)
        term = product(near_blocks[step], up, ((0,), (0,)))
        term = term + product(far_blocks[step], down, ((0,), (0,)))
        square_tile = term if square_tile is None else square_tile + term
        if not last:
            up, down, square_tile = lax.optimization_barrier((next_up, next_down, square_tile))
    poly_tile = COEF_B * gram_tile + COEF_C * square_tile

    tiles = {0: poly_tile}
    for k in range(1, col_count):
        low_bit = k & -k
        tiles[k] = swap(tiles[k ^ low_bit], low_bit)
    applied = None
    for k in range(0, col_count, 2):
        pair = jnp.concatenate(
            [
                jnp.where(upper, tiles[k + 1], tiles[k]),
                jnp.where(upper, tiles[k], tiles[k + 1]),
            ],
            axis=1,
        )
        at = ((my_col ^ k) >> 1) * (2 * width)
        term = product(pair, lax.dynamic_slice_in_dim(slab, at, 2 * width, 0), ((1,), (0,)))
        applied = term if applied is None else applied + term
    return (COEF_A * iterate + applied) * scale


def solution(mesh):
    placed = P("row", "col")

    def run(iterate):
        scale = 0.2 * math.sqrt(max(iterate.shape))
        return jax.shard_map(
            lambda block: body(scale, block),
            mesh=mesh,
            in_specs=(placed,),
            out_specs=placed,
            check_vma=False,
        )(iterate)

    return run
```

time: 908 us -> 585 us (0.64)
  waiting for transfers between devices: 795 us -> 346 us
  starting transfers between devices: 0.2 us -> 46.8 us
  local copies, waits for them, and re-layouts: 7.04 us -> 53.1 us
  other arithmetic: 2.25 us -> 18.2 us
    all_gather x5 -> x0, waiting for transfers between devices: 674 us -> none  [the longest x3 448 us: body(): lax.all_gather(piece, 'row', axis=0, tiled=True)]
    ppermute x0 -> x55, waiting for transfers between devices: none -> 346 us  [the longest x28 231 us: shift(): return lax.ppermute(value, 'row', pairs)]
    psum x1 -> x0, waiting for transfers between devices: 120 us -> none  [body(): gram_panel = lax.psum(partial_value, 'col')]
    ppermute x0 -> x55, starting transfers between devices: none -> 46.8 us  [the longest x28 31.6 us: shift(): return lax.ppermute(value, 'row', pairs)]
    dynamic_update_slice x0 -> x15, local copies, waits for them, and re-layouts: none -> 29.5 us  [the longest x7 15.1 us: body(): slab = lax.dynamic_update_slice(slab, up, (near_at, 0))]
    squeeze x0 -> x6, local copies, waits for them, and re-layouts: none -> 11.1 us  [the longest x3 6.09 us: body(): lax.dynamic_index_in_dim(near_all, (mine - at) % row_count, 0, False)]
    dot_general x7 -> x34, matrix products: 89.7 us -> 97 us  [product(): lax.dot_general(left, right, (dims, ((), ())), precision=PREC, preferred_...]
  transfers between devices with their start and end apart: 6 -> 55, of which waited for: 6 -> 41; matrix products, arithmetic and copies ran while one was open for 3% -> 21% of each run, Pallas kernels for 0% -> 0%
where the time goes in v3:
time: 585 us; the launch traced here: 576 us
  waiting for transfers between devices  346 us (59%)
  matrix products  97 us (17%)
  local copies, waits for them, and re-layouts  53.1 us (9%)
  starting transfers between devices  46.8 us (8%)
  other arithmetic  18.2 us (3%)
  between operations  14.9 us (3%)
    ppermute x28, waiting for transfers between devices, shift(): return lax.ppermute(value, 'row', pairs)  231 us
    ppermute x27, waiting for transfers between devices, swap(): return lax.ppermute(value, 'col', [(k, k ^ bit) for k in range(count)])  116 us
    dot_general x34, matrix products, product(): lax.dot_general(left, right, (dims, ((), ())), precision=PREC, preferred_...  97 us
    ppermute x28, starting transfers between devices, shift(): return lax.ppermute(value, 'row', pairs)  31.6 us
    ppermute x27, starting transfers between devices, swap(): return lax.ppermute(value, 'col', [(k, k ^ bit) for k in range(count)])  15.2 us
    dynamic_update_slice x7, local copies, waits for them, and re-layouts, body(): slab = lax.dynamic_update_slice(slab, up, (near_at, 0))  15.1 us
    dynamic_update_slice x7, local copies, waits for them, and re-layouts, body(): slab = lax.dynamic_update_slice(slab, down, (far_at, 0))  14 us
  transfers between devices with their start and end apart: 55, of which 41 were waited for; matrix products, arithmetic and copies ran while one was open for 21% of the time, Pallas kernels for 0%

profile of v3, /device:TPU:0, one launch (start us, length us, event | category | flops | bytes accessed | tf_op | source)
XLA Modules:
  0.0 576.3 jit_solution(16967466014141658137)
XLA Ops:
  0.0 4.6 fusion.32
  4.6 3.0 collective-permute-start
  9.5 4.7 broadcast_select_fusion.27
  18.3 10.8 %collective-permute-done.3 = f32[224,448]{1,0:T(8,128)S(1)} collective-permute-done((f32[224,448]{1,0:T(8,128)S(1)}, f32[224,448]{1,0:T(8,128)S(1)}, u32[]{:S(2)}, u32[]{:S(2)}) %collective-permute-start.3) | collective-permute-done | bytes 401440 | tf_op jit(solution)/shard_map/ppermute | solution.py:32
  34.0 18.7 %collective-permute-done = f32[224,2304]{1,0:T(8,128)S(1)} collective-permute-done((f32[224,2304]{1,0:T(8,128)}, f32[224,2304]{1,0:T(8,128)S(1)}, u32[]{:S(2)}, u32[]{:S(2)}) %collective-permute-start) | collective-permute-done | bytes 2064416 | tf_op jit(solution)/shard_map/ppermute | solution.py:27
  54.6 4.8 fusion.34
  61.3 2.9 broadcast_select_fusion.24
  64.2 2.3 broadcast_in_dim.8
  70.0 11.2 %collective-permute-done.8 = f32[224,448]{1,0:T(8,128)S(1)} collective-permute-done((f32[224,448]{1,0:T(8,128)S(1)}, f32[224,448]{1,0:T(8,128)S(1)}, u32[]{:S(2)}, u32[]{:S(2)}) %collective-permute-start.8) | collective-permute-done | bytes 401440 | tf_op jit(solution)/shard_map/ppermute | solution.py:32
  84.5 20.7 %collective-permute-done.5 = f32[224,2304]{1,0:T(8,128)} collective-permute-done((f32[224,2304]{1,0:T(8,128)S(1)}, f32[224,2304]{1,0:T(8,128)}, u32[]{:S(2)}, u32[]{:S(2)}) %collective-permute-start.5) | collective-permute-done | bytes 2064416 | tf_op jit(solution)/shard_map/ppermute | solution.py:27
  107.0 3.5 fusion.35
  111.2 4.5 broadcast_select_fusion.21
  120.4 3.0 constant_dynamic-update-slice_fusion.11
  123.4 8.1 %collective-permute-done.13 = f32[224,448]{1,0:T(8,128)S(1)} collective-permute-done((f32[224,448]{1,0:T(8,128)S(1)}, f32[224,448]{1,0:T(8,128)S(1)}, u32[]{:S(2)}, u32[]{:S(2)}) %collective-permute-start.13) | collective-permute-done | bytes 401440 | tf_op jit(solution)/shard_map/ppermute | solution.py:32
  131.7 3.2 constant_dynamic-update-slice_fusion.10
  135.9 19.2 %collective-permute-done.10 = f32[224,2304]{1,0:T(8,128)} collective-permute-done((f32[224,2304]{1,0:T(8,128)}, f32[224,2304]{1,0:T(8,128)}, u32[]{:S(2)}, u32[]{:S(2)}) %collective-permute-start.10) | collective-permute-done | bytes 2064416 | tf_op jit(solution)/shard_map/ppermute | solution.py:27
  156.6 2.1 fusion.36
  159.3 4.7 broadcast_select_fusion.18
  176.3 3.0 constant_dynamic-update-slice_fusion.9
  179.4 8.5 %collective-permute-done.18 = f32[224,448]{1,0:T(8,128)S(1)} collective-permute-done((f32[224,448]{1,0:T(8,128)S(1)}, f32[224,448]{1,0:T(8,128)S(1)}, u32[]{:S(2)}, u32[]{:S(2)}) %collective-permute-start.18) | collective-permute-done | bytes 401440 | tf_op jit(solution)/shard_map/ppermute | solution.py:32
  189.9 12.1 %collective-permute-done.15 = f32[224,2304]{1,0:T(8,128)} collective-permute-done((f32[224,2304]{1,0:T(8,128)}, f32[224,2304]{1,0:T(8,128)}, u32[]{:S(2)}, u32[]{:S(2)}) %collective-permute-start.15) | collective-permute-done | bytes 2064416 | tf_op jit(solution)/shard_map/ppermute | solution.py:27
  203.8 3.7 fusion.37
  208.1 3.8 broadcast_select_fusion.15
  215.4 3.0 constant_dynamic-update-slice_fusion.7
  218.4 8.0 %collective-permute-done.23 = f32[224,448]{1,0:T(8,128)S(1)} collective-permute-done((f32[224,448]{1,0:T(8,128)S(1)}, f32[224,448]{1,0:T(8,128)S(1)}, u32[]{:S(2)}, u32[]{:S(2)}) %collective-permute-start.23) | collective-permute-done | bytes 401440 | tf_op jit(solution)/shard_map/ppermute | solution.py:32
  226.6 3.1 constant_dynamic-update-slice_fusion.6
  229.8 20.0 %collective-permute-done.20 = f32[224,2304]{1,0:T(8,128)S(1)} collective-permute-done((f32[224,2304]{1,0:T(8,128)}, f32[224,2304]{1,0:T(8,128)S(1)}, u32[]{:S(2)}, u32[]{:S(2)}) %collective-permute-start.20) | collective-permute-done | bytes 2064416 | tf_op jit(solution)/shard_map/ppermute | solution.py:27
  249.7 2.4 collective-permute-start.26
  254.3 2.1 broadcast_select_fusion.12
  261.5 9.6 %collective-permute-done.28 = f32[224,448]{1,0:T(8,128)S(1)} collective-permute-done((f32[224,448]{1,0:T(8,128)S(1)}, f32[224,448]{1,0:T(8,128)S(1)}, u32[]{:S(2)}, u32[]{:S(2)}) %collective-permute-start.28) | collective-permute-done | bytes 401440 | tf_op jit(solution)/shard_map/ppermute | solution.py:32
  273.2 21.7 %collective-permute-done.25 = f32[224,2304]{1,0:T(8,128)S(1)} collective-permute-done((f32[224,2304]{1,0:T(8,128)S(1)}, f32[224,2304]{1,0:T(8,128)S(1)}, u32[]{:S(2)}, u32[]{:S(2)}) %collective-permute-start.25) | collective-permute-done | bytes 2064416 | tf_op jit(solution)/shard_map/ppermute | solution.py:27
  299.4 2.1 broadcast_select_fusion.9
  306.8 9.4 %collective-permute-done.33 = f32[224,448]{1,0:T(8,128)S(1)} collective-permute-done((f32[224,448]{1,0:T(8,128)S(1)}, f32[224,448]{1,0:T(8,128)S(1)}, u32[]{:S(2)}, u32[]{:S(2)}) %collective-permute-start.33) | collective-permute-done | bytes 401440 | tf_op jit(solution)/shard_map/ppermute | solution.py:32
  318.3 19.8 %collective-permute-done.30 = f32[224,2304]{1,0:T(8,128)S(1)} collective-permute-done((f32[224,2304]{1,0:T(8,128)S(1)}, f32[224,2304]{1,0:T(8,128)S(1)}, u32[]{:S(2)}, u32[]{:S(2)}) %collective-permute-start.30) | collective-permute-done | bytes 2064416 | tf_op jit(solution)/shard_map/ppermute | solution.py:27
  338.1 2.1 fusion.40
  346.0 11.0 %collective-permute-done.36 = f32[224,448]{1,0:T(8,128)S(1)} collective-permute-done((f32[224,448]{1,0:T(8,128)S(1)}, f32[224,448]{1,0:T(8,128)S(1)}, u32[]{:S(2)}, u32[]{:S(2)}) %collective-permute-start.36) | collective-permute-done | bytes 401440 | tf_op jit(solution)/shard_map/ppermute | solution.py:32
  363.9 2.1 dynamic-slice_bitcast_fusion.3
  378.2 15.9 %collective-permute-done.38 = f32[224,896]{1,0:T(8,128)S(1)} collective-permute-done((f32[224,896]{1,0:T(8,128)S(1)}, f32[224,896]{1,0:T(8,128)S(1)}, u32[]{:S(2)}, u32[]{:S(2)}) %collective-permute-start.38) | collective-permute-done | bytes 802848 | tf_op jit(solution)/shard_map/ppermute | solution.py:27
  399.0 14.2 %collective-permute-done.40 = f32[224,896]{1,0:T(8,128)S(1)} collective-permute-done((f32[224,896]{1,0:T(8,128)S(1)}, f32[224,896]{1,0:T(8,128)S(1)}, u32[]{:S(2)}, u32[]{:S(2)}) %collective-permute-start.40) | collective-permute-done | bytes 802848 | tf_op jit(solution)/shard_map/ppermute | solution.py:27
  418.2 13.8 %collective-permute-done.42 = f32[224,896]{1,0:T(8,128)S(1)} collective-permute-done((f32[224,896]{1,0:T(8,128)S(1)}, f32[224,896]{1,0:T(8,128)S(1)}, u32[]{:S(2)}, u32[]{:S(2)}) %collective-permute-start.42) | collective-permute-done | bytes 802848 | tf_op jit(solution)/shard_map/ppermute | solution.py:27
  436.7 13.2 %collective-permute-done.44 = f32[224,896]{1,0:T(8,128)S(1)} collective-permute-done((f32[224,896]{1,0:T(8,128)S(1)}, f32[224,896]{1,0:T(8,128)S(1)}, u32[]{:S(2)}, u32[]{:S(2)}) %collective-permute-start.44) | collective-permute-done | bytes 802848 | tf_op jit(solution)/shard_map/ppermute | solution.py:27
  454.9 13.1 %collective-permute-done.46 = f32[224,896]{1,0:T(8,128)S(1)} collective-permute-done((f32[224,896]{1,0:T(8,128)S(1)}, f32[224,896]{1,0:T(8,128)S(1)}, u32[]{:S(2)}, u32[]{:S(2)}) %collective-permute-start.46) | collective-permute-done | bytes 802848 | tf_op jit(solution)/shard_map/ppermute | solution.py:27
  473.0 13.5 %collective-permute-done.48 = f32[224,896]{1,0:T(8,128)S(1)} collective-permute-done((f32[224,896]{1,0:T(8,128)S(1)}, f32[224,896]{1,0:T(8,128)S(1)}, u32[]{:S(2)}, u32[]{:S(2)}) %collective-permute-start.48) | collective-permute-done | bytes 802848 | tf_op jit(solution)/shard_map/ppermute | solution.py:27
  491.4 9.1 %collective-permute-done.50 = f32[224,896]{1,0:T(8,128)S(1)} collective-permute-done((f32[224,896]{1,0:T(8,128)S(1)}, f32[224,896]{1,0:T(8,128)S(1)}, u32[]{:S(2)}, u32[]{:S(2)}) %collective-permute-start.50) | collective-permute-done | bytes 802848 | tf_op jit(solution)/shard_map/ppermute | solution.py:27
  507.8 27.1 %collective-permute-done.53 = f32[448,896]{1,0:T(8,128)} collective-permute-done((f32[448,896]{1,0:T(8,128)}, f32[448,896]{1,0:T(8,128)}, u32[]{:S(2)}, u32[]{:S(2)}) %collective-permute-start.53) | collective-permute-done | bytes 1605664 | tf_op jit(solution)/shard_map/ppermute | solution.py:32
  534.9 3.0 constant_dynamic-update-slice_fusion.1
  541.4 15.3 %fusion.2 = f32[448,2304]{1,0:T(8,128)S(1)} fusion(f32[3584,2304]{1,0:T(8,128)} %constant_dynamic-update-slice_fusion, s32[]{:T(128)S(6)} %select_n.368, f32[448,896]{1,0:T(8,128)S(1)} %get-tuple-element.124, f32[448,896]{1,0:T(8,128)S(1)} %get-tuple-element.123), kind=kOutput, calls=%fused_computation.2 | convolution fusion | flops 11098931200 | bytes 23855108 | tf_op jit(solution)/shard_map/dot_general | solution.py:15
  559.4 16.7 %fusion.10 = f32[448,2304]{1,0:T(8,128)} fusion(f32[448,2304]{1,0:T(8,128)S(1)} %fusion.2, f32[3584,2304]{1,0:T(8,128)} %constant_dynamic-update-slice_fusion, s32[]{:T(128)S(6)} %select_n.371, f32[448,2304]{1,0:T(8,128)S(1)} %copy-done.4, f32[448,896]{1,0:T(8,128)S(1)} %get-tuple-element.122, f32[448,896]{1,0:T(8,128)S(1)} %get-tuple-element.121), kind=kOutput, calls=%fused_computation.6 | convolution fusion | flops 11103059968 | bytes 32112644 | tf_op jit(solution)/shard_map/dot_general | solution.py:15
  (261 shorter events, 126.7 us)
Async XLA Ops:
  4.6 48.1 %collective-permute-start = (f32[224,2304]{1,0:T(8,128)}, f32[224,2304]{1,0:T(8,128)S(1)}, u32[]{:S(2)}, u32[]{:S(2)}) collective-permute-start(f32[224,2304]{1,0:T(8,128)} %get-tuple-element.116), channel_id=1, source_target_pairs={{0,8},{8,16},{16,24},{24,28},{28,20},{20,12},{12,4},{4,0},{1,9},{9... | collective-permute-start | bytes 6193160 | tf_op jit(solution)/shard_map/ppermute | solution.py:27
  7.6 46.7 %collective-permute-start.1 = (f32[224,2304]{1,0:T(8,128)}, f32[224,2304]{1,0:T(8,128)}, u32[]{:S(2)}, u32[]{:S(2)}) collective-permute-start(f32[224,2304]{1,0:T(8,128)} %get-tuple-element.115), channel_id=1, source_target_pairs={{0,4},{8,0},{16,8},{24,16},{28,24},{20,28},{12,20},{4,12},{1,5},{9... | collective-permute-start | bytes 6193160 | tf_op jit(solution)/shard_map/ppermute | solution.py:27
  16.3 12.8 %collective-permute-start.3 = (f32[224,448]{1,0:T(8,128)S(1)}, f32[224,448]{1,0:T(8,128)S(1)}, u32[]{:S(2)}, u32[]{:S(2)}) collective-permute-start(f32[224,448]{1,0:T(8,128)S(1)} %select_add_fusion.7), channel_id=1, source_target_pairs={{0,2},{1,3},{2,0},{3,1},{4,6},{5,7},{6,4},{7,5},{8,10},{9,11},{10,... | collective-permute-start | bytes 1204232 | tf_op jit(solution)/shard_map/ppermute | solution.py:32
  29.2 2.9 collective-permute-start.4
  54.3 50.8 %collective-permute-start.6 = (f32[224,2304]{1,0:T(8,128)}, f32[224,2304]{1,0:T(8,128)}, u32[]{:S(2)}, u32[]{:S(2)}) collective-permute-start(f32[224,2304]{1,0:T(8,128)} %collective-permute-done.1), channel_id=1, source_target_pairs={{0,4},{8,0},{16,8},{24,16},{28,24},{20,28},{12,20},{4,12},{1,5},{9... | collective-permute-start | bytes 6193160 | tf_op jit(solution)/shard_map/ppermute | solution.py:27
  59.5 45.7 %collective-permute-start.5 = (f32[224,2304]{1,0:T(8,128)S(1)}, f32[224,2304]{1,0:T(8,128)}, u32[]{:S(2)}, u32[]{:S(2)}) collective-permute-start(f32[224,2304]{1,0:T(8,128)S(1)} %collective-permute-done), channel_id=1, source_target_pairs={{0,8},{8,16},{16,24},{24,28},{28,20},{20,12},{12,4},{4,0},{1,9},{9... | collective-permute-start | bytes 6193160 | tf_op jit(solution)/shard_map/ppermute | solution.py:27
  64.2 2.8 collective-permute-start.7
  68.3 13.0 %collective-permute-start.8 = (f32[224,448]{1,0:T(8,128)S(1)}, f32[224,448]{1,0:T(8,128)S(1)}, u32[]{:S(2)}, u32[]{:S(2)}) collective-permute-start(f32[224,448]{1,0:T(8,128)S(1)} %select_add_fusion.6), channel_id=1, source_target_pairs={{0,2},{1,3},{2,0},{3,1},{4,6},{5,7},{6,4},{7,5},{8,10},{9,11},{10,... | collective-permute-start | bytes 1204232 | tf_op jit(solution)/shard_map/ppermute | solution.py:32
  105.1 49.9 %collective-permute-start.11 = (f32[224,2304]{1,0:T(8,128)}, f32[224,2304]{1,0:T(8,128)S(1)}, u32[]{:S(2)}, u32[]{:S(2)}) collective-permute-start(f32[224,2304]{1,0:T(8,128)} %collective-permute-done.6), channel_id=1, source_target_pairs={{0,4},{8,0},{16,8},{24,16},{28,24},{20,28},{12,20},{4,12},{1,5},{9... | collective-permute-start | bytes 6193160 | tf_op jit(solution)/shard_map/ppermute | solution.py:27
  110.5 44.6 %collective-permute-start.10 = (f32[224,2304]{1,0:T(8,128)}, f32[224,2304]{1,0:T(8,128)}, u32[]{:S(2)}, u32[]{:S(2)}) collective-permute-start(f32[224,2304]{1,0:T(8,128)} %collective-permute-done.5), channel_id=1, source_target_pairs={{0,8},{8,16},{16,24},{24,28},{28,20},{20,12},{12,4},{4,0},{1,9},{9... | collective-permute-start | bytes 6193160 | tf_op jit(solution)/shard_map/ppermute | solution.py:27
  115.7 2.0 collective-permute-start.12
  118.9 12.6 %collective-permute-start.13 = (f32[224,448]{1,0:T(8,128)S(1)}, f32[224,448]{1,0:T(8,128)S(1)}, u32[]{:S(2)}, u32[]{:S(2)}) collective-permute-start(f32[224,448]{1,0:T(8,128)S(1)} %select_add_fusion.5), channel_id=1, source_target_pairs={{0,2},{1,3},{2,0},{3,1},{4,6},{5,7},{6,4},{7,5},{8,10},{9,11},{10,... | collective-permute-start | bytes 1204232 | tf_op jit(solution)/shard_map/ppermute | solution.py:32
  131.6 3.3 collective-permute-start.14
  155.1 47.0 %collective-permute-start.16 = (f32[224,2304]{1,0:T(8,128)S(1)}, f32[224,2304]{1,0:T(8,128)}, u32[]{:S(2)}, u32[]{:S(2)}) collective-permute-start(f32[224,2304]{1,0:T(8,128)S(1)} %collective-permute-done.11), channel_id=1, source_target_pairs={{0,4},{8,0},{16,8},{24,16},{28,24},{20,28},{12,20},{4,12},{1,5},{9... | collective-permute-start | bytes 6193160 | tf_op jit(solution)/shard_map/ppermute | solution.py:27
  158.7 43.3 %collective-permute-start.15 = (f32[224,2304]{1,0:T(8,128)}, f32[224,2304]{1,0:T(8,128)}, u32[]{:S(2)}, u32[]{:S(2)}) collective-permute-start(f32[224,2304]{1,0:T(8,128)} %collective-permute-done.10), channel_id=1, source_target_pairs={{0,8},{8,16},{16,24},{24,28},{28,20},{20,12},{12,4},{4,0},{1,9},{9... | collective-permute-start | bytes 6193160 | tf_op jit(solution)/shard_map/ppermute | solution.py:27
  164.0 8.6 %collective-permute-start.17 = (f32[224,448]{1,0:T(8,128)}, f32[224,448]{1,0:T(8,128)}, u32[]{:S(2)}, u32[]{:S(2)}) collective-permute-start(f32[224,448]{1,0:T(8,128)} %get-tuple-element.149), channel_id=1, source_target_pairs={{0,1},{1,0},{2,3},{3,2},{4,5},{5,4},{6,7},{7,6},{8,9},{9,8},{10,11... | collective-permute-start | bytes 1204232 | tf_op jit(solution)/shard_map/ppermute | solution.py:32
  174.8 13.0 %collective-permute-start.18 = (f32[224,448]{1,0:T(8,128)S(1)}, f32[224,448]{1,0:T(8,128)S(1)}, u32[]{:S(2)}, u32[]{:S(2)}) collective-permute-start(f32[224,448]{1,0:T(8,128)S(1)} %select_add_fusion.4), channel_id=1, source_target_pairs={{0,2},{1,3},{2,0},{3,1},{4,6},{5,7},{6,4},{7,5},{8,10},{9,11},{10,... | collective-permute-start | bytes 1204232 | tf_op jit(solution)/shard_map/ppermute | solution.py:32
  187.9 1.9 collective-permute-start.19
  202.1 47.7 %collective-permute-start.21 = (f32[224,2304]{1,0:T(8,128)}, f32[224,2304]{1,0:T(8,128)S(1)}, u32[]{:S(2)}, u32[]{:S(2)}) collective-permute-start(f32[224,2304]{1,0:T(8,128)} %collective-permute-done.16), channel_id=1, source_target_pairs={{0,4},{8,0},{16,8},{24,16},{28,24},{20,28},{12,20},{4,12},{1,5},{9... | collective-permute-start | bytes 6193160 | tf_op jit(solution)/shard_map/ppermute | solution.py:27
  207.6 42.2 %collective-permute-start.20 = (f32[224,2304]{1,0:T(8,128)}, f32[224,2304]{1,0:T(8,128)S(1)}, u32[]{:S(2)}, u32[]{:S(2)}) collective-permute-start(f32[224,2304]{1,0:T(8,128)} %collective-permute-done.15), channel_id=1, source_target_pairs={{0,8},{8,16},{16,24},{24,28},{28,20},{20,12},{12,4},{4,0},{1,9},{9... | collective-permute-start | bytes 6193160 | tf_op jit(solution)/shard_map/ppermute | solution.py:27
  211.8 1.9 collective-permute-start.22
  213.8 12.6 %collective-permute-start.23 = (f32[224,448]{1,0:T(8,128)S(1)}, f32[224,448]{1,0:T(8,128)S(1)}, u32[]{:S(2)}, u32[]{:S(2)}) collective-permute-start(f32[224,448]{1,0:T(8,128)S(1)} %select_add_fusion.3), channel_id=1, source_target_pairs={{0,2},{1,3},{2,0},{3,1},{4,6},{5,7},{6,4},{7,5},{8,10},{9,11},{10,... | collective-permute-start | bytes 1204232 | tf_op jit(solution)/shard_map/ppermute | solution.py:32
  226.5 3.1 collective-permute-start.24
  249.7 45.2 %collective-permute-start.26 = (f32[224,2304]{1,0:T(8,128)S(1)}, f32[224,2304]{1,0:T(8,128)S(1)}, u32[]{:S(2)}, u32[]{:S(2)}) collective-permute-start(f32[224,2304]{1,0:T(8,128)S(1)} %collective-permute-done.21), channel_id=1, source_target_pairs={{0,4},{8,0},{16,8},{24,16},{28,24},{20,28},{12,20},{4,12},{1,5},{9... | collective-permute-start | bytes 6193160 | tf_op jit(solution)/shard_map/ppermute | solution.py:27
  254.3 40.7 %collective-permute-start.25 = (f32[224,2304]{1,0:T(8,128)S(1)}, f32[224,2304]{1,0:T(8,128)S(1)}, u32[]{:S(2)}, u32[]{:S(2)}) collective-permute-start(f32[224,2304]{1,0:T(8,128)S(1)} %collective-permute-done.20), channel_id=1, source_target_pairs={{0,8},{8,16},{16,24},{24,28},{28,20},{20,12},{12,4},{4,0},{1,9},{9... | collective-permute-start | bytes 6193160 | tf_op jit(solution)/shard_map/ppermute | solution.py:27
  258.5 12.6 %collective-permute-start.28 = (f32[224,448]{1,0:T(8,128)S(1)}, f32[224,448]{1,0:T(8,128)S(1)}, u32[]{:S(2)}, u32[]{:S(2)}) collective-permute-start(f32[224,448]{1,0:T(8,128)S(1)} %select_add_fusion.2), channel_id=1, source_target_pairs={{0,2},{1,3},{2,0},{3,1},{4,6},{5,7},{6,4},{7,5},{8,10},{9,11},{10,... | collective-permute-start | bytes 1204232 | tf_op jit(solution)/shard_map/ppermute | solution.py:32
  294.9 43.1 %collective-permute-start.31 = (f32[224,2304]{1,0:T(8,128)S(1)}, f32[224,2304]{1,0:T(8,128)S(1)}, u32[]{:S(2)}, u32[]{:S(2)}) collective-permute-start(f32[224,2304]{1,0:T(8,128)S(1)} %collective-permute-done.26), channel_id=1, source_target_pairs={{0,4},{8,0},{16,8},{24,16},{28,24},{20,28},{12,20},{4,12},{1,5},{9... | collective-permute-start | bytes 6193160 | tf_op jit(solution)/shard_map/ppermute | solution.py:27
  299.2 38.9 %collective-permute-start.30 = (f32[224,2304]{1,0:T(8,128)S(1)}, f32[224,2304]{1,0:T(8,128)S(1)}, u32[]{:S(2)}, u32[]{:S(2)}) collective-permute-start(f32[224,2304]{1,0:T(8,128)S(1)} %collective-permute-done.25), channel_id=1, source_target_pairs={{0,8},{8,16},{16,24},{24,28},{28,20},{20,12},{12,4},{4,0},{1,9},{9... | collective-permute-start | bytes 6193160 | tf_op jit(solution)/shard_map/ppermute | solution.py:27
  303.6 12.6 %collective-permute-start.33 = (f32[224,448]{1,0:T(8,128)S(1)}, f32[224,448]{1,0:T(8,128)S(1)}, u32[]{:S(2)}, u32[]{:S(2)}) collective-permute-start(f32[224,448]{1,0:T(8,128)S(1)} %select_add_fusion.1), channel_id=1, source_target_pairs={{0,2},{1,3},{2,0},{3,1},{4,6},{5,7},{6,4},{7,5},{8,10},{9,11},{10,... | collective-permute-start | bytes 1204232 | tf_op jit(solution)/shard_map/ppermute | solution.py:32
  344.4 12.6 %collective-permute-start.36 = (f32[224,448]{1,0:T(8,128)S(1)}, f32[224,448]{1,0:T(8,128)S(1)}, u32[]{:S(2)}, u32[]{:S(2)}) collective-permute-start(f32[224,448]{1,0:T(8,128)S(1)} %select_add_fusion), channel_id=1, source_target_pairs={{0,2},{1,3},{2,0},{3,1},{4,6},{5,7},{6,4},{7,5},{8,10},{9,11},{10,... | collective-permute-start | bytes 1204232 | tf_op jit(solution)/shard_map/ppermute | solution.py:32
  357.1 1.9 collective-permute-start.37
  374.1 20.0 %collective-permute-start.38 = (f32[224,896]{1,0:T(8,128)S(1)}, f32[224,896]{1,0:T(8,128)S(1)}, u32[]{:S(2)}, u32[]{:S(2)}) collective-permute-start(f32[224,896]{1,0:T(8,128)S(1)} %get-tuple-element.126), channel_id=1, source_target_pairs={{0,8},{8,16},{16,24},{24,28},{28,20},{20,12},{12,4},{4,0},{1,9},{9... | collective-permute-start | bytes 2408456 | tf_op jit(solution)/shard_map/ppermute | solution.py:27
  374.7 19.7 %collective-permute-start.39 = (f32[224,896]{1,0:T(8,128)S(1)}, f32[224,896]{1,0:T(8,128)S(1)}, u32[]{:S(2)}, u32[]{:S(2)}) collective-permute-start(f32[224,896]{1,0:T(8,128)S(1)} %get-tuple-element.125), channel_id=1, source_target_pairs={{0,4},{8,0},{16,8},{24,16},{28,24},{20,28},{12,20},{4,12},{1,5},{9... | collective-permute-start | bytes 2408456 | tf_op jit(solution)/shard_map/ppermute | solution.py:27
  394.4 18.8 %collective-permute-start.40 = (f32[224,896]{1,0:T(8,128)S(1)}, f32[224,896]{1,0:T(8,128)S(1)}, u32[]{:S(2)}, u32[]{:S(2)}) collective-permute-start(f32[224,896]{1,0:T(8,128)S(1)} %collective-permute-done.38), channel_id=1, source_target_pairs={{0,8},{8,16},{16,24},{24,28},{28,20},{20,12},{12,4},{4,0},{1,9},{9... | collective-permute-start | bytes 2408456 | tf_op jit(solution)/shard_map/ppermute | solution.py:27
  394.8 19.1 %collective-permute-start.41 = (f32[224,896]{1,0:T(8,128)S(1)}, f32[224,896]{1,0:T(8,128)S(1)}, u32[]{:S(2)}, u32[]{:S(2)}) collective-permute-start(f32[224,896]{1,0:T(8,128)S(1)} %collective-permute-done.39), channel_id=1, source_target_pairs={{0,4},{8,0},{16,8},{24,16},{28,24},{20,28},{12,20},{4,12},{1,5},{9... | collective-permute-start | bytes 2408456 | tf_op jit(solution)/shard_map/ppermute | solution.py:27
  413.9 18.0 %collective-permute-start.42 = (f32[224,896]{1,0:T(8,128)S(1)}, f32[224,896]{1,0:T(8,128)S(1)}, u32[]{:S(2)}, u32[]{:S(2)}) collective-permute-start(f32[224,896]{1,0:T(8,128)S(1)} %collective-permute-done.40), channel_id=1, source_target_pairs={{0,8},{8,16},{16,24},{24,28},{28,20},{20,12},{12,4},{4,0},{1,9},{9... | collective-permute-start | bytes 2408456 | tf_op jit(solution)/shard_map/ppermute | solution.py:27
  414.9 17.6 %collective-permute-start.43 = (f32[224,896]{1,0:T(8,128)S(1)}, f32[224,896]{1,0:T(8,128)S(1)}, u32[]{:S(2)}, u32[]{:S(2)}) collective-permute-start(f32[224,896]{1,0:T(8,128)S(1)} %collective-permute-done.41), channel_id=1, source_target_pairs={{0,4},{8,0},{16,8},{24,16},{28,24},{20,28},{12,20},{4,12},{1,5},{9... | collective-permute-start | bytes 2408456 | tf_op jit(solution)/shard_map/ppermute | solution.py:27
  432.5 17.5 %collective-permute-start.44 = (f32[224,896]{1,0:T(8,128)S(1)}, f32[224,896]{1,0:T(8,128)S(1)}, u32[]{:S(2)}, u32[]{:S(2)}) collective-permute-start(f32[224,896]{1,0:T(8,128)S(1)} %collective-permute-done.42), channel_id=1, source_target_pairs={{0,8},{8,16},{16,24},{24,28},{28,20},{20,12},{12,4},{4,0},{1,9},{9... | collective-permute-start | bytes 2408456 | tf_op jit(solution)/shard_map/ppermute | solution.py:27
  432.9 17.8 %collective-permute-start.45 = (f32[224,896]{1,0:T(8,128)S(1)}, f32[224,896]{1,0:T(8,128)S(1)}, u32[]{:S(2)}, u32[]{:S(2)}) collective-permute-start(f32[224,896]{1,0:T(8,128)S(1)} %collective-permute-done.43), channel_id=1, source_target_pairs={{0,4},{8,0},{16,8},{24,16},{28,24},{20,28},{12,20},{4,12},{1,5},{9... | collective-permute-start | bytes 2408456 | tf_op jit(solution)/shard_map/ppermute | solution.py:27
  450.7 17.3 %collective-permute-start.46 = (f32[224,896]{1,0:T(8,128)S(1)}, f32[224,896]{1,0:T(8,128)S(1)}, u32[]{:S(2)}, u32[]{:S(2)}) collective-permute-start(f32[224,896]{1,0:T(8,128)S(1)} %collective-permute-done.44), channel_id=1, source_target_pairs={{0,8},{8,16},{16,24},{24,28},{28,20},{20,12},{12,4},{4,0},{1,9},{9... | collective-permute-start | bytes 2408456 | tf_op jit(solution)/shard_map/ppermute | solution.py:27
  450.9 17.8 %collective-permute-start.47 = (f32[224,896]{1,0:T(8,128)S(1)}, f32[224,896]{1,0:T(8,128)S(1)}, u32[]{:S(2)}, u32[]{:S(2)}) collective-permute-start(f32[224,896]{1,0:T(8,128)S(1)} %collective-permute-done.45), channel_id=1, source_target_pairs={{0,4},{8,0},{16,8},{24,16},{28,24},{20,28},{12,20},{4,12},{1,5},{9... | collective-permute-start | bytes 2408456 | tf_op jit(solution)/shard_map/ppermute | solution.py:27
  468.7 17.7 %collective-permute-start.48 = (f32[224,896]{1,0:T(8,128)S(1)}, f32[224,896]{1,0:T(8,128)S(1)}, u32[]{:S(2)}, u32[]{:S(2)}) collective-permute-start(f32[224,896]{1,0:T(8,128)S(1)} %collective-permute-done.46), channel_id=1, source_target_pairs={{0,8},{8,16},{16,24},{24,28},{28,20},{20,12},{12,4},{4,0},{1,9},{9... | collective-permute-start | bytes 2408456 | tf_op jit(solution)/shard_map/ppermute | solution.py:27
  469.4 17.6 %collective-permute-start.49 = (f32[224,896]{1,0:T(8,128)S(1)}, f32[224,896]{1,0:T(8,128)S(1)}, u32[]{:S(2)}, u32[]{:S(2)}) collective-permute-start(f32[224,896]{1,0:T(8,128)S(1)} %collective-permute-done.47), channel_id=1, source_target_pairs={{0,4},{8,0},{16,8},{24,16},{28,24},{20,28},{12,20},{4,12},{1,5},{9... | collective-permute-start | bytes 2408456 | tf_op jit(solution)/shard_map/ppermute | solution.py:27
  487.0 13.5 %collective-permute-start.50 = (f32[224,896]{1,0:T(8,128)S(1)}, f32[224,896]{1,0:T(8,128)S(1)}, u32[]{:S(2)}, u32[]{:S(2)}) collective-permute-start(f32[224,896]{1,0:T(8,128)S(1)} %collective-permute-done.48), channel_id=1, source_target_pairs={{0,8},{8,16},{16,24},{24,28},{28,20},{20,12},{12,4},{4,0},{1,9},{9... | collective-permute-start | bytes 2408456 | tf_op jit(solution)/shard_map/ppermute | solution.py:27
  487.7 13.3 %collective-permute-start.51 = (f32[224,896]{1,0:T(8,128)S(1)}, f32[224,896]{1,0:T(8,128)S(1)}, u32[]{:S(2)}, u32[]{:S(2)}) collective-permute-start(f32[224,896]{1,0:T(8,128)S(1)} %collective-permute-done.49), channel_id=1, source_target_pairs={{0,4},{8,0},{16,8},{24,16},{28,24},{20,28},{12,20},{4,12},{1,5},{9... | collective-permute-start | bytes 2408456 | tf_op jit(solution)/shard_map/ppermute | solution.py:27
  505.1 29.7 %collective-permute-start.53 = (f32[448,896]{1,0:T(8,128)}, f32[448,896]{1,0:T(8,128)}, u32[]{:S(2)}, u32[]{:S(2)}) collective-permute-start(f32[448,896]{1,0:T(8,128)} %multiply_add_fusion), channel_id=1, source_target_pairs={{0,2},{1,3},{2,0},{3,1},{4,6},{5,7},{6,4},{7,5},{8,10},{9,11},{10,... | collective-permute-start | bytes 4816904 | tf_op jit(solution)/shard_map/ppermute | solution.py:32
  506.3 33.0 %collective-permute-start.52 = (f32[448,896]{1,0:T(8,128)}, f32[448,896]{1,0:T(8,128)}, u32[]{:S(2)}, u32[]{:S(2)}) collective-permute-start(f32[448,896]{1,0:T(8,128)} %multiply_add_fusion), channel_id=1, source_target_pairs={{0,1},{1,0},{2,3},{3,2},{4,5},{5,4},{6,7},{7,6},{8,9},{9,8},{10,11... | collective-permute-start | bytes 4816904 | tf_op jit(solution)/shard_map/ppermute | solution.py:32
  534.9 21.9 %collective-permute-start.54 = (f32[448,896]{1,0:T(8,128)}, f32[448,896]{1,0:T(8,128)S(1)}, u32[]{:S(2)}, u32[]{:S(2)}) collective-permute-start(f32[448,896]{1,0:T(8,128)} %collective-permute-done.53), channel_id=1, source_target_pairs={{0,1},{1,0},{2,3},{3,2},{4,5},{5,4},{6,7},{7,6},{8,9},{9,8},{10,11... | collective-permute-start | bytes 4816904 | tf_op jit(solution)/shard_map/ppermute | solution.py:32
  (53 other events, 1068.2 us)

commit v4 on v3

--- a/solution.py
+++ b/solution.py
@@ -73,26 +73,35 @@
             slab = lax.dynamic_update_slice(slab, down, (far_at, 0))
         near_part = product(up, iterate, ((1,), (1,)))
         far_part = product(down, iterate, ((1,), (1,)))
-        near_part, far_part = sum_over_col(near_part, far_part, upper)
+        waiting = [near_part, far_part]
+        if step >= row_count - 2:
+            waiting = list(sum_over_col(near_part, far_part, upper))
         if not last:
-            held = (next_up, next_down, near_part, far_part)
-            if slab is None:
-                next_up, next_down, near_part, far_part = lax.optimization_barrier(held)
-            else:
-                next_up, next_down, near_part, far_part, slab = lax.optimization_barrier(
-                    held + (slab,)
-                )
-            up, down = next_up, next_down
-        near_blocks.append(near_part)
-        far_blocks.append(far_part)
+            held = [next_up, next_down] + waiting
+            if step >= 1:
+                held += [slab]
+                if step < row_count - 2:
+                    held += [near_blocks.pop(), far_blocks.pop()]
+            held = list(lax.optimization_barrier(tuple(held)))
+            up, down, near_part, far_part = held[:4]
+            waiting = held[2:4]
+            if step >= 1:
+                slab = held[4]
+                if step < row_count - 2:
+                    near_blocks.append(held[5])
+                    far_blocks.append(held[6])
+            if step < row_count - 2:
+                waiting = sum_over_col(near_part, far_part, upper)
+        near_blocks.append(waiting[0])
+        far_blocks.append(waiting[1])
 
-    near_all = jnp.stack(near_blocks)
-    far_all = jnp.stack(far_blocks)
+    near_all = jnp.concatenate(near_blocks, axis=0)
+    far_all = jnp.concatenate(far_blocks, axis=0)
     parts = []
     for k in range(per):
         at = my_col * per + k
-        parts.append(lax.dynamic_index_in_dim(near_all, (mine - at) % row_count, 0, False))
-        parts.append(lax.dynamic_index_in_dim(far_all, (at - mine) % row_count, 0, False))
+        parts.append(lax.dynamic_slice_in_dim(near_all, (mine - at) % row_count * near, near))
+        parts.append(lax.dynamic_slice_in_dim(far_all, (at - mine) % row_count * near, near))
     gram_tile = jnp.concatenate(parts, axis=0).T
 
     up, down = gram_tile[:near], gram_tile[near:]
@@ -111,9 +120,14 @@
     tiles = {0: poly_tile}
     for k in range(1, col_count):
         low_bit = k & -k
+        if low_bit == 1 and k > 1:
+            continue
         tiles[k] = swap(tiles[k ^ low_bit], low_bit)
     applied = None
     for k in range(0, col_count, 2):
+        if applied is not None:
+            tiles[k], applied = lax.optimization_barrier((tiles[k], applied))
+            tiles[k + 1] = swap(tiles[k], 1)
         pair = jnp.concatenate(
             [
                 jnp.where(upper, tiles[k + 1], tiles[k]),

time: 585 us -> 591 us (1.010)
  other arithmetic: 18.2 us -> 30.5 us
  matrix products: 97 us -> 109 us
  waiting for transfers between devices: 346 us -> 337 us
  local copies, waits for them, and re-layouts: 53.1 us -> 46 us
    ppermute x27, waiting for transfers between devices: 116 us -> 85.3 us  [swap(): return lax.ppermute(value, 'col', [(k, k ^ bit) for k in range(count)])]
    ppermute x28, waiting for transfers between devices: 231 us -> 251 us  [shift(): return lax.ppermute(value, 'row', pairs)]
    dot_general x34, matrix products: 97 us -> 109 us  [product(): lax.dot_general(left, right, (dims, ((), ())), precision=PREC, preferred_...]
    squeeze x6 -> x0, local copies, waits for them, and re-layouts: 11.1 us -> none  [the longest x3 6.09 us: body(): lax.dynamic_index_in_dim(near_all, (mine - at) % row_count, 0, False)]
    slice x1 -> x3, local copies, waits for them, and re-layouts: 0.11 us -> 6.37 us  [body(): up, down = (gram_tile[:near], gram_tile[near:])]
  transfers between devices with their start and end apart: 55 -> 55, of which waited for: 41 -> 39; matrix products, arithmetic and copies ran while one was open for 21% -> 24% of each run, Pallas kernels for 0% -> 0%
where the time goes in v4:
time: 591 us; the launch traced here: 582 us
  waiting for transfers between devices  337 us (57%)
  matrix products  109 us (18%)
  local copies, waits for them, and re-layouts  46 us (8%)
  starting transfers between devices  45.7 us (8%)
  other arithmetic  30.5 us (5%)
  between operations  14.3 us (2%)
    ppermute x28, waiting for transfers between devices, shift(): return lax.ppermute(value, 'row', pairs)  251 us
    dot_general x34, matrix products, product(): lax.dot_general(left, right, (dims, ((), ())), precision=PREC, preferred_...  109 us
    ppermute x27, waiting for transfers between devices, swap(): return lax.ppermute(value, 'col', [(k, k ^ bit) for k in range(count)])  85.3 us
    ppermute x28, starting transfers between devices, shift(): return lax.ppermute(value, 'row', pairs)  30.5 us
    ppermute x27, starting transfers between devices, swap(): return lax.ppermute(value, 'col', [(k, k ^ bit) for k in range(count)])  15.1 us
  transfers between devices with their start and end apart: 55, of which 39 were waited for; matrix products, arithmetic and copies ran while one was open for 24% of the time, Pallas kernels for 0%

profile of v4, /device:TPU:0, one launch (start us, length us, event | category | flops | bytes accessed | tf_op | source)
XLA Modules:
  0.0 582.1 jit_solution(4557479477259777188)
XLA Ops:
  0.0 4.5 fusion.29
  4.5 3.0 collective-permute-start
  15.4 4.8 fusion.25
  22.1 30.4 %collective-permute-done = f32[224,2304]{1,0:T(8,128)S(1)} collective-permute-done((f32[224,2304]{1,0:T(8,128)}, f32[224,2304]{1,0:T(8,128)S(1)}, u32[]{:S(2)}, u32[]{:S(2)}) %collective-permute-start) | collective-permute-done | bytes 2064416 | tf_op jit(solution)/shard_map/ppermute | solution.py:27
  61.8 3.5 fusion.32
  68.3 11.0 %collective-permute-done.5 = f32[224,448]{1,0:T(8,128)S(1)} collective-permute-done((f32[224,448]{1,0:T(8,128)S(1)}, f32[224,448]{1,0:T(8,128)S(1)}, u32[]{:S(2)}, u32[]{:S(2)}) %collective-permute-start.5) | collective-permute-done | bytes 401440 | tf_op jit(solution)/shard_map/ppermute | solution.py:32
  82.1 17.8 %collective-permute-done.2 = f32[224,2304]{1,0:T(8,128)} collective-permute-done((f32[224,2304]{1,0:T(8,128)S(1)}, f32[224,2304]{1,0:T(8,128)}, u32[]{:S(2)}, u32[]{:S(2)}) %collective-permute-start.2) | collective-permute-done | bytes 2064416 | tf_op jit(solution)/shard_map/ppermute | solution.py:27
  99.9 4.5 collective-permute-done.3
  107.4 4.3 fusion.33
  111.6 4.3 fusion.34
  120.4 9.1 %collective-permute-done.10 = f32[224,448]{1,0:T(8,128)S(1)} collective-permute-done((f32[224,448]{1,0:T(8,128)S(1)}, f32[224,448]{1,0:T(8,128)S(1)}, u32[]{:S(2)}, u32[]{:S(2)}) %collective-permute-start.10) | collective-permute-done | bytes 401440 | tf_op jit(solution)/shard_map/ppermute | solution.py:32
  132.5 20.2 %collective-permute-done.7 = f32[224,2304]{1,0:T(8,128)S(1)} collective-permute-done((f32[224,2304]{1,0:T(8,128)}, f32[224,2304]{1,0:T(8,128)S(1)}, u32[]{:S(2)}, u32[]{:S(2)}) %collective-permute-start.7) | collective-permute-done | bytes 2064416 | tf_op jit(solution)/shard_map/ppermute | solution.py:27
  157.0 2.7 fusion.35
  159.7 2.7 fusion.36
  165.3 10.7 %collective-permute-done.15 = f32[224,448]{1,0:T(8,128)S(1)} collective-permute-done((f32[224,448]{1,0:T(8,128)S(1)}, f32[224,448]{1,0:T(8,128)S(1)}, u32[]{:S(2)}, u32[]{:S(2)}) %collective-permute-start.15) | collective-permute-done | bytes 401440 | tf_op jit(solution)/shard_map/ppermute | solution.py:32
  179.0 23.5 %collective-permute-done.12 = f32[224,2304]{1,0:T(8,128)} collective-permute-done((f32[224,2304]{1,0:T(8,128)S(1)}, f32[224,2304]{1,0:T(8,128)}, u32[]{:S(2)}, u32[]{:S(2)}) %collective-permute-start.12) | collective-permute-done | bytes 2064416 | tf_op jit(solution)/shard_map/ppermute | solution.py:27
  206.7 4.3 fusion.37
  211.0 4.3 fusion.38
  219.8 9.1 %collective-permute-done.20 = f32[224,448]{1,0:T(8,128)S(1)} collective-permute-done((f32[224,448]{1,0:T(8,128)S(1)}, f32[224,448]{1,0:T(8,128)S(1)}, u32[]{:S(2)}, u32[]{:S(2)}) %collective-permute-start.20) | collective-permute-done | bytes 401440 | tf_op jit(solution)/shard_map/ppermute | solution.py:32
  231.9 20.2 %collective-permute-done.17 = f32[224,2304]{1,0:T(8,128)S(1)} collective-permute-done((f32[224,2304]{1,0:T(8,128)}, f32[224,2304]{1,0:T(8,128)S(1)}, u32[]{:S(2)}, u32[]{:S(2)}) %collective-permute-start.17) | collective-permute-done | bytes 2064416 | tf_op jit(solution)/shard_map/ppermute | solution.py:27
  255.3 2.7 fusion.39
  258.0 2.7 fusion.40
  263.6 10.7 %collective-permute-done.25 = f32[224,448]{1,0:T(8,128)S(1)} collective-permute-done((f32[224,448]{1,0:T(8,128)S(1)}, f32[224,448]{1,0:T(8,128)S(1)}, u32[]{:S(2)}, u32[]{:S(2)}) %collective-permute-start.25) | collective-permute-done | bytes 401440 | tf_op jit(solution)/shard_map/ppermute | solution.py:32
  277.9 22.9 %collective-permute-done.22 = f32[224,2304]{1,0:T(8,128)} collective-permute-done((f32[224,2304]{1,0:T(8,128)S(1)}, f32[224,2304]{1,0:T(8,128)}, u32[]{:S(2)}, u32[]{:S(2)}) %collective-permute-start.22) | collective-permute-done | bytes 2064416 | tf_op jit(solution)/shard_map/ppermute | solution.py:27
  300.9 3.5 fusion.41
  306.9 4.5 broadcast_select_fusion.10
  320.5 3.1 constant_dynamic-update-slice_fusion.15
  323.6 8.3 %collective-permute-done.33 = f32[224,448]{1,0:T(8,128)S(1)} collective-permute-done((f32[224,448]{1,0:T(8,128)S(1)}, f32[224,448]{1,0:T(8,128)S(1)}, u32[]{:S(2)}, u32[]{:S(2)}) %collective-permute-start.33) | collective-permute-done | bytes 401440 | tf_op jit(solution)/shard_map/ppermute | solution.py:32
  332.1 3.2 constant_dynamic-update-slice_fusion.14
  337.1 15.7 %collective-permute-done.30 = f32[224,2304]{1,0:T(8,128)} collective-permute-done((f32[224,2304]{1,0:T(8,128)}, f32[224,2304]{1,0:T(8,128)}, u32[]{:S(2)}, u32[]{:S(2)}) %collective-permute-start.30) | collective-permute-done | bytes 2064416 | tf_op jit(solution)/shard_map/ppermute | solution.py:27
  355.0 3.8 broadcast_select_fusion.7
  362.7 10.9 %collective-permute-done.36 = f32[224,448]{1,0:T(8,128)S(1)} collective-permute-done((f32[224,448]{1,0:T(8,128)S(1)}, f32[224,448]{1,0:T(8,128)S(1)}, u32[]{:S(2)}, u32[]{:S(2)}) %collective-permute-start.36) | collective-permute-done | bytes 401440 | tf_op jit(solution)/shard_map/ppermute | solution.py:32
  378.2 2.4 copy.19
  381.0 2.4 copy.20
  388.0 12.9 %collective-permute-done.38 = f32[224,896]{1,0:T(8,128)} collective-permute-done((f32[224,896]{1,0:T(8,128)}, f32[224,896]{1,0:T(8,128)}, u32[]{:S(2)}, u32[]{:S(2)}) %collective-permute-start.38) | collective-permute-done | bytes 802848 | tf_op jit(solution)/shard_map/ppermute | solution.py:27
  400.9 2.5 collective-permute-done.39
  409.3 13.0 %collective-permute-done.40 = f32[224,896]{1,0:T(8,128)S(1)} collective-permute-done((f32[224,896]{1,0:T(8,128)}, f32[224,896]{1,0:T(8,128)S(1)}, u32[]{:S(2)}, u32[]{:S(2)}) %collective-permute-start.40) | collective-permute-done | bytes 802848 | tf_op jit(solution)/shard_map/ppermute | solution.py:27
  427.1 13.3 %collective-permute-done.42 = f32[224,896]{1,0:T(8,128)S(1)} collective-permute-done((f32[224,896]{1,0:T(8,128)S(1)}, f32[224,896]{1,0:T(8,128)S(1)}, u32[]{:S(2)}, u32[]{:S(2)}) %collective-permute-start.42) | collective-permute-done | bytes 802848 | tf_op jit(solution)/shard_map/ppermute | solution.py:27
  445.2 13.3 %collective-permute-done.44 = f32[224,896]{1,0:T(8,128)S(1)} collective-permute-done((f32[224,896]{1,0:T(8,128)S(1)}, f32[224,896]{1,0:T(8,128)S(1)}, u32[]{:S(2)}, u32[]{:S(2)}) %collective-permute-start.44) | collective-permute-done | bytes 802848 | tf_op jit(solution)/shard_map/ppermute | solution.py:27
  463.2 13.3 %collective-permute-done.46 = f32[224,896]{1,0:T(8,128)S(1)} collective-permute-done((f32[224,896]{1,0:T(8,128)S(1)}, f32[224,896]{1,0:T(8,128)S(1)}, u32[]{:S(2)}, u32[]{:S(2)}) %collective-permute-start.46) | collective-permute-done | bytes 802848 | tf_op jit(solution)/shard_map/ppermute | solution.py:27
  481.9 13.1 %collective-permute-done.48 = f32[224,896]{1,0:T(8,128)S(1)} collective-permute-done((f32[224,896]{1,0:T(8,128)S(1)}, f32[224,896]{1,0:T(8,128)S(1)}, u32[]{:S(2)}, u32[]{:S(2)}) %collective-permute-start.48) | collective-permute-done | bytes 802848 | tf_op jit(solution)/shard_map/ppermute | solution.py:27
  500.0 8.9 %collective-permute-done.50 = f32[224,896]{1,0:T(8,128)S(1)} collective-permute-done((f32[224,896]{1,0:T(8,128)S(1)}, f32[224,896]{1,0:T(8,128)S(1)}, u32[]{:S(2)}, u32[]{:S(2)}) %collective-permute-start.50) | collective-permute-done | bytes 802848 | tf_op jit(solution)/shard_map/ppermute | solution.py:27
  516.9 3.1 constant_dynamic-update-slice_fusion.13
  521.5 2.7 copy.39
  526.2 18.6 %fusion.2 = f32[448,2304]{1,0:T(8,128)} fusion(f32[3584,2304]{1,0:T(8,128)} %constant_dynamic-update-slice_fusion.12, s32[]{:T(128)S(6)} %select_n.367, f32[448,896]{0,1:T(8,128)S(1)} %get-tuple-element.144, f32[448,896]{0,1:T(8,128)S(1)} %get-tuple-element.143), kind=kOutput, calls=%fused_computation.2 | convolution fusion | flops 11098931200 | bytes 23855108 | tf_op jit(solution)/shard_map/dot_general | solution.py:15
  544.7 8.3 %collective-permute-done.52 = f32[448,896]{1,0:T(8,128)} collective-permute-done((f32[448,896]{1,0:T(8,128)S(1)}, f32[448,896]{1,0:T(8,128)}, u32[]{:S(2)}, u32[]{:S(2)}) %collective-permute-start.52) | collective-permute-done | bytes 1605664 | tf_op jit(solution)/shard_map/ppermute | solution.py:32
  560.4 18.3 %fusion = f32[448,2304]{1,0:T(8,128)S(1)} fusion(f32[3584,2304]{1,0:T(8,128)} %constant_dynamic-update-slice_fusion.12, s32[]{:T(128)S(6)} %select_n.370, f32[448,896]{0,1:T(8,128)S(1)} %get-tuple-element.142, f32[448,896]{0,1:T(8,128)S(1)} %get-tuple-element.141), kind=kOutput, calls=%fused_computation | convolution fusion | flops 11098931200 | bytes 23855108 | tf_op jit(solution)/shard_map/dot_general | solution.py:15
  578.7 2.8 add_multiply_fusion
  (282 shorter events, 132.4 us)
Async XLA Ops:
  4.5 48.1 %collective-permute-start = (f32[224,2304]{1,0:T(8,128)}, f32[224,2304]{1,0:T(8,128)S(1)}, u32[]{:S(2)}, u32[]{:S(2)}) collective-permute-start(f32[224,2304]{1,0:T(8,128)} %get-tuple-element.140), channel_id=1, source_target_pairs={{0,8},{8,16},{16,24},{24,28},{28,20},{20,12},{12,4},{4,0},{1,9},{9... | collective-permute-start | bytes 6193160 | tf_op jit(solution)/shard_map/ppermute | solution.py:27
  7.5 46.7 %collective-permute-start.1 = (f32[224,2304]{1,0:T(8,128)}, f32[224,2304]{1,0:T(8,128)}, u32[]{:S(2)}, u32[]{:S(2)}) collective-permute-start(f32[224,2304]{1,0:T(8,128)} %get-tuple-element.139), channel_id=1, source_target_pairs={{0,4},{8,0},{16,8},{24,16},{28,24},{20,28},{12,20},{4,12},{1,5},{9... | collective-permute-start | bytes 6193160 | tf_op jit(solution)/shard_map/ppermute | solution.py:27
  54.2 45.6 %collective-permute-start.2 = (f32[224,2304]{1,0:T(8,128)S(1)}, f32[224,2304]{1,0:T(8,128)}, u32[]{:S(2)}, u32[]{:S(2)}) collective-permute-start(f32[224,2304]{1,0:T(8,128)S(1)} %collective-permute-done), channel_id=1, source_target_pairs={{0,8},{8,16},{16,24},{24,28},{28,20},{20,12},{12,4},{4,0},{1,9},{9... | collective-permute-start | bytes 6193160 | tf_op jit(solution)/shard_map/ppermute | solution.py:27
  56.7 8.7 %collective-permute-start.4 = (f32[224,448]{1,0:T(8,128)}, f32[224,448]{1,0:T(8,128)}, u32[]{:S(2)}, u32[]{:S(2)}) collective-permute-start(f32[224,448]{1,0:T(8,128)} %broadcast_select_fusion.27), channel_id=1, source_target_pairs={{0,1},{1,0},{2,3},{3,2},{4,5},{5,4},{6,7},{7,6},{8,9},{9,8},{10,11... | collective-permute-start | bytes 1204232 | tf_op jit(solution)/shard_map/ppermute | solution.py:32
  56.7 47.7 %collective-permute-start.3 = (f32[224,2304]{1,0:T(8,128)}, f32[224,2304]{1,0:T(8,128)}, u32[]{:S(2)}, u32[]{:S(2)}) collective-permute-start(f32[224,2304]{1,0:T(8,128)} %collective-permute-done.1), channel_id=1, source_target_pairs={{0,4},{8,0},{16,8},{24,16},{28,24},{20,28},{12,20},{4,12},{1,5},{9... | collective-permute-start | bytes 6193160 | tf_op jit(solution)/shard_map/ppermute | solution.py:27
  66.5 12.7 %collective-permute-start.5 = (f32[224,448]{1,0:T(8,128)S(1)}, f32[224,448]{1,0:T(8,128)S(1)}, u32[]{:S(2)}, u32[]{:S(2)}) collective-permute-start(f32[224,448]{1,0:T(8,128)S(1)} %select_add_fusion.7), channel_id=1, source_target_pairs={{0,2},{1,3},{2,0},{3,1},{4,6},{5,7},{6,4},{7,5},{8,10},{9,11},{10,... | collective-permute-start | bytes 1204232 | tf_op jit(solution)/shard_map/ppermute | solution.py:32
  105.2 10.8 %collective-permute-start.9 = (f32[224,448]{1,0:T(8,128)}, f32[224,448]{1,0:T(8,128)}, u32[]{:S(2)}, u32[]{:S(2)}) collective-permute-start(f32[224,448]{1,0:T(8,128)} %broadcast_select_fusion.24), channel_id=1, source_target_pairs={{0,1},{1,0},{2,3},{3,2},{4,5},{5,4},{6,7},{7,6},{8,9},{9,8},{10,11... | collective-permute-start | bytes 1204232 | tf_op jit(solution)/shard_map/ppermute | solution.py:32
  105.2 47.6 %collective-permute-start.7 = (f32[224,2304]{1,0:T(8,128)}, f32[224,2304]{1,0:T(8,128)S(1)}, u32[]{:S(2)}, u32[]{:S(2)}) collective-permute-start(f32[224,2304]{1,0:T(8,128)} %collective-permute-done.2), channel_id=1, source_target_pairs={{0,8},{8,16},{16,24},{24,28},{28,20},{20,12},{12,4},{4,0},{1,9},{9... | collective-permute-start | bytes 6193160 | tf_op jit(solution)/shard_map/ppermute | solution.py:27
  106.8 47.4 %collective-permute-start.8 = (f32[224,2304]{1,0:T(8,128)}, f32[224,2304]{1,0:T(8,128)S(1)}, u32[]{:S(2)}, u32[]{:S(2)}) collective-permute-start(f32[224,2304]{1,0:T(8,128)} %collective-permute-done.3), channel_id=1, source_target_pairs={{0,4},{8,0},{16,8},{24,16},{28,24},{20,28},{12,20},{4,12},{1,5},{9... | collective-permute-start | bytes 6193160 | tf_op jit(solution)/shard_map/ppermute | solution.py:27
  117.1 12.4 %collective-permute-start.10 = (f32[224,448]{1,0:T(8,128)S(1)}, f32[224,448]{1,0:T(8,128)S(1)}, u32[]{:S(2)}, u32[]{:S(2)}) collective-permute-start(f32[224,448]{1,0:T(8,128)S(1)} %select_add_fusion.6), channel_id=1, source_target_pairs={{0,2},{1,3},{2,0},{3,1},{4,6},{5,7},{6,4},{7,5},{8,10},{9,11},{10,... | collective-permute-start | bytes 1204232 | tf_op jit(solution)/shard_map/ppermute | solution.py:32
  155.0 7.4 %collective-permute-start.14 = (f32[224,448]{1,0:T(8,128)}, f32[224,448]{1,0:T(8,128)}, u32[]{:S(2)}, u32[]{:S(2)}) collective-permute-start(f32[224,448]{1,0:T(8,128)} %broadcast_select_fusion.21), channel_id=1, source_target_pairs={{0,1},{1,0},{2,3},{3,2},{4,5},{5,4},{6,7},{7,6},{8,9},{9,8},{10,11... | collective-permute-start | bytes 1204232 | tf_op jit(solution)/shard_map/ppermute | solution.py:32
  155.0 47.4 %collective-permute-start.12 = (f32[224,2304]{1,0:T(8,128)S(1)}, f32[224,2304]{1,0:T(8,128)}, u32[]{:S(2)}, u32[]{:S(2)}) collective-permute-start(f32[224,2304]{1,0:T(8,128)S(1)} %collective-permute-done.7), channel_id=1, source_target_pairs={{0,8},{8,16},{16,24},{24,28},{28,20},{20,12},{12,4},{4,0},{1,9},{9... | collective-permute-start | bytes 6193160 | tf_op jit(solution)/shard_map/ppermute | solution.py:27
  156.5 47.2 %collective-permute-start.13 = (f32[224,2304]{1,0:T(8,128)S(1)}, f32[224,2304]{1,0:T(8,128)}, u32[]{:S(2)}, u32[]{:S(2)}) collective-permute-start(f32[224,2304]{1,0:T(8,128)S(1)} %collective-permute-done.8), channel_id=1, source_target_pairs={{0,4},{8,0},{16,8},{24,16},{28,24},{20,28},{12,20},{4,12},{1,5},{9... | collective-permute-start | bytes 6193160 | tf_op jit(solution)/shard_map/ppermute | solution.py:27
  163.6 12.4 %collective-permute-start.15 = (f32[224,448]{1,0:T(8,128)S(1)}, f32[224,448]{1,0:T(8,128)S(1)}, u32[]{:S(2)}, u32[]{:S(2)}) collective-permute-start(f32[224,448]{1,0:T(8,128)S(1)} %select_add_fusion.5), channel_id=1, source_target_pairs={{0,2},{1,3},{2,0},{3,1},{4,6},{5,7},{6,4},{7,5},{8,10},{9,11},{10,... | collective-permute-start | bytes 1204232 | tf_op jit(solution)/shard_map/ppermute | solution.py:32
  204.5 10.8 %collective-permute-start.19 = (f32[224,448]{1,0:T(8,128)}, f32[224,448]{1,0:T(8,128)}, u32[]{:S(2)}, u32[]{:S(2)}) collective-permute-start(f32[224,448]{1,0:T(8,128)} %broadcast_select_fusion.18), channel_id=1, source_target_pairs={{0,1},{1,0},{2,3},{3,2},{4,5},{5,4},{6,7},{7,6},{8,9},{9,8},{10,11... | collective-permute-start | bytes 1204232 | tf_op jit(solution)/shard_map/ppermute | solution.py:32
  204.5 47.6 %collective-permute-start.17 = (f32[224,2304]{1,0:T(8,128)}, f32[224,2304]{1,0:T(8,128)S(1)}, u32[]{:S(2)}, u32[]{:S(2)}) collective-permute-start(f32[224,2304]{1,0:T(8,128)} %collective-permute-done.12), channel_id=1, source_target_pairs={{0,8},{8,16},{16,24},{24,28},{28,20},{20,12},{12,4},{4,0},{1,9},{9... | collective-permute-start | bytes 6193160 | tf_op jit(solution)/shard_map/ppermute | solution.py:27
  205.0 47.5 %collective-permute-start.18 = (f32[224,2304]{1,0:T(8,128)}, f32[224,2304]{1,0:T(8,128)S(1)}, u32[]{:S(2)}, u32[]{:S(2)}) collective-permute-start(f32[224,2304]{1,0:T(8,128)} %collective-permute-done.13), channel_id=1, source_target_pairs={{0,4},{8,0},{16,8},{24,16},{28,24},{20,28},{12,20},{4,12},{1,5},{9... | collective-permute-start | bytes 6193160 | tf_op jit(solution)/shard_map/ppermute | solution.py:27
  216.5 12.4 %collective-permute-start.20 = (f32[224,448]{1,0:T(8,128)S(1)}, f32[224,448]{1,0:T(8,128)S(1)}, u32[]{:S(2)}, u32[]{:S(2)}) collective-permute-start(f32[224,448]{1,0:T(8,128)S(1)} %select_add_fusion.4), channel_id=1, source_target_pairs={{0,2},{1,3},{2,0},{3,1},{4,6},{5,7},{6,4},{7,5},{8,10},{9,11},{10,... | collective-permute-start | bytes 1204232 | tf_op jit(solution)/shard_map/ppermute | solution.py:32
  253.3 7.4 %collective-permute-start.24 = (f32[224,448]{1,0:T(8,128)}, f32[224,448]{1,0:T(8,128)}, u32[]{:S(2)}, u32[]{:S(2)}) collective-permute-start(f32[224,448]{1,0:T(8,128)} %broadcast_select_fusion.15), channel_id=1, source_target_pairs={{0,1},{1,0},{2,3},{3,2},{4,5},{5,4},{6,7},{7,6},{8,9},{9,8},{10,11... | collective-permute-start | bytes 1204232 | tf_op jit(solution)/shard_map/ppermute | solution.py:32
  253.3 47.4 %collective-permute-start.22 = (f32[224,2304]{1,0:T(8,128)S(1)}, f32[224,2304]{1,0:T(8,128)}, u32[]{:S(2)}, u32[]{:S(2)}) collective-permute-start(f32[224,2304]{1,0:T(8,128)S(1)} %collective-permute-done.17), channel_id=1, source_target_pairs={{0,8},{8,16},{16,24},{24,28},{28,20},{20,12},{12,4},{4,0},{1,9},{9... | collective-permute-start | bytes 6193160 | tf_op jit(solution)/shard_map/ppermute | solution.py:27
  253.7 47.2 %collective-permute-start.23 = (f32[224,2304]{1,0:T(8,128)S(1)}, f32[224,2304]{1,0:T(8,128)}, u32[]{:S(2)}, u32[]{:S(2)}) collective-permute-start(f32[224,2304]{1,0:T(8,128)S(1)} %collective-permute-done.18), channel_id=1, source_target_pairs={{0,4},{8,0},{16,8},{24,16},{28,24},{20,28},{12,20},{4,12},{1,5},{9... | collective-permute-start | bytes 6193160 | tf_op jit(solution)/shard_map/ppermute | solution.py:27
  261.9 12.4 %collective-permute-start.25 = (f32[224,448]{1,0:T(8,128)S(1)}, f32[224,448]{1,0:T(8,128)S(1)}, u32[]{:S(2)}, u32[]{:S(2)}) collective-permute-start(f32[224,448]{1,0:T(8,128)S(1)} %select_add_fusion.3), channel_id=1, source_target_pairs={{0,2},{1,3},{2,0},{3,1},{4,6},{5,7},{6,4},{7,5},{8,10},{9,11},{10,... | collective-permute-start | bytes 1204232 | tf_op jit(solution)/shard_map/ppermute | solution.py:32
  304.4 48.4 %collective-permute-start.31 = (f32[224,2304]{1,0:T(8,128)}, f32[224,2304]{1,0:T(8,128)S(1)}, u32[]{:S(2)}, u32[]{:S(2)}) collective-permute-start(f32[224,2304]{1,0:T(8,128)} %collective-permute-done.23), channel_id=1, source_target_pairs={{0,4},{8,0},{16,8},{24,16},{28,24},{20,28},{12,20},{4,12},{1,5},{9... | collective-permute-start | bytes 6193160 | tf_op jit(solution)/shard_map/ppermute | solution.py:27
  306.0 46.8 %collective-permute-start.30 = (f32[224,2304]{1,0:T(8,128)}, f32[224,2304]{1,0:T(8,128)}, u32[]{:S(2)}, u32[]{:S(2)}) collective-permute-start(f32[224,2304]{1,0:T(8,128)} %collective-permute-done.22), channel_id=1, source_target_pairs={{0,8},{8,16},{16,24},{24,28},{28,20},{20,12},{12,4},{4,0},{1,9},{9... | collective-permute-start | bytes 6193160 | tf_op jit(solution)/shard_map/ppermute | solution.py:27
  311.3 6.4 %collective-permute-start.32 = (f32[224,448]{1,0:T(8,128)}, f32[224,448]{1,0:T(8,128)}, u32[]{:S(2)}, u32[]{:S(2)}) collective-permute-start(f32[224,448]{1,0:T(8,128)} %get-tuple-element.167), channel_id=1, source_target_pairs={{0,1},{1,0},{2,3},{3,2},{4,5},{5,4},{6,7},{7,6},{8,9},{9,8},{10,11... | collective-permute-start | bytes 1204232 | tf_op jit(solution)/shard_map/ppermute | solution.py:32
  317.7 17.6 %collective-permute-start.27 = (f32[224,448]{1,0:T(8,128)S(1)}, f32[224,448]{1,0:T(8,128)S(1)}, u32[]{:S(2)}, u32[]{:S(2)}) collective-permute-start(f32[224,448]{1,0:T(8,128)S(1)} %broadcast_select_fusion.12), channel_id=1, source_target_pairs={{0,1},{1,0},{2,3},{3,2},{4,5},{5,4},{6,7},{7,6},{8,9},{9,8},{10,11... | collective-permute-start | bytes 1204232 | tf_op jit(solution)/shard_map/ppermute | solution.py:32
  318.9 13.0 %collective-permute-start.33 = (f32[224,448]{1,0:T(8,128)S(1)}, f32[224,448]{1,0:T(8,128)S(1)}, u32[]{:S(2)}, u32[]{:S(2)}) collective-permute-start(f32[224,448]{1,0:T(8,128)S(1)} %select_add_fusion.1), channel_id=1, source_target_pairs={{0,2},{1,3},{2,0},{3,1},{4,6},{5,7},{6,4},{7,5},{8,10},{9,11},{10,... | collective-permute-start | bytes 1204232 | tf_op jit(solution)/shard_map/ppermute | solution.py:32
  332.0 5.0 collective-permute-start.34
  335.4 24.7 %collective-permute-start.28 = (f32[224,448]{1,0:T(8,128)S(1)}, f32[224,448]{1,0:T(8,128)S(1)}, u32[]{:S(2)}, u32[]{:S(2)}) collective-permute-start(f32[224,448]{1,0:T(8,128)S(1)} %select_add_fusion.2), channel_id=1, source_target_pairs={{0,2},{1,3},{2,0},{3,1},{4,6},{5,7},{6,4},{7,5},{8,10},{9,11},{10,... | collective-permute-start | bytes 1204232 | tf_op jit(solution)/shard_map/ppermute | solution.py:32
  360.1 13.5 %collective-permute-start.29 = (f32[224,448]{1,0:T(8,128)S(1)}, f32[224,448]{1,0:T(8,128)S(1)}, u32[]{:S(2)}, u32[]{:S(2)}) collective-permute-start(f32[224,448]{1,0:T(8,128)S(1)} %add.332), channel_id=1, source_target_pairs={{0,1},{1,0},{2,3},{3,2},{4,5},{5,4},{6,7},{7,6},{8,9},{9,8},{10,11... | collective-permute-start | bytes 1204232 | tf_op jit(solution)/shard_map/ppermute | solution.py:32
  360.9 12.6 %collective-permute-start.36 = (f32[224,448]{1,0:T(8,128)S(1)}, f32[224,448]{1,0:T(8,128)S(1)}, u32[]{:S(2)}, u32[]{:S(2)}) collective-permute-start(f32[224,448]{1,0:T(8,128)S(1)} %select_add_fusion), channel_id=1, source_target_pairs={{0,2},{1,3},{2,0},{3,1},{4,6},{5,7},{6,4},{7,5},{8,10},{9,11},{10,... | collective-permute-start | bytes 1204232 | tf_op jit(solution)/shard_map/ppermute | solution.py:32
  380.6 20.2 %collective-permute-start.38 = (f32[224,896]{1,0:T(8,128)}, f32[224,896]{1,0:T(8,128)}, u32[]{:S(2)}, u32[]{:S(2)}) collective-permute-start(f32[224,896]{1,0:T(8,128)} %copy.19), channel_id=1, source_target_pairs={{0,8},{8,16},{16,24},{24,28},{28,20},{20,12},{12,4},{4,0},{1,9},{9... | collective-permute-start | bytes 2408456 | tf_op jit(solution)/shard_map/ppermute | solution.py:27
  383.4 19.9 %collective-permute-start.39 = (f32[224,896]{1,0:T(8,128)}, f32[224,896]{1,0:T(8,128)S(1)}, u32[]{:S(2)}, u32[]{:S(2)}) collective-permute-start(f32[224,896]{1,0:T(8,128)} %copy.20), channel_id=1, source_target_pairs={{0,4},{8,0},{16,8},{24,16},{28,24},{20,28},{12,20},{4,12},{1,5},{9... | collective-permute-start | bytes 2408456 | tf_op jit(solution)/shard_map/ppermute | solution.py:27
  403.3 19.0 %collective-permute-start.40 = (f32[224,896]{1,0:T(8,128)}, f32[224,896]{1,0:T(8,128)S(1)}, u32[]{:S(2)}, u32[]{:S(2)}) collective-permute-start(f32[224,896]{1,0:T(8,128)} %collective-permute-done.38), channel_id=1, source_target_pairs={{0,8},{8,16},{16,24},{24,28},{28,20},{20,12},{12,4},{4,0},{1,9},{9... | collective-permute-start | bytes 2408456 | tf_op jit(solution)/shard_map/ppermute | solution.py:27
  403.8 18.7 %collective-permute-start.41 = (f32[224,896]{1,0:T(8,128)S(1)}, f32[224,896]{1,0:T(8,128)S(1)}, u32[]{:S(2)}, u32[]{:S(2)}) collective-permute-start(f32[224,896]{1,0:T(8,128)S(1)} %collective-permute-done.39), channel_id=1, source_target_pairs={{0,4},{8,0},{16,8},{24,16},{28,24},{20,28},{12,20},{4,12},{1,5},{9... | collective-permute-start | bytes 2408456 | tf_op jit(solution)/shard_map/ppermute | solution.py:27
  422.4 18.1 %collective-permute-start.42 = (f32[224,896]{1,0:T(8,128)S(1)}, f32[224,896]{1,0:T(8,128)S(1)}, u32[]{:S(2)}, u32[]{:S(2)}) collective-permute-start(f32[224,896]{1,0:T(8,128)S(1)} %collective-permute-done.40), channel_id=1, source_target_pairs={{0,8},{8,16},{16,24},{24,28},{28,20},{20,12},{12,4},{4,0},{1,9},{9... | collective-permute-start | bytes 2408456 | tf_op jit(solution)/shard_map/ppermute | solution.py:27
  422.9 17.6 %collective-permute-start.43 = (f32[224,896]{1,0:T(8,128)S(1)}, f32[224,896]{1,0:T(8,128)S(1)}, u32[]{:S(2)}, u32[]{:S(2)}) collective-permute-start(f32[224,896]{1,0:T(8,128)S(1)} %collective-permute-done.41), channel_id=1, source_target_pairs={{0,4},{8,0},{16,8},{24,16},{28,24},{20,28},{12,20},{4,12},{1,5},{9... | collective-permute-start | bytes 2408456 | tf_op jit(solution)/shard_map/ppermute | solution.py:27
  440.5 18.1 %collective-permute-start.44 = (f32[224,896]{1,0:T(8,128)S(1)}, f32[224,896]{1,0:T(8,128)S(1)}, u32[]{:S(2)}, u32[]{:S(2)}) collective-permute-start(f32[224,896]{1,0:T(8,128)S(1)} %collective-permute-done.42), channel_id=1, source_target_pairs={{0,8},{8,16},{16,24},{24,28},{28,20},{20,12},{12,4},{4,0},{1,9},{9... | collective-permute-start | bytes 2408456 | tf_op jit(solution)/shard_map/ppermute | solution.py:27
  441.7 16.9 %collective-permute-start.45 = (f32[224,896]{1,0:T(8,128)S(1)}, f32[224,896]{1,0:T(8,128)S(1)}, u32[]{:S(2)}, u32[]{:S(2)}) collective-permute-start(f32[224,896]{1,0:T(8,128)S(1)} %collective-permute-done.43), channel_id=1, source_target_pairs={{0,4},{8,0},{16,8},{24,16},{28,24},{20,28},{12,20},{4,12},{1,5},{9... | collective-permute-start | bytes 2408456 | tf_op jit(solution)/shard_map/ppermute | solution.py:27
  458.5 18.1 %collective-permute-start.46 = (f32[224,896]{1,0:T(8,128)S(1)}, f32[224,896]{1,0:T(8,128)S(1)}, u32[]{:S(2)}, u32[]{:S(2)}) collective-permute-start(f32[224,896]{1,0:T(8,128)S(1)} %collective-permute-done.44), channel_id=1, source_target_pairs={{0,8},{8,16},{16,24},{24,28},{28,20},{20,12},{12,4},{4,0},{1,9},{9... | collective-permute-start | bytes 2408456 | tf_op jit(solution)/shard_map/ppermute | solution.py:27
  460.0 16.9 %collective-permute-start.47 = (f32[224,896]{1,0:T(8,128)S(1)}, f32[224,896]{1,0:T(8,128)S(1)}, u32[]{:S(2)}, u32[]{:S(2)}) collective-permute-start(f32[224,896]{1,0:T(8,128)S(1)} %collective-permute-done.45), channel_id=1, source_target_pairs={{0,4},{8,0},{16,8},{24,16},{28,24},{20,28},{12,20},{4,12},{1,5},{9... | collective-permute-start | bytes 2408456 | tf_op jit(solution)/shard_map/ppermute | solution.py:27
  476.9 18.0 %collective-permute-start.48 = (f32[224,896]{1,0:T(8,128)S(1)}, f32[224,896]{1,0:T(8,128)S(1)}, u32[]{:S(2)}, u32[]{:S(2)}) collective-permute-start(f32[224,896]{1,0:T(8,128)S(1)} %collective-permute-done.46), channel_id=1, source_target_pairs={{0,8},{8,16},{16,24},{24,28},{28,20},{20,12},{12,4},{4,0},{1,9},{9... | collective-permute-start | bytes 2408456 | tf_op jit(solution)/shard_map/ppermute | solution.py:27
  478.3 17.0 %collective-permute-start.49 = (f32[224,896]{1,0:T(8,128)S(1)}, f32[224,896]{1,0:T(8,128)S(1)}, u32[]{:S(2)}, u32[]{:S(2)}) collective-permute-start(f32[224,896]{1,0:T(8,128)S(1)} %collective-permute-done.47), channel_id=1, source_target_pairs={{0,4},{8,0},{16,8},{24,16},{28,24},{20,28},{12,20},{4,12},{1,5},{9... | collective-permute-start | bytes 2408456 | tf_op jit(solution)/shard_map/ppermute | solution.py:27
  495.3 13.6 %collective-permute-start.50 = (f32[224,896]{1,0:T(8,128)S(1)}, f32[224,896]{1,0:T(8,128)S(1)}, u32[]{:S(2)}, u32[]{:S(2)}) collective-permute-start(f32[224,896]{1,0:T(8,128)S(1)} %collective-permute-done.48), channel_id=1, source_target_pairs={{0,8},{8,16},{16,24},{24,28},{28,20},{20,12},{12,4},{4,0},{1,9},{9... | collective-permute-start | bytes 2408456 | tf_op jit(solution)/shard_map/ppermute | solution.py:27
  496.7 12.6 %collective-permute-start.51 = (f32[224,896]{1,0:T(8,128)S(1)}, f32[224,896]{1,0:T(8,128)S(1)}, u32[]{:S(2)}, u32[]{:S(2)}) collective-permute-start(f32[224,896]{1,0:T(8,128)S(1)} %collective-permute-done.49), channel_id=1, source_target_pairs={{0,4},{8,0},{16,8},{24,16},{28,24},{20,28},{12,20},{4,12},{1,5},{9... | collective-permute-start | bytes 2408456 | tf_op jit(solution)/shard_map/ppermute | solution.py:27
  513.9 7.6 %collective-permute-start.53 = (f32[448,896]{1,0:T(8,128)S(1)}, f32[448,896]{1,0:T(8,128)}, u32[]{:S(2)}, u32[]{:S(2)}) collective-permute-start(f32[448,896]{1,0:T(8,128)S(1)} %copy.37), channel_id=1, source_target_pairs={{0,1},{1,0},{2,3},{3,2},{4,5},{5,4},{6,7},{7,6},{8,9},{9,8},{10,11... | collective-permute-start | bytes 4816904 | tf_op jit(solution)/shard_map/ppermute | solution.py:32
  515.3 37.7 %collective-permute-start.52 = (f32[448,896]{1,0:T(8,128)S(1)}, f32[448,896]{1,0:T(8,128)}, u32[]{:S(2)}, u32[]{:S(2)}) collective-permute-start(f32[448,896]{1,0:T(8,128)S(1)} %copy.37), channel_id=1, source_target_pairs={{0,2},{1,3},{2,0},{3,1},{4,6},{5,7},{6,4},{7,5},{8,10},{9,11},{10,... | collective-permute-start | bytes 4816904 | tf_op jit(solution)/shard_map/ppermute | solution.py:32
  553.0 3.7 collective-permute-start.54
  (60 other events, 635.6 us)

commit v5 on v4

--- a/solution.py
+++ b/solution.py
@@ -17,6 +17,18 @@
     )
 
 
+def split(value):
+    high = lax.reduce_precision(value, exponent_bits=8, mantissa_bits=7)
+    return high.astype(jnp.bfloat16), (value - high).astype(jnp.bfloat16)
+
+
+def keep(slab, value, at, span):
+    high, low = split(value)
+    to = at // span * (2 * span) + at % span
+    slab = lax.dynamic_update_slice(slab, high, (to, 0))
+    return lax.dynamic_update_slice(slab, low, (to + span, 0))
+
+
 def ring_order(count):
     return list(range(0, count, 2)) + list(range(1, count, 2))[::-1]
 
@@ -32,8 +44,11 @@
     return lax.ppermute(value, "col", [(k, k ^ bit) for k in range(count)])
 
 
-def sum_over_col(low, high, upper):
-    mine = jnp.where(upper, high, low) + swap(jnp.where(upper, low, high), 1)
+def core_sum(low, high, upper):
+    return jnp.where(upper, high, low) + swap(jnp.where(upper, low, high), 1)
+
+
+def chip_sum(mine, upper):
     bit = 2
     while bit < lax.axis_size("col"):
         mine = mine + swap(mine, bit)
@@ -56,7 +71,8 @@
     upper = (my_col & 1) != 0
 
     up, down = iterate[:near], iterate[near:]
-    near_blocks, far_blocks = [], []
+    blocks = []
+    half_summed = raw = None
     slab = None
     for step in range(row_count):
         last = step == row_count - 1
@@ -65,36 +81,33 @@
         near_at = (mine - step) % row_count * rows
         far_at = (mine + step) % row_count * rows + near
         if step == 1:
-            slab = jnp.broadcast_to(up[:1], (total, cols))
-            own_at = mine * rows
-            slab = lax.dynamic_update_slice(slab, iterate, (own_at, 0))
+            slab = jnp.broadcast_to(up[:1].astype(jnp.bfloat16), (2 * total, cols))
+            slab = keep(slab, iterate, mine * rows, 2 * width)
         if step >= 1:
-            slab = lax.dynamic_update_slice(slab, up, (near_at, 0))
-            slab = lax.dynamic_update_slice(slab, down, (far_at, 0))
+            slab = keep(slab, up, near_at, 2 * width)
+            slab = keep(slab, down, far_at, 2 * width)
         near_part = product(up, iterate, ((1,), (1,)))
         far_part = product(down, iterate, ((1,), (1,)))
-        waiting = [near_part, far_part]
-        if step >= row_count - 2:
-            waiting = list(sum_over_col(near_part, far_part, upper))
+        finished = []
+        if step < row_count - 2:
+            if half_summed is not None:
+                finished.append(chip_sum(half_summed, upper))
+            half_summed = None if raw is None else core_sum(*raw, upper)
+            raw = (near_part, far_part)
+        else:
+            if half_summed is not None:
+                finished.append(chip_sum(half_summed, upper))
+            if raw is not None:
+                finished.append(chip_sum(core_sum(*raw, upper), upper))
+            half_summed, raw = core_sum(near_part, far_part, upper), None
+            if last:
+                finished.append(chip_sum(half_summed, upper))
         if not last:
-            held = [next_up, next_down] + waiting
-            if step >= 1:
-                held += [slab]
-                if step < row_count - 2:
-                    held += [near_blocks.pop(), far_blocks.pop()]
-            held = list(lax.optimization_barrier(tuple(held)))
-            up, down, near_part, far_part = held[:4]
-            waiting = held[2:4]
-            if step >= 1:
-                slab = held[4]
-                if step < row_count - 2:
-                    near_blocks.append(held[5])
-                    far_blocks.append(held[6])
-            if step < row_count - 2:
-                waiting = sum_over_col(near_part, far_part, upper)
-        near_blocks.append(waiting[0])
-        far_blocks.append(waiting[1])
+            held = ((next_up, next_down), finished, half_summed, raw, slab)
+            (up, down), finished, half_summed, raw, slab = lax.optimization_barrier(held)
+        blocks += finished
 
+    near_blocks, far_blocks = zip(*blocks)
     near_all = jnp.concatenate(near_blocks, axis=0)
     far_all = jnp.concatenate(far_blocks, axis=0)
     parts = []
@@ -114,7 +127,9 @@
         term = term + product(far_blocks[step], down, ((0,), (0,)))
         square_tile = term if square_tile is None else square_tile + term
         if not last:
-            up, down, square_tile = lax.optimization_barrier((next_up, next_down, square_tile))
+            up, down, square_tile, slab = lax.optimization_barrier(
+                (next_up, next_down, square_tile, slab)
+            )
     poly_tile = COEF_B * gram_tile + COEF_C * square_tile
 
     tiles = {0: poly_tile}
@@ -135,8 +150,13 @@
             ],
             axis=1,
         )
-        at = ((my_col ^ k) >> 1) * (2 * width)
-        term = product(pair, lax.dynamic_slice_in_dim(slab, at, 2 * width, 0), ((1,), (0,)))
+        high, low = split(pair)
+        at = ((my_col ^ k) >> 1) * (4 * width)
+        kept = lax.dynamic_slice_in_dim(slab, at, 4 * width, 0)
+        term = jnp.dot(
+            jnp.concatenate([high, high], axis=1), kept, preferred_element_type=jnp.float32
+        )
+        term = term + jnp.dot(low, kept[: 2 * width], preferred_element_type=jnp.float32)
         applied = term if applied is None else applied + term
     return (COEF_A * iterate + applied) * scale
 

time: 591 us -> 653 us (1.10)
  local copies, waits for them, and re-layouts: 46 us -> 228 us
  waiting for transfers between devices: 337 us -> 158 us
  other arithmetic: 30.5 us -> 78.6 us
  matrix products: 109 us -> 121 us
    dynamic_update_slice x15 -> x30, local copies, waits for them, and re-layouts: 20.9 us -> 191 us  [the longest x15 95.5 us: keep(): slab = lax.dynamic_update_slice(slab, high, (to, 0))]
    ppermute x28, waiting for transfers between devices: 251 us -> 118 us  [shift(): return lax.ppermute(value, 'row', pairs)]
    ppermute x27, waiting for transfers between devices: 85.3 us -> 40.5 us  [swap(): return lax.ppermute(value, 'col', [(k, k ^ bit) for k in range(count)])]
    dot_general x0 -> x4, matrix products: none -> 42.6 us  [the longest x2 26.3 us: body(): jnp.dot(jnp.concatenate([high, high], axis=1), kept, preferred_element_ty...]
    convert_element_type x0 -> x16, other arithmetic: none -> 40.5 us  [split(): return (high.astype(jnp.bfloat16), (value - high).astype(jnp.bfloat16))]
    dot_general x34 -> x32, matrix products: 109 us -> 77.9 us  [product(): lax.dot_general(left, right, (dims, ((), ())), precision=PREC, preferred_...]
    broadcast_in_dim x1, local copies, waits for them, and re-layouts: 2.28 us -> 10.9 us  [body(): slab = jnp.broadcast_to(up[:1].astype(jnp.bfloat16), (2 * total, cols))]
  transfers between devices with their start and end apart: 55 -> 55, of which waited for: 39 -> 30; matrix products, arithmetic and copies ran while one was open for 24% -> 56% of each run, Pallas kernels for 0% -> 0%
where the time goes in v5:
time: 653 us; the launch traced here: 643 us
  local copies, waits for them, and re-layouts  228 us (35%)
  waiting for transfers between devices  158 us (24%)
  matrix products  121 us (19%)
  other arithmetic  78.6 us (12%)
  starting transfers between devices  43.1 us (7%)
  between operations  14.1 us (2%)
    ppermute x28, waiting for transfers between devices, shift(): return lax.ppermute(value, 'row', pairs)  118 us
    dynamic_update_slice x15, local copies, waits for them, and re-layouts, keep(): slab = lax.dynamic_update_slice(slab, high, (to, 0))  95.5 us
    dynamic_update_slice x15, local copies, waits for them, and re-layouts, keep(): return lax.dynamic_update_slice(slab, low, (to + span, 0))  95 us
    dot_general x32, matrix products, product(): lax.dot_general(left, right, (dims, ((), ())), precision=PREC, preferred_...  77.9 us
    convert_element_type x16, other arithmetic, split(): return (high.astype(jnp.bfloat16), (value - high).astype(jnp.bfloat16))  40.5 us
    ppermute x27, waiting for transfers between devices, swap(): return lax.ppermute(value, 'col', [(k, k ^ bit) for k in range(count)])  40.5 us
    ppermute x28, starting transfers between devices, shift(): return lax.ppermute(value, 'row', pairs)  30.8 us
    dot_general x2, matrix products, body(): jnp.dot(jnp.concatenate([high, high], axis=1), kept, preferred_element_ty...  26.3 us
  transfers between devices with their start and end apart: 55, of which 30 were waited for; matrix products, arithmetic and copies ran while one was open for 56% of the time, Pallas kernels for 0%

profile of v5, /device:TPU:0, one launch (start us, length us, event | category | flops | bytes accessed | tf_op | source)
XLA Modules:
  0.0 642.8 jit_solution(15328273414400116653)
XLA Ops:
  20.8 4.8 fusion.59
  30.3 22.2 %collective-permute-done = f32[224,2304]{1,0:T(8,128)S(1)} collective-permute-done((f32[224,2304]{1,0:T(8,128)}, f32[224,2304]{1,0:T(8,128)S(1)}, u32[]{:S(2)}, u32[]{:S(2)}) %collective-permute-start) | collective-permute-done | bytes 2064416 | tf_op jit(solution)/shard_map/ppermute | solution.py:39
  63.4 10.9 %broadcast_in_dim.8 = bf16[7168,2304]{1,0:T(8,128)(2,1)} broadcast(bf16[2304]{0:T(1024)(128)(2,1)S(1)} %fusion.47), dimensions={1} | broadcast | bytes 33034752 | tf_op jit(solution)/shard_map/broadcast_in_dim | solution.py:84
  74.3 10.5 %dynamic_update_slice.90 = bf16[7168,2304]{1,0:T(8,128)(2,1)} dynamic-update-slice(bf16[7168,2304]{1,0:T(8,128)(2,1)} %broadcast_in_dim.8, bf16[448,2304]{1,0:T(8,128)(2,1)} %get-tuple-element.166, s32[]{:T(128)S(6)} %select_n.450, s32[]{:T(128)} %constant.209.clone.1) | dynamic-update-slice | bytes 4128772 | tf_op jit(solution)/shard_map/dynamic_update_slice | solution.py:28
  84.8 10.5 %dynamic_update_slice.91 = bf16[7168,2304]{1,0:T(8,128)(2,1)} dynamic-update-slice(bf16[7168,2304]{1,0:T(8,128)(2,1)} %dynamic_update_slice.90, bf16[448,2304]{1,0:T(8,128)(2,1)} %get-tuple-element.165, s32[]{:T(128)S(6)} %select_n.451, s32[]{:T(128)} %constant.209.clone.1) | dynamic-update-slice | bytes 4128772 | tf_op jit(solution)/shard_map/dynamic_update_slice | solution.py:29
  95.3 6.1 dynamic_update_slice.92
  101.3 6.1 dynamic_update_slice.93
  107.4 6.1 dynamic_update_slice.94
  113.5 6.0 dynamic_update_slice.95
  147.6 6.1 dynamic_update_slice.96
  153.7 6.1 dynamic_update_slice.97
  159.8 6.1 dynamic_update_slice.98
  165.8 6.1 dynamic_update_slice.99
  198.0 6.1 dynamic_update_slice.100
  204.1 6.1 dynamic_update_slice.101
  210.2 6.1 dynamic_update_slice.102
  216.2 6.1 dynamic_update_slice.103
  226.3 5.1 collective-permute-done.11
  249.5 6.1 dynamic_update_slice.104
  255.6 6.1 dynamic_update_slice.105
  261.6 6.1 dynamic_update_slice.106
  267.7 6.1 dynamic_update_slice.107
  302.3 6.1 dynamic_update_slice.108
  308.4 6.1 dynamic_update_slice.109
  314.4 6.1 dynamic_update_slice.110
  320.5 6.1 dynamic_update_slice.111
  347.6 5.5 collective-permute-done.27
  355.5 6.1 dynamic_update_slice.112
  361.5 6.1 dynamic_update_slice.113
  367.6 6.1 dynamic_update_slice.114
  373.7 6.1 dynamic_update_slice.115
  397.3 7.0 %collective-permute-done.33 = f32[224,448]{1,0:T(8,128)S(1)} collective-permute-done((f32[224,448]{1,0:T(8,128)S(1)}, f32[224,448]{1,0:T(8,128)S(1)}, u32[]{:S(2)}, u32[]{:S(2)}) %collective-permute-start.33) | collective-permute-done | bytes 401440 | tf_op jit(solution)/shard_map/ppermute | solution.py:44
  404.6 9.2 %collective-permute-done.36 = f32[224,448]{1,0:T(8,128)S(1)} collective-permute-done((f32[224,448]{1,0:T(8,128)S(1)}, f32[224,448]{1,0:T(8,128)S(1)}, u32[]{:S(2)}, u32[]{:S(2)}) %collective-permute-start.36) | collective-permute-done | bytes 401440 | tf_op jit(solution)/shard_map/ppermute | solution.py:44
  428.5 6.1 dynamic_update_slice.116
  434.6 6.1 dynamic_update_slice.117
  440.7 6.1 dynamic_update_slice.118
  446.7 5.6 dynamic_update_slice.119
  462.4 12.5 %collective-permute-done.40 = f32[224,896]{1,0:T(8,128)S(1)} collective-permute-done((f32[224,896]{1,0:T(8,128)}, f32[224,896]{1,0:T(8,128)S(1)}, u32[]{:S(2)}, u32[]{:S(2)}) %collective-permute-start.40) | collective-permute-done | bytes 802848 | tf_op jit(solution)/shard_map/ppermute | solution.py:39
  481.6 13.6 %collective-permute-done.42 = f32[224,896]{1,0:T(8,128)S(1)} collective-permute-done((f32[224,896]{1,0:T(8,128)S(1)}, f32[224,896]{1,0:T(8,128)S(1)}, u32[]{:S(2)}, u32[]{:S(2)}) %collective-permute-start.42) | collective-permute-done | bytes 802848 | tf_op jit(solution)/shard_map/ppermute | solution.py:39
  501.2 13.2 %collective-permute-done.44 = f32[224,896]{1,0:T(8,128)S(1)} collective-permute-done((f32[224,896]{1,0:T(8,128)S(1)}, f32[224,896]{1,0:T(8,128)S(1)}, u32[]{:S(2)}, u32[]{:S(2)}) %collective-permute-start.44) | collective-permute-done | bytes 802848 | tf_op jit(solution)/shard_map/ppermute | solution.py:39
  519.6 13.1 %collective-permute-done.46 = f32[224,896]{1,0:T(8,128)S(1)} collective-permute-done((f32[224,896]{1,0:T(8,128)S(1)}, f32[224,896]{1,0:T(8,128)S(1)}, u32[]{:S(2)}, u32[]{:S(2)}) %collective-permute-start.46) | collective-permute-done | bytes 802848 | tf_op jit(solution)/shard_map/ppermute | solution.py:39
  537.7 12.8 %collective-permute-done.48 = f32[224,896]{1,0:T(8,128)S(1)} collective-permute-done((f32[224,896]{1,0:T(8,128)S(1)}, f32[224,896]{1,0:T(8,128)S(1)}, u32[]{:S(2)}, u32[]{:S(2)}) %collective-permute-start.48) | collective-permute-done | bytes 802848 | tf_op jit(solution)/shard_map/ppermute | solution.py:39
  555.6 9.4 %collective-permute-done.50 = f32[224,896]{1,0:T(8,128)S(1)} collective-permute-done((f32[224,896]{1,0:T(8,128)S(1)}, f32[224,896]{1,0:T(8,128)S(1)}, u32[]{:S(2)}, u32[]{:S(2)}) %collective-permute-start.50) | collective-permute-done | bytes 802848 | tf_op jit(solution)/shard_map/ppermute | solution.py:39
  579.5 7.0 %fusion.6 = f32[448,2304]{1,0:T(8,128)S(1)} fusion(bf16[7168,2304]{1,0:T(8,128)(2,1)} %dynamic_update_slice.119, s32[]{:T(128)S(6)} %select_n.563, f32[448,896]{0,1:T(8,128)S(1)} %get-tuple-element.172, f32[448,896]{0,1:T(8,128)S(1)} %get-tuple-element.171), kind=kOutput, calls=%fused_computation.6 | convolution fusion | flops 3702587392 | bytes 15597572 | tf_op jit(solution)/shard_map/dot_general | solution.py:159
  586.5 13.4 %fusion.8 = f32[448,2304]{1,0:T(8,128)} fusion(f32[448,2304]{1,0:T(8,128)S(1)} %fusion.6, bf16[7168,2304]{1,0:T(8,128)(2,1)} %dynamic_update_slice.119, s32[]{:T(128)S(6)} %select_n.563, bf16[448,1792]{0,1:T(8,128)(2,1)S(1)} %reduce-precision_convert_fusion.2), kind=kOutput, calls=%fused_computation.14 | convolution fusion | flops 7406206976 | bytes 26378244 | tf_op jit(solution)/shard_map/dot_general | solution.py:156
  599.9 8.7 %collective-permute-done.52 = f32[448,896]{1,0:T(8,128)} collective-permute-done((f32[448,896]{1,0:T(8,128)}, f32[448,896]{1,0:T(8,128)}, u32[]{:S(2)}, u32[]{:S(2)}) %collective-permute-start.52) | collective-permute-done | bytes 1605664 | tf_op jit(solution)/shard_map/ppermute | solution.py:44
  617.6 9.3 %fusion.4 = f32[448,2304]{1,0:T(8,128)} fusion(bf16[7168,2304]{1,0:T(8,128)(2,1)} %dynamic_update_slice.119, s32[]{:T(128)S(6)} %select_n.566, f32[448,896]{0,1:T(8,128)S(1)} %get-tuple-element.170, f32[448,896]{0,1:T(8,128)S(1)} %get-tuple-element.169), kind=kOutput, calls=%fused_computation.4 | convolution fusion | flops 3702587392 | bytes 15597572 | tf_op jit(solution)/shard_map/dot_general | solution.py:159
  626.9 12.9 %fusion.11 = f32[448,2304]{1,0:T(8,128)S(1)} fusion(f32[448,2304]{1,0:T(8,128)} %fusion.4, bf16[7168,2304]{1,0:T(8,128)(2,1)} %dynamic_update_slice.119, s32[]{:T(128)S(6)} %select_n.566, bf16[448,1792]{0,1:T(8,128)(2,1)S(1)} %reduce-precision_convert_fusion.1), kind=kOutput, calls=%fused_computation.15 | convolution fusion | flops 7406206976 | bytes 26378244 | tf_op jit(solution)/shard_map/dot_general | solution.py:156
  (322 shorter events, 247.4 us)
Async XLA Ops:
  4.5 48.1 %collective-permute-start = (f32[224,2304]{1,0:T(8,128)}, f32[224,2304]{1,0:T(8,128)S(1)}, u32[]{:S(2)}, u32[]{:S(2)}) collective-permute-start(f32[224,2304]{1,0:T(8,128)} %get-tuple-element.168), channel_id=1, source_target_pairs={{0,8},{8,16},{16,24},{24,28},{28,20},{20,12},{12,4},{4,0},{1,9},{9... | collective-permute-start | bytes 6193160 | tf_op jit(solution)/shard_map/ppermute | solution.py:39
  7.5 46.7 %collective-permute-start.1 = (f32[224,2304]{1,0:T(8,128)}, f32[224,2304]{1,0:T(8,128)}, u32[]{:S(2)}, u32[]{:S(2)}) collective-permute-start(f32[224,2304]{1,0:T(8,128)} %get-tuple-element.167), channel_id=1, source_target_pairs={{0,4},{8,0},{16,8},{24,16},{28,24},{20,28},{12,20},{4,12},{1,5},{9... | collective-permute-start | bytes 6193160 | tf_op jit(solution)/shard_map/ppermute | solution.py:39
  55.1 69.2 %collective-permute-start.4 = (f32[224,448]{1,0:T(8,128)}, f32[224,448]{1,0:T(8,128)}, u32[]{:S(2)}, u32[]{:S(2)}) collective-permute-start(f32[224,448]{1,0:T(8,128)} %broadcast_select_fusion.27), channel_id=1, source_target_pairs={{0,1},{1,0},{2,3},{3,2},{4,5},{5,4},{6,7},{7,6},{8,9},{9,8},{10,11... | collective-permute-start | bytes 1204232 | tf_op jit(solution)/shard_map/ppermute | solution.py:44
  55.1 70.4 %collective-permute-start.2 = (f32[224,2304]{1,0:T(8,128)S(1)}, f32[224,2304]{1,0:T(8,128)}, u32[]{:S(2)}, u32[]{:S(2)}) collective-permute-start(f32[224,2304]{1,0:T(8,128)S(1)} %collective-permute-done), channel_id=1, source_target_pairs={{0,8},{8,16},{16,24},{24,28},{28,20},{20,12},{12,4},{4,0},{1,9},{9... | collective-permute-start | bytes 6193160 | tf_op jit(solution)/shard_map/ppermute | solution.py:39
  56.7 68.8 %collective-permute-start.3 = (f32[224,2304]{1,0:T(8,128)}, f32[224,2304]{1,0:T(8,128)}, u32[]{:S(2)}, u32[]{:S(2)}) collective-permute-start(f32[224,2304]{1,0:T(8,128)} %collective-permute-done.1), channel_id=1, source_target_pairs={{0,4},{8,0},{16,8},{24,16},{28,24},{20,28},{12,20},{4,12},{1,5},{9... | collective-permute-start | bytes 6193160 | tf_op jit(solution)/shard_map/ppermute | solution.py:39
  128.6 47.0 %collective-permute-start.5 = (f32[224,2304]{1,0:T(8,128)}, f32[224,2304]{1,0:T(8,128)S(1)}, u32[]{:S(2)}, u32[]{:S(2)}) collective-permute-start(f32[224,2304]{1,0:T(8,128)} %collective-permute-done.2), channel_id=1, source_target_pairs={{0,8},{8,16},{16,24},{24,28},{28,20},{20,12},{12,4},{4,0},{1,9},{9... | collective-permute-start | bytes 6193160 | tf_op jit(solution)/shard_map/ppermute | solution.py:39
  130.2 12.1 %collective-permute-start.7 = (f32[224,448]{1,0:T(8,128)S(1)}, f32[224,448]{1,0:T(8,128)S(1)}, u32[]{:S(2)}, u32[]{:S(2)}) collective-permute-start(f32[224,448]{1,0:T(8,128)S(1)} %select_add_fusion.7), channel_id=1, source_target_pairs={{0,2},{1,3},{2,0},{3,1},{4,6},{5,7},{6,4},{7,5},{8,10},{9,11},{10,... | collective-permute-start | bytes 1204232 | tf_op jit(solution)/shard_map/ppermute | solution.py:44
  131.7 47.0 %collective-permute-start.6 = (f32[224,2304]{1,0:T(8,128)}, f32[224,2304]{1,0:T(8,128)}, u32[]{:S(2)}, u32[]{:S(2)}) collective-permute-start(f32[224,2304]{1,0:T(8,128)} %collective-permute-done.3), channel_id=1, source_target_pairs={{0,4},{8,0},{16,8},{24,16},{28,24},{20,28},{12,20},{4,12},{1,5},{9... | collective-permute-start | bytes 6193160 | tf_op jit(solution)/shard_map/ppermute | solution.py:39
  136.6 35.3 %collective-permute-start.9 = (f32[224,448]{1,0:T(8,128)}, f32[224,448]{1,0:T(8,128)}, u32[]{:S(2)}, u32[]{:S(2)}) collective-permute-start(f32[224,448]{1,0:T(8,128)} %broadcast_select_fusion.24), channel_id=1, source_target_pairs={{0,1},{1,0},{2,3},{3,2},{4,5},{5,4},{6,7},{7,6},{8,9},{9,8},{10,11... | collective-permute-start | bytes 1204232 | tf_op jit(solution)/shard_map/ppermute | solution.py:44
  143.1 30.0 %collective-permute-start.8 = (f32[224,448]{1,0:T(8,128)}, f32[224,448]{1,0:T(8,128)}, u32[]{:S(2)}, u32[]{:S(2)}) collective-permute-start(f32[224,448]{1,0:T(8,128)} %add.527), channel_id=1, source_target_pairs={{0,1},{1,0},{2,3},{3,2},{4,5},{5,4},{6,7},{7,6},{8,9},{9,8},{10,11... | collective-permute-start | bytes 1204232 | tf_op jit(solution)/shard_map/ppermute | solution.py:44
  180.3 46.0 %collective-permute-start.10 = (f32[224,2304]{1,0:T(8,128)}, f32[224,2304]{1,0:T(8,128)S(1)}, u32[]{:S(2)}, u32[]{:S(2)}) collective-permute-start(f32[224,2304]{1,0:T(8,128)} %copy-done.11), channel_id=1, source_target_pairs={{0,8},{8,16},{16,24},{24,28},{28,20},{20,12},{12,4},{4,0},{1,9},{9... | collective-permute-start | bytes 6193160 | tf_op jit(solution)/shard_map/ppermute | solution.py:39
  185.7 10.7 %collective-permute-start.12 = (f32[224,448]{1,0:T(8,128)S(1)}, f32[224,448]{1,0:T(8,128)S(1)}, u32[]{:S(2)}, u32[]{:S(2)}) collective-permute-start(f32[224,448]{1,0:T(8,128)S(1)} %select_add_fusion.6), channel_id=1, source_target_pairs={{0,2},{1,3},{2,0},{3,1},{4,6},{5,7},{6,4},{7,5},{8,10},{9,11},{10,... | collective-permute-start | bytes 1204232 | tf_op jit(solution)/shard_map/ppermute | solution.py:44
  186.2 45.1 %collective-permute-start.11 = (f32[224,2304]{1,0:T(8,128)}, f32[224,2304]{1,0:T(8,128)}, u32[]{:S(2)}, u32[]{:S(2)}) collective-permute-start(f32[224,2304]{1,0:T(8,128)} %collective-permute-done.6), channel_id=1, source_target_pairs={{0,4},{8,0},{16,8},{24,16},{28,24},{20,28},{12,20},{4,12},{1,5},{9... | collective-permute-start | bytes 6193160 | tf_op jit(solution)/shard_map/ppermute | solution.py:39
  190.6 32.5 %collective-permute-start.14 = (f32[224,448]{1,0:T(8,128)}, f32[224,448]{1,0:T(8,128)}, u32[]{:S(2)}, u32[]{:S(2)}) collective-permute-start(f32[224,448]{1,0:T(8,128)} %broadcast_select_fusion.21), channel_id=1, source_target_pairs={{0,1},{1,0},{2,3},{3,2},{4,5},{5,4},{6,7},{7,6},{8,9},{9,8},{10,11... | collective-permute-start | bytes 1204232 | tf_op jit(solution)/shard_map/ppermute | solution.py:44
  197.2 27.1 %collective-permute-start.13 = (f32[224,448]{1,0:T(8,128)}, f32[224,448]{1,0:T(8,128)}, u32[]{:S(2)}, u32[]{:S(2)}) collective-permute-start(f32[224,448]{1,0:T(8,128)} %add.543), channel_id=1, source_target_pairs={{0,1},{1,0},{2,3},{3,2},{4,5},{5,4},{6,7},{7,6},{8,9},{9,8},{10,11... | collective-permute-start | bytes 1204232 | tf_op jit(solution)/shard_map/ppermute | solution.py:44
  232.9 46.0 %collective-permute-start.15 = (f32[224,2304]{1,0:T(8,128)S(1)}, f32[224,2304]{1,0:T(8,128)}, u32[]{:S(2)}, u32[]{:S(2)}) collective-permute-start(f32[224,2304]{1,0:T(8,128)S(1)} %collective-permute-done.10), channel_id=1, source_target_pairs={{0,8},{8,16},{16,24},{24,28},{28,20},{20,12},{12,4},{4,0},{1,9},{9... | collective-permute-start | bytes 6193160 | tf_op jit(solution)/shard_map/ppermute | solution.py:39
  236.8 10.5 %collective-permute-start.17 = (f32[224,448]{1,0:T(8,128)S(1)}, f32[224,448]{1,0:T(8,128)S(1)}, u32[]{:S(2)}, u32[]{:S(2)}) collective-permute-start(f32[224,448]{1,0:T(8,128)S(1)} %select_add_fusion.5), channel_id=1, source_target_pairs={{0,2},{1,3},{2,0},{3,1},{4,6},{5,7},{6,4},{7,5},{8,10},{9,11},{10,... | collective-permute-start | bytes 1204232 | tf_op jit(solution)/shard_map/ppermute | solution.py:44
  238.4 43.8 %collective-permute-start.16 = (f32[224,2304]{1,0:T(8,128)}, f32[224,2304]{1,0:T(8,128)}, u32[]{:S(2)}, u32[]{:S(2)}) collective-permute-start(f32[224,2304]{1,0:T(8,128)} %collective-permute-done.11), channel_id=1, source_target_pairs={{0,4},{8,0},{16,8},{24,16},{28,24},{20,28},{12,20},{4,12},{1,5},{9... | collective-permute-start | bytes 6193160 | tf_op jit(solution)/shard_map/ppermute | solution.py:39
  242.8 32.8 %collective-permute-start.19 = (f32[224,448]{1,0:T(8,128)}, f32[224,448]{1,0:T(8,128)}, u32[]{:S(2)}, u32[]{:S(2)}) collective-permute-start(f32[224,448]{1,0:T(8,128)} %broadcast_select_fusion.18), channel_id=1, source_target_pairs={{0,1},{1,0},{2,3},{3,2},{4,5},{5,4},{6,7},{7,6},{8,9},{9,8},{10,11... | collective-permute-start | bytes 1204232 | tf_op jit(solution)/shard_map/ppermute | solution.py:44
  248.1 28.6 %collective-permute-start.18 = (f32[224,448]{1,0:T(8,128)}, f32[224,448]{1,0:T(8,128)}, u32[]{:S(2)}, u32[]{:S(2)}) collective-permute-start(f32[224,448]{1,0:T(8,128)} %add.559), channel_id=1, source_target_pairs={{0,1},{1,0},{2,3},{3,2},{4,5},{5,4},{6,7},{7,6},{8,9},{9,8},{10,11... | collective-permute-start | bytes 1204232 | tf_op jit(solution)/shard_map/ppermute | solution.py:44
  285.3 44.1 %collective-permute-start.20 = (f32[224,2304]{1,0:T(8,128)}, f32[224,2304]{1,0:T(8,128)}, u32[]{:S(2)}, u32[]{:S(2)}) collective-permute-start(f32[224,2304]{1,0:T(8,128)} %collective-permute-done.15), channel_id=1, source_target_pairs={{0,8},{8,16},{16,24},{24,28},{28,20},{20,12},{12,4},{4,0},{1,9},{9... | collective-permute-start | bytes 6193160 | tf_op jit(solution)/shard_map/ppermute | solution.py:39
  286.8 9.6 %collective-permute-start.22 = (f32[224,448]{1,0:T(8,128)S(1)}, f32[224,448]{1,0:T(8,128)S(1)}, u32[]{:S(2)}, u32[]{:S(2)}) collective-permute-start(f32[224,448]{1,0:T(8,128)S(1)} %select_add_fusion.4), channel_id=1, source_target_pairs={{0,2},{1,3},{2,0},{3,1},{4,6},{5,7},{6,4},{7,5},{8,10},{9,11},{10,... | collective-permute-start | bytes 1204232 | tf_op jit(solution)/shard_map/ppermute | solution.py:44
  287.8 43.1 %collective-permute-start.21 = (f32[224,2304]{1,0:T(8,128)}, f32[224,2304]{1,0:T(8,128)S(1)}, u32[]{:S(2)}, u32[]{:S(2)}) collective-permute-start(f32[224,2304]{1,0:T(8,128)} %collective-permute-done.16), channel_id=1, source_target_pairs={{0,4},{8,0},{16,8},{24,16},{28,24},{20,28},{12,20},{4,12},{1,5},{9... | collective-permute-start | bytes 6193160 | tf_op jit(solution)/shard_map/ppermute | solution.py:39
  291.9 34.7 %collective-permute-start.24 = (f32[224,448]{1,0:T(8,128)}, f32[224,448]{1,0:T(8,128)}, u32[]{:S(2)}, u32[]{:S(2)}) collective-permute-start(f32[224,448]{1,0:T(8,128)} %broadcast_select_fusion.15), channel_id=1, source_target_pairs={{0,1},{1,0},{2,3},{3,2},{4,5},{5,4},{6,7},{7,6},{8,9},{9,8},{10,11... | collective-permute-start | bytes 1204232 | tf_op jit(solution)/shard_map/ppermute | solution.py:44
  297.3 30.5 %collective-permute-start.23 = (f32[224,448]{1,0:T(8,128)}, f32[224,448]{1,0:T(8,128)}, u32[]{:S(2)}, u32[]{:S(2)}) collective-permute-start(f32[224,448]{1,0:T(8,128)} %add.575), channel_id=1, source_target_pairs={{0,1},{1,0},{2,3},{3,2},{4,5},{5,4},{6,7},{7,6},{8,9},{9,8},{10,11... | collective-permute-start | bytes 1204232 | tf_op jit(solution)/shard_map/ppermute | solution.py:44
  334.9 49.6 %collective-permute-start.25 = (f32[224,2304]{1,0:T(8,128)}, f32[224,2304]{1,0:T(8,128)}, u32[]{:S(2)}, u32[]{:S(2)}) collective-permute-start(f32[224,2304]{1,0:T(8,128)} %collective-permute-done.20), channel_id=1, source_target_pairs={{0,8},{8,16},{16,24},{24,28},{28,20},{20,12},{12,4},{4,0},{1,9},{9... | collective-permute-start | bytes 6193160 | tf_op jit(solution)/shard_map/ppermute | solution.py:39
  339.1 45.4 %collective-permute-start.26 = (f32[224,2304]{1,0:T(8,128)}, f32[224,2304]{1,0:T(8,128)S(1)}, u32[]{:S(2)}, u32[]{:S(2)}) collective-permute-start(f32[224,2304]{1,0:T(8,128)} %copy-done.9), channel_id=1, source_target_pairs={{0,4},{8,0},{16,8},{24,16},{28,24},{20,28},{12,20},{4,12},{1,5},{9... | collective-permute-start | bytes 6193160 | tf_op jit(solution)/shard_map/ppermute | solution.py:39
  339.7 13.4 %collective-permute-start.27 = (f32[224,448]{1,0:T(8,128)S(1)}, f32[224,448]{1,0:T(8,128)S(1)}, u32[]{:S(2)}, u32[]{:S(2)}) collective-permute-start(f32[224,448]{1,0:T(8,128)S(1)} %select_add_fusion.3), channel_id=1, source_target_pairs={{0,2},{1,3},{2,0},{3,1},{4,6},{5,7},{6,4},{7,5},{8,10},{9,11},{10,... | collective-permute-start | bytes 1204232 | tf_op jit(solution)/shard_map/ppermute | solution.py:44
  345.9 35.6 %collective-permute-start.32 = (f32[224,448]{1,0:T(8,128)}, f32[224,448]{1,0:T(8,128)}, u32[]{:S(2)}, u32[]{:S(2)}) collective-permute-start(f32[224,448]{1,0:T(8,128)} %get-tuple-element.223), channel_id=1, source_target_pairs={{0,1},{1,0},{2,3},{3,2},{4,5},{5,4},{6,7},{7,6},{8,9},{9,8},{10,11... | collective-permute-start | bytes 1204232 | tf_op jit(solution)/shard_map/ppermute | solution.py:44
  347.0 32.8 %collective-permute-start.30 = (f32[224,448]{1,0:T(8,128)}, f32[224,448]{1,0:T(8,128)}, u32[]{:S(2)}, u32[]{:S(2)}) collective-permute-start(f32[224,448]{1,0:T(8,128)} %select_add_fusion.2), channel_id=1, source_target_pairs={{0,2},{1,3},{2,0},{3,1},{4,6},{5,7},{6,4},{7,5},{8,10},{9,11},{10,... | collective-permute-start | bytes 1204232 | tf_op jit(solution)/shard_map/ppermute | solution.py:44
  353.9 29.1 %collective-permute-start.28 = (f32[224,448]{1,0:T(8,128)}, f32[224,448]{1,0:T(8,128)}, u32[]{:S(2)}, u32[]{:S(2)}) collective-permute-start(f32[224,448]{1,0:T(8,128)} %add.591), channel_id=1, source_target_pairs={{0,1},{1,0},{2,3},{3,2},{4,5},{5,4},{6,7},{7,6},{8,9},{9,8},{10,11... | collective-permute-start | bytes 1204232 | tf_op jit(solution)/shard_map/ppermute | solution.py:44
  390.9 13.4 %collective-permute-start.33 = (f32[224,448]{1,0:T(8,128)S(1)}, f32[224,448]{1,0:T(8,128)S(1)}, u32[]{:S(2)}, u32[]{:S(2)}) collective-permute-start(f32[224,448]{1,0:T(8,128)S(1)} %select_add_fusion.1), channel_id=1, source_target_pairs={{0,2},{1,3},{2,0},{3,1},{4,6},{5,7},{6,4},{7,5},{8,10},{9,11},{10,... | collective-permute-start | bytes 1204232 | tf_op jit(solution)/shard_map/ppermute | solution.py:44
  392.7 21.1 %collective-permute-start.36 = (f32[224,448]{1,0:T(8,128)S(1)}, f32[224,448]{1,0:T(8,128)S(1)}, u32[]{:S(2)}, u32[]{:S(2)}) collective-permute-start(f32[224,448]{1,0:T(8,128)S(1)} %select_add_fusion), channel_id=1, source_target_pairs={{0,2},{1,3},{2,0},{3,1},{4,6},{5,7},{6,4},{7,5},{8,10},{9,11},{10,... | collective-permute-start | bytes 1204232 | tf_op jit(solution)/shard_map/ppermute | solution.py:44
  420.8 34.5 %collective-permute-start.38 = (f32[224,896]{1,0:T(8,128)}, f32[224,896]{1,0:T(8,128)}, u32[]{:S(2)}, u32[]{:S(2)}) collective-permute-start(f32[224,896]{1,0:T(8,128)} %copy.19), channel_id=1, source_target_pairs={{0,8},{8,16},{16,24},{24,28},{28,20},{20,12},{12,4},{4,0},{1,9},{9... | collective-permute-start | bytes 2408456 | tf_op jit(solution)/shard_map/ppermute | solution.py:39
  424.7 30.6 %collective-permute-start.39 = (f32[224,896]{1,0:T(8,128)}, f32[224,896]{1,0:T(8,128)}, u32[]{:S(2)}, u32[]{:S(2)}) collective-permute-start(f32[224,896]{1,0:T(8,128)} %copy.20), channel_id=1, source_target_pairs={{0,4},{8,0},{16,8},{24,16},{28,24},{20,28},{12,20},{4,12},{1,5},{9... | collective-permute-start | bytes 2408456 | tf_op jit(solution)/shard_map/ppermute | solution.py:39
  455.3 19.6 %collective-permute-start.40 = (f32[224,896]{1,0:T(8,128)}, f32[224,896]{1,0:T(8,128)S(1)}, u32[]{:S(2)}, u32[]{:S(2)}) collective-permute-start(f32[224,896]{1,0:T(8,128)} %collective-permute-done.38), channel_id=1, source_target_pairs={{0,8},{8,16},{16,24},{24,28},{28,20},{20,12},{12,4},{4,0},{1,9},{9... | collective-permute-start | bytes 2408456 | tf_op jit(solution)/shard_map/ppermute | solution.py:39
  457.3 19.5 %collective-permute-start.41 = (f32[224,896]{1,0:T(8,128)}, f32[224,896]{1,0:T(8,128)S(1)}, u32[]{:S(2)}, u32[]{:S(2)}) collective-permute-start(f32[224,896]{1,0:T(8,128)} %collective-permute-done.39), channel_id=1, source_target_pairs={{0,4},{8,0},{16,8},{24,16},{28,24},{20,28},{12,20},{4,12},{1,5},{9... | collective-permute-start | bytes 2408456 | tf_op jit(solution)/shard_map/ppermute | solution.py:39
  476.8 18.4 %collective-permute-start.42 = (f32[224,896]{1,0:T(8,128)S(1)}, f32[224,896]{1,0:T(8,128)S(1)}, u32[]{:S(2)}, u32[]{:S(2)}) collective-permute-start(f32[224,896]{1,0:T(8,128)S(1)} %collective-permute-done.40), channel_id=1, source_target_pairs={{0,8},{8,16},{16,24},{24,28},{28,20},{20,12},{12,4},{4,0},{1,9},{9... | collective-permute-start | bytes 2408456 | tf_op jit(solution)/shard_map/ppermute | solution.py:39
  478.6 17.9 %collective-permute-start.43 = (f32[224,896]{1,0:T(8,128)S(1)}, f32[224,896]{1,0:T(8,128)S(1)}, u32[]{:S(2)}, u32[]{:S(2)}) collective-permute-start(f32[224,896]{1,0:T(8,128)S(1)} %collective-permute-done.41), channel_id=1, source_target_pairs={{0,4},{8,0},{16,8},{24,16},{28,24},{20,28},{12,20},{4,12},{1,5},{9... | collective-permute-start | bytes 2408456 | tf_op jit(solution)/shard_map/ppermute | solution.py:39
  496.5 17.9 %collective-permute-start.44 = (f32[224,896]{1,0:T(8,128)S(1)}, f32[224,896]{1,0:T(8,128)S(1)}, u32[]{:S(2)}, u32[]{:S(2)}) collective-permute-start(f32[224,896]{1,0:T(8,128)S(1)} %collective-permute-done.42), channel_id=1, source_target_pairs={{0,8},{8,16},{16,24},{24,28},{28,20},{20,12},{12,4},{4,0},{1,9},{9... | collective-permute-start | bytes 2408456 | tf_op jit(solution)/shard_map/ppermute | solution.py:39
  497.1 17.5 %collective-permute-start.45 = (f32[224,896]{1,0:T(8,128)S(1)}, f32[224,896]{1,0:T(8,128)S(1)}, u32[]{:S(2)}, u32[]{:S(2)}) collective-permute-start(f32[224,896]{1,0:T(8,128)S(1)} %collective-permute-done.43), channel_id=1, source_target_pairs={{0,4},{8,0},{16,8},{24,16},{28,24},{20,28},{12,20},{4,12},{1,5},{9... | collective-permute-start | bytes 2408456 | tf_op jit(solution)/shard_map/ppermute | solution.py:39
  514.7 18.1 %collective-permute-start.46 = (f32[224,896]{1,0:T(8,128)S(1)}, f32[224,896]{1,0:T(8,128)S(1)}, u32[]{:S(2)}, u32[]{:S(2)}) collective-permute-start(f32[224,896]{1,0:T(8,128)S(1)} %collective-permute-done.44), channel_id=1, source_target_pairs={{0,8},{8,16},{16,24},{24,28},{28,20},{20,12},{12,4},{4,0},{1,9},{9... | collective-permute-start | bytes 2408456 | tf_op jit(solution)/shard_map/ppermute | solution.py:39
  515.3 17.8 %collective-permute-start.47 = (f32[224,896]{1,0:T(8,128)S(1)}, f32[224,896]{1,0:T(8,128)S(1)}, u32[]{:S(2)}, u32[]{:S(2)}) collective-permute-start(f32[224,896]{1,0:T(8,128)S(1)} %collective-permute-done.45), channel_id=1, source_target_pairs={{0,4},{8,0},{16,8},{24,16},{28,24},{20,28},{12,20},{4,12},{1,5},{9... | collective-permute-start | bytes 2408456 | tf_op jit(solution)/shard_map/ppermute | solution.py:39
  533.0 17.6 %collective-permute-start.48 = (f32[224,896]{1,0:T(8,128)S(1)}, f32[224,896]{1,0:T(8,128)S(1)}, u32[]{:S(2)}, u32[]{:S(2)}) collective-permute-start(f32[224,896]{1,0:T(8,128)S(1)} %collective-permute-done.46), channel_id=1, source_target_pairs={{0,8},{8,16},{16,24},{24,28},{28,20},{20,12},{12,4},{4,0},{1,9},{9... | collective-permute-start | bytes 2408456 | tf_op jit(solution)/shard_map/ppermute | solution.py:39
  533.3 17.6 %collective-permute-start.49 = (f32[224,896]{1,0:T(8,128)S(1)}, f32[224,896]{1,0:T(8,128)S(1)}, u32[]{:S(2)}, u32[]{:S(2)}) collective-permute-start(f32[224,896]{1,0:T(8,128)S(1)} %collective-permute-done.47), channel_id=1, source_target_pairs={{0,4},{8,0},{16,8},{24,16},{28,24},{20,28},{12,20},{4,12},{1,5},{9... | collective-permute-start | bytes 2408456 | tf_op jit(solution)/shard_map/ppermute | solution.py:39
  550.9 14.2 %collective-permute-start.50 = (f32[224,896]{1,0:T(8,128)S(1)}, f32[224,896]{1,0:T(8,128)S(1)}, u32[]{:S(2)}, u32[]{:S(2)}) collective-permute-start(f32[224,896]{1,0:T(8,128)S(1)} %collective-permute-done.48), channel_id=1, source_target_pairs={{0,8},{8,16},{16,24},{24,28},{28,20},{20,12},{12,4},{4,0},{1,9},{9... | collective-permute-start | bytes 2408456 | tf_op jit(solution)/shard_map/ppermute | solution.py:39
  551.4 14.0 %collective-permute-start.51 = (f32[224,896]{1,0:T(8,128)S(1)}, f32[224,896]{1,0:T(8,128)S(1)}, u32[]{:S(2)}, u32[]{:S(2)}) collective-permute-start(f32[224,896]{1,0:T(8,128)S(1)} %collective-permute-done.49), channel_id=1, source_target_pairs={{0,4},{8,0},{16,8},{24,16},{28,24},{20,28},{12,20},{4,12},{1,5},{9... | collective-permute-start | bytes 2408456 | tf_op jit(solution)/shard_map/ppermute | solution.py:39
  570.8 37.8 %collective-permute-start.52 = (f32[448,896]{1,0:T(8,128)}, f32[448,896]{1,0:T(8,128)}, u32[]{:S(2)}, u32[]{:S(2)}) collective-permute-start(f32[448,896]{1,0:T(8,128)} %copy.37), channel_id=1, source_target_pairs={{0,2},{1,3},{2,0},{3,1},{4,6},{5,7},{6,4},{7,5},{8,10},{9,11},{10,... | collective-permute-start | bytes 4816904 | tf_op jit(solution)/shard_map/ppermute | solution.py:44
  (63 other events, 653.2 us)

commit v6 on v3

--- a/solution.py
+++ b/solution.py
@@ -86,13 +86,13 @@
         near_blocks.append(near_part)
         far_blocks.append(far_part)
 
-    near_all = jnp.stack(near_blocks)
-    far_all = jnp.stack(far_blocks)
+    near_all = jnp.concatenate(near_blocks, axis=0)
+    far_all = jnp.concatenate(far_blocks, axis=0)
     parts = []
     for k in range(per):
         at = my_col * per + k
-        parts.append(lax.dynamic_index_in_dim(near_all, (mine - at) % row_count, 0, False))
-        parts.append(lax.dynamic_index_in_dim(far_all, (at - mine) % row_count, 0, False))
+        parts.append(lax.dynamic_slice_in_dim(near_all, (mine - at) % row_count * near, near))
+        parts.append(lax.dynamic_slice_in_dim(far_all, (at - mine) % row_count * near, near))
     gram_tile = jnp.concatenate(parts, axis=0).T
 
     up, down = gram_tile[:near], gram_tile[near:]
@@ -105,15 +105,22 @@
         term = term + product(far_blocks[step], down, ((0,), (0,)))
         square_tile = term if square_tile is None else square_tile + term
         if not last:
-            up, down, square_tile = lax.optimization_barrier((next_up, next_down, square_tile))
+            up, down, square_tile, slab = lax.optimization_barrier(
+                (next_up, next_down, square_tile, slab)
+            )
     poly_tile = COEF_B * gram_tile + COEF_C * square_tile
 
     tiles = {0: poly_tile}
     for k in range(1, col_count):
         low_bit = k & -k
+        if low_bit == 1 and k > 1:
+            continue
         tiles[k] = swap(tiles[k ^ low_bit], low_bit)
     applied = None
     for k in range(0, col_count, 2):
+        if applied is not None:
+            tiles[k], applied = lax.optimization_barrier((tiles[k], applied))
+            tiles[k + 1] = swap(tiles[k], 1)
         pair = jnp.concatenate(
             [
                 jnp.where(upper, tiles[k + 1], tiles[k]),

time: 585 us -> 573 us (0.979)
  waiting for transfers between devices: 346 us -> 309 us
  matrix products: 97 us -> 110 us
  local copies, waits for them, and re-layouts: 53.1 us -> 61.3 us
  other arithmetic: 18.2 us -> 25.1 us
    ppermute x27, waiting for transfers between devices: 116 us -> 95.2 us  [swap(): return lax.ppermute(value, 'col', [(k, k ^ bit) for k in range(count)])]
    ppermute x28, waiting for transfers between devices: 231 us -> 214 us  [shift(): return lax.ppermute(value, 'row', pairs)]
    dot_general x34, matrix products: 97 us -> 110 us  [product(): lax.dot_general(left, right, (dims, ((), ())), precision=PREC, preferred_...]
    squeeze x6 -> x0, local copies, waits for them, and re-layouts: 11.1 us -> none  [the longest x3 6.09 us: body(): lax.dynamic_index_in_dim(near_all, (mine - at) % row_count, 0, False)]
    slice x1 -> x3, local copies, waits for them, and re-layouts: 0.11 us -> 6.27 us  [body(): up, down = (gram_tile[:near], gram_tile[near:])]
  transfers between devices with their start and end apart: 55 -> 55, of which waited for: 41 -> 42; matrix products, arithmetic and copies ran while one was open for 21% -> 23% of each run, Pallas kernels for 0% -> 0%
where the time goes in v6:
time: 573 us; the launch traced here: 566 us
  waiting for transfers between devices  309 us (54%)
  matrix products  110 us (19%)
  local copies, waits for them, and re-layouts  61.3 us (11%)
  starting transfers between devices  46.5 us (8%)
  other arithmetic  25.1 us (4%)
  between operations  14.7 us (3%)
    ppermute x28, waiting for transfers between devices, shift(): return lax.ppermute(value, 'row', pairs)  214 us
    dot_general x34, matrix products, product(): lax.dot_general(left, right, (dims, ((), ())), precision=PREC, preferred_...  110 us
    ppermute x27, waiting for transfers between devices, swap(): return lax.ppermute(value, 'col', [(k, k ^ bit) for k in range(count)])  95.2 us
    ppermute x28, starting transfers between devices, shift(): return lax.ppermute(value, 'row', pairs)  31 us
    dynamic_update_slice x7, local copies, waits for them, and re-layouts, body(): slab = lax.dynamic_update_slice(slab, down, (far_at, 0))  17.3 us
    dynamic_update_slice x7, local copies, waits for them, and re-layouts, body(): slab = lax.dynamic_update_slice(slab, up, (near_at, 0))  16.7 us
    ppermute x27, starting transfers between devices, swap(): return lax.ppermute(value, 'col', [(k, k ^ bit) for k in range(count)])  15.4 us
  transfers between devices with their start and end apart: 55, of which 42 were waited for; matrix products, arithmetic and copies ran while one was open for 23% of the time, Pallas kernels for 0%

profile of v6, /device:TPU:0, one launch (start us, length us, event | category | flops | bytes accessed | tf_op | source)
XLA Modules:
  0.0 566.1 jit_solution(8961359884178214235)
XLA Ops:
  0.0 4.6 fusion.25
  4.6 3.0 collective-permute-start
  9.5 4.7 broadcast_select_fusion.27
  18.3 10.8 %collective-permute-done.3 = f32[224,448]{1,0:T(8,128)S(1)} collective-permute-done((f32[224,448]{1,0:T(8,128)S(1)}, f32[224,448]{1,0:T(8,128)S(1)}, u32[]{:S(2)}, u32[]{:S(2)}) %collective-permute-start.3) | collective-permute-done | bytes 401440 | tf_op jit(solution)/shard_map/ppermute | solution.py:32
  34.0 18.7 %collective-permute-done = f32[224,2304]{1,0:T(8,128)S(1)} collective-permute-done((f32[224,2304]{1,0:T(8,128)}, f32[224,2304]{1,0:T(8,128)S(1)}, u32[]{:S(2)}, u32[]{:S(2)}) %collective-permute-start) | collective-permute-done | bytes 2064416 | tf_op jit(solution)/shard_map/ppermute | solution.py:27
  54.3 4.8 fusion.27
  61.4 2.9 broadcast_select_fusion.24
  70.2 11.3 %collective-permute-done.8 = f32[224,448]{1,0:T(8,128)S(1)} collective-permute-done((f32[224,448]{1,0:T(8,128)S(1)}, f32[224,448]{1,0:T(8,128)S(1)}, u32[]{:S(2)}, u32[]{:S(2)}) %collective-permute-start.8) | collective-permute-done | bytes 401440 | tf_op jit(solution)/shard_map/ppermute | solution.py:32
  84.6 20.7 %collective-permute-done.5 = f32[224,2304]{1,0:T(8,128)} collective-permute-done((f32[224,2304]{1,0:T(8,128)S(1)}, f32[224,2304]{1,0:T(8,128)}, u32[]{:S(2)}, u32[]{:S(2)}) %collective-permute-start.5) | collective-permute-done | bytes 2064416 | tf_op jit(solution)/shard_map/ppermute | solution.py:27
  105.3 3.5 fusion.28
  110.9 4.5 broadcast_select_fusion.21
  120.1 3.0 constant_dynamic-update-slice_fusion.25
  123.1 8.1 %collective-permute-done.13 = f32[224,448]{1,0:T(8,128)S(1)} collective-permute-done((f32[224,448]{1,0:T(8,128)S(1)}, f32[224,448]{1,0:T(8,128)S(1)}, u32[]{:S(2)}, u32[]{:S(2)}) %collective-permute-start.13) | collective-permute-done | bytes 401440 | tf_op jit(solution)/shard_map/ppermute | solution.py:32
  131.4 3.2 constant_dynamic-update-slice_fusion.24
  135.6 19.2 %collective-permute-done.10 = f32[224,2304]{1,0:T(8,128)} collective-permute-done((f32[224,2304]{1,0:T(8,128)}, f32[224,2304]{1,0:T(8,128)}, u32[]{:S(2)}, u32[]{:S(2)}) %collective-permute-start.10) | collective-permute-done | bytes 2064416 | tf_op jit(solution)/shard_map/ppermute | solution.py:27
  159.5 4.7 broadcast_select_fusion.18
  169.2 3.0 constant_dynamic-update-slice_fusion.23
  172.2 7.9 %collective-permute-done.18 = f32[224,448]{1,0:T(8,128)S(1)} collective-permute-done((f32[224,448]{1,0:T(8,128)S(1)}, f32[224,448]{1,0:T(8,128)S(1)}, u32[]{:S(2)}, u32[]{:S(2)}) %collective-permute-start.18) | collective-permute-done | bytes 401440 | tf_op jit(solution)/shard_map/ppermute | solution.py:32
  183.1 19.2 %collective-permute-done.15 = f32[224,2304]{1,0:T(8,128)} collective-permute-done((f32[224,2304]{1,0:T(8,128)}, f32[224,2304]{1,0:T(8,128)}, u32[]{:S(2)}, u32[]{:S(2)}) %collective-permute-start.15) | collective-permute-done | bytes 2064416 | tf_op jit(solution)/shard_map/ppermute | solution.py:27
  202.3 3.7 fusion.30
  208.1 4.7 broadcast_select_fusion.15
  217.9 3.0 constant_dynamic-update-slice_fusion.21
  220.9 7.9 %collective-permute-done.23 = f32[224,448]{1,0:T(8,128)S(1)} collective-permute-done((f32[224,448]{1,0:T(8,128)S(1)}, f32[224,448]{1,0:T(8,128)S(1)}, u32[]{:S(2)}, u32[]{:S(2)}) %collective-permute-start.23) | collective-permute-done | bytes 401440 | tf_op jit(solution)/shard_map/ppermute | solution.py:32
  228.9 3.2 constant_dynamic-update-slice_fusion.20
  233.1 16.9 %collective-permute-done.20 = f32[224,2304]{1,0:T(8,128)} collective-permute-done((f32[224,2304]{1,0:T(8,128)}, f32[224,2304]{1,0:T(8,128)}, u32[]{:S(2)}, u32[]{:S(2)}) %collective-permute-start.20) | collective-permute-done | bytes 2064416 | tf_op jit(solution)/shard_map/ppermute | solution.py:27
  254.2 4.7 broadcast_select_fusion.12
  270.0 3.0 constant_dynamic-update-slice_fusion.19
  273.0 8.4 %collective-permute-done.28 = f32[224,448]{1,0:T(8,128)S(1)} collective-permute-done((f32[224,448]{1,0:T(8,128)S(1)}, f32[224,448]{1,0:T(8,128)S(1)}, u32[]{:S(2)}, u32[]{:S(2)}) %collective-permute-start.28) | collective-permute-done | bytes 401440 | tf_op jit(solution)/shard_map/ppermute | solution.py:32
  283.4 10.6 %collective-permute-done.25 = f32[224,2304]{1,0:T(8,128)} collective-permute-done((f32[224,2304]{1,0:T(8,128)}, f32[224,2304]{1,0:T(8,128)}, u32[]{:S(2)}, u32[]{:S(2)}) %collective-permute-start.25) | collective-permute-done | bytes 2064416 | tf_op jit(solution)/shard_map/ppermute | solution.py:27
  294.0 3.7 fusion.32
  300.0 3.8 broadcast_select_fusion.9
  307.3 3.0 constant_dynamic-update-slice_fusion.17
  310.3 8.0 %collective-permute-done.33 = f32[224,448]{1,0:T(8,128)S(1)} collective-permute-done((f32[224,448]{1,0:T(8,128)S(1)}, f32[224,448]{1,0:T(8,128)S(1)}, u32[]{:S(2)}, u32[]{:S(2)}) %collective-permute-start.33) | collective-permute-done | bytes 401440 | tf_op jit(solution)/shard_map/ppermute | solution.py:32
  318.5 3.1 constant_dynamic-update-slice_fusion.16
  321.8 16.8 %collective-permute-done.30 = f32[224,2304]{1,0:T(8,128)S(1)} collective-permute-done((f32[224,2304]{1,0:T(8,128)}, f32[224,2304]{1,0:T(8,128)S(1)}, u32[]{:S(2)}, u32[]{:S(2)}) %collective-permute-start.30) | collective-permute-done | bytes 2064416 | tf_op jit(solution)/shard_map/ppermute | solution.py:27
  346.7 10.8 %collective-permute-done.36 = f32[224,448]{1,0:T(8,128)S(1)} collective-permute-done((f32[224,448]{1,0:T(8,128)S(1)}, f32[224,448]{1,0:T(8,128)S(1)}, u32[]{:S(2)}, u32[]{:S(2)}) %collective-permute-start.36) | collective-permute-done | bytes 401440 | tf_op jit(solution)/shard_map/ppermute | solution.py:32
  368.9 3.1 constant_dynamic-update-slice_fusion.14
  373.9 10.9 %collective-permute-done.38 = f32[224,896]{1,0:T(8,128)} collective-permute-done((f32[224,896]{1,0:T(8,128)}, f32[224,896]{1,0:T(8,128)}, u32[]{:S(2)}, u32[]{:S(2)}) %collective-permute-start.38) | collective-permute-done | bytes 802848 | tf_op jit(solution)/shard_map/ppermute | solution.py:27
  393.4 13.0 %collective-permute-done.40 = f32[224,896]{1,0:T(8,128)S(1)} collective-permute-done((f32[224,896]{1,0:T(8,128)}, f32[224,896]{1,0:T(8,128)S(1)}, u32[]{:S(2)}, u32[]{:S(2)}) %collective-permute-start.40) | collective-permute-done | bytes 802848 | tf_op jit(solution)/shard_map/ppermute | solution.py:27
  411.8 13.2 %collective-permute-done.42 = f32[224,896]{1,0:T(8,128)S(1)} collective-permute-done((f32[224,896]{1,0:T(8,128)S(1)}, f32[224,896]{1,0:T(8,128)S(1)}, u32[]{:S(2)}, u32[]{:S(2)}) %collective-permute-start.42) | collective-permute-done | bytes 802848 | tf_op jit(solution)/shard_map/ppermute | solution.py:27
  430.2 12.7 %collective-permute-done.44 = f32[224,896]{1,0:T(8,128)S(1)} collective-permute-done((f32[224,896]{1,0:T(8,128)S(1)}, f32[224,896]{1,0:T(8,128)S(1)}, u32[]{:S(2)}, u32[]{:S(2)}) %collective-permute-start.44) | collective-permute-done | bytes 802848 | tf_op jit(solution)/shard_map/ppermute | solution.py:27
  448.3 13.1 %collective-permute-done.46 = f32[224,896]{1,0:T(8,128)S(1)} collective-permute-done((f32[224,896]{1,0:T(8,128)S(1)}, f32[224,896]{1,0:T(8,128)S(1)}, u32[]{:S(2)}, u32[]{:S(2)}) %collective-permute-start.46) | collective-permute-done | bytes 802848 | tf_op jit(solution)/shard_map/ppermute | solution.py:27
  466.7 13.0 %collective-permute-done.48 = f32[224,896]{1,0:T(8,128)S(1)} collective-permute-done((f32[224,896]{1,0:T(8,128)S(1)}, f32[224,896]{1,0:T(8,128)S(1)}, u32[]{:S(2)}, u32[]{:S(2)}) %collective-permute-start.48) | collective-permute-done | bytes 802848 | tf_op jit(solution)/shard_map/ppermute | solution.py:27
  484.8 8.7 %collective-permute-done.50 = f32[224,896]{1,0:T(8,128)S(1)} collective-permute-done((f32[224,896]{1,0:T(8,128)S(1)}, f32[224,896]{1,0:T(8,128)S(1)}, u32[]{:S(2)}, u32[]{:S(2)}) %collective-permute-start.50) | collective-permute-done | bytes 802848 | tf_op jit(solution)/shard_map/ppermute | solution.py:27
  507.5 18.6 %fusion.2 = f32[448,2304]{1,0:T(8,128)} fusion(f32[3584,2304]{1,0:T(8,128)} %constant_dynamic-update-slice_fusion.14, s32[]{:T(128)S(6)} %select_n.367, f32[448,896]{0,1:T(8,128)S(1)} %get-tuple-element.138, f32[448,896]{0,1:T(8,128)S(1)} %get-tuple-element.137), kind=kOutput, calls=%fused_computation.2 | convolution fusion | flops 11098931200 | bytes 23855108 | tf_op jit(solution)/shard_map/dot_general | solution.py:15
  526.1 10.7 %collective-permute-done.52 = f32[448,896]{1,0:T(8,128)S(1)} collective-permute-done((f32[448,896]{1,0:T(8,128)}, f32[448,896]{1,0:T(8,128)S(1)}, u32[]{:S(2)}, u32[]{:S(2)}) %collective-permute-start.52) | collective-permute-done | bytes 1605664 | tf_op jit(solution)/shard_map/ppermute | solution.py:32
  545.1 18.0 %fusion = f32[448,2304]{1,0:T(8,128)S(1)} fusion(f32[3584,2304]{1,0:T(8,128)} %constant_dynamic-update-slice_fusion.14, s32[]{:T(128)S(6)} %select_n.370, f32[448,896]{0,1:T(8,128)S(1)} %get-tuple-element.136, f32[448,896]{0,1:T(8,128)S(1)} %get-tuple-element.135), kind=kOutput, calls=%fused_computation | convolution fusion | flops 11098931200 | bytes 23855108 | tf_op jit(solution)/shard_map/dot_general | solution.py:15
  563.1 2.8 add_multiply_fusion
  (276 shorter events, 140.8 us)
Async XLA Ops:
  4.6 48.1 %collective-permute-start = (f32[224,2304]{1,0:T(8,128)}, f32[224,2304]{1,0:T(8,128)S(1)}, u32[]{:S(2)}, u32[]{:S(2)}) collective-permute-start(f32[224,2304]{1,0:T(8,128)} %get-tuple-element.134), channel_id=1, source_target_pairs={{0,8},{8,16},{16,24},{24,28},{28,20},{20,12},{12,4},{4,0},{1,9},{9... | collective-permute-start | bytes 6193160 | tf_op jit(solution)/shard_map/ppermute | solution.py:27
  7.6 46.7 %collective-permute-start.1 = (f32[224,2304]{1,0:T(8,128)}, f32[224,2304]{1,0:T(8,128)}, u32[]{:S(2)}, u32[]{:S(2)}) collective-permute-start(f32[224,2304]{1,0:T(8,128)} %get-tuple-element.133), channel_id=1, source_target_pairs={{0,4},{8,0},{16,8},{24,16},{28,24},{20,28},{12,20},{4,12},{1,5},{9... | collective-permute-start | bytes 6193160 | tf_op jit(solution)/shard_map/ppermute | solution.py:27
  16.3 12.9 %collective-permute-start.3 = (f32[224,448]{1,0:T(8,128)S(1)}, f32[224,448]{1,0:T(8,128)S(1)}, u32[]{:S(2)}, u32[]{:S(2)}) collective-permute-start(f32[224,448]{1,0:T(8,128)S(1)} %select_add_fusion.7), channel_id=1, source_target_pairs={{0,2},{1,3},{2,0},{3,1},{4,6},{5,7},{6,4},{7,5},{8,10},{9,11},{10,... | collective-permute-start | bytes 1204232 | tf_op jit(solution)/shard_map/ppermute | solution.py:32
  29.2 2.9 collective-permute-start.4
  59.2 46.2 %collective-permute-start.6 = (f32[224,2304]{1,0:T(8,128)}, f32[224,2304]{1,0:T(8,128)}, u32[]{:S(2)}, u32[]{:S(2)}) collective-permute-start(f32[224,2304]{1,0:T(8,128)} %collective-permute-done.1), channel_id=1, source_target_pairs={{0,4},{8,0},{16,8},{24,16},{28,24},{20,28},{12,20},{4,12},{1,5},{9... | collective-permute-start | bytes 6193160 | tf_op jit(solution)/shard_map/ppermute | solution.py:27
  59.5 45.8 %collective-permute-start.5 = (f32[224,2304]{1,0:T(8,128)S(1)}, f32[224,2304]{1,0:T(8,128)}, u32[]{:S(2)}, u32[]{:S(2)}) collective-permute-start(f32[224,2304]{1,0:T(8,128)S(1)} %collective-permute-done), channel_id=1, source_target_pairs={{0,8},{8,16},{16,24},{24,28},{28,20},{20,12},{12,4},{4,0},{1,9},{9... | collective-permute-start | bytes 6193160 | tf_op jit(solution)/shard_map/ppermute | solution.py:27
  64.3 2.8 collective-permute-start.7
  68.4 13.0 %collective-permute-start.8 = (f32[224,448]{1,0:T(8,128)S(1)}, f32[224,448]{1,0:T(8,128)S(1)}, u32[]{:S(2)}, u32[]{:S(2)}) collective-permute-start(f32[224,448]{1,0:T(8,128)S(1)} %select_add_fusion.6), channel_id=1, source_target_pairs={{0,2},{1,3},{2,0},{3,1},{4,6},{5,7},{6,4},{7,5},{8,10},{9,11},{10,... | collective-permute-start | bytes 1204232 | tf_op jit(solution)/shard_map/ppermute | solution.py:32
  108.8 46.0 %collective-permute-start.11 = (f32[224,2304]{1,0:T(8,128)}, f32[224,2304]{1,0:T(8,128)S(1)}, u32[]{:S(2)}, u32[]{:S(2)}) collective-permute-start(f32[224,2304]{1,0:T(8,128)} %collective-permute-done.6), channel_id=1, source_target_pairs={{0,4},{8,0},{16,8},{24,16},{28,24},{20,28},{12,20},{4,12},{1,5},{9... | collective-permute-start | bytes 6193160 | tf_op jit(solution)/shard_map/ppermute | solution.py:27
  110.4 44.5 %collective-permute-start.10 = (f32[224,2304]{1,0:T(8,128)}, f32[224,2304]{1,0:T(8,128)}, u32[]{:S(2)}, u32[]{:S(2)}) collective-permute-start(f32[224,2304]{1,0:T(8,128)} %collective-permute-done.5), channel_id=1, source_target_pairs={{0,8},{8,16},{16,24},{24,28},{28,20},{20,12},{12,4},{4,0},{1,9},{9... | collective-permute-start | bytes 6193160 | tf_op jit(solution)/shard_map/ppermute | solution.py:27
  115.4 2.0 collective-permute-start.12
  118.6 12.6 %collective-permute-start.13 = (f32[224,448]{1,0:T(8,128)S(1)}, f32[224,448]{1,0:T(8,128)S(1)}, u32[]{:S(2)}, u32[]{:S(2)}) collective-permute-start(f32[224,448]{1,0:T(8,128)S(1)} %select_add_fusion.5), channel_id=1, source_target_pairs={{0,2},{1,3},{2,0},{3,1},{4,6},{5,7},{6,4},{7,5},{8,10},{9,11},{10,... | collective-permute-start | bytes 1204232 | tf_op jit(solution)/shard_map/ppermute | solution.py:32
  131.3 3.3 collective-permute-start.14
  157.0 45.3 %collective-permute-start.16 = (f32[224,2304]{1,0:T(8,128)S(1)}, f32[224,2304]{1,0:T(8,128)}, u32[]{:S(2)}, u32[]{:S(2)}) collective-permute-start(f32[224,2304]{1,0:T(8,128)S(1)} %collective-permute-done.11), channel_id=1, source_target_pairs={{0,4},{8,0},{16,8},{24,16},{28,24},{20,28},{12,20},{4,12},{1,5},{9... | collective-permute-start | bytes 6193160 | tf_op jit(solution)/shard_map/ppermute | solution.py:27
  158.6 43.7 %collective-permute-start.15 = (f32[224,2304]{1,0:T(8,128)}, f32[224,2304]{1,0:T(8,128)}, u32[]{:S(2)}, u32[]{:S(2)}) collective-permute-start(f32[224,2304]{1,0:T(8,128)} %collective-permute-done.10), channel_id=1, source_target_pairs={{0,8},{8,16},{16,24},{24,28},{28,20},{20,12},{12,4},{4,0},{1,9},{9... | collective-permute-start | bytes 6193160 | tf_op jit(solution)/shard_map/ppermute | solution.py:27
  164.2 2.2 collective-permute-start.17
  167.6 12.5 %collective-permute-start.18 = (f32[224,448]{1,0:T(8,128)S(1)}, f32[224,448]{1,0:T(8,128)S(1)}, u32[]{:S(2)}, u32[]{:S(2)}) collective-permute-start(f32[224,448]{1,0:T(8,128)S(1)} %select_add_fusion.4), channel_id=1, source_target_pairs={{0,2},{1,3},{2,0},{3,1},{4,6},{5,7},{6,4},{7,5},{8,10},{9,11},{10,... | collective-permute-start | bytes 1204232 | tf_op jit(solution)/shard_map/ppermute | solution.py:32
  206.1 43.9 %collective-permute-start.21 = (f32[224,2304]{1,0:T(8,128)}, f32[224,2304]{1,0:T(8,128)S(1)}, u32[]{:S(2)}, u32[]{:S(2)}) collective-permute-start(f32[224,2304]{1,0:T(8,128)} %collective-permute-done.16), channel_id=1, source_target_pairs={{0,4},{8,0},{16,8},{24,16},{28,24},{20,28},{12,20},{4,12},{1,5},{9... | collective-permute-start | bytes 6193160 | tf_op jit(solution)/shard_map/ppermute | solution.py:27
  207.7 42.3 %collective-permute-start.20 = (f32[224,2304]{1,0:T(8,128)}, f32[224,2304]{1,0:T(8,128)}, u32[]{:S(2)}, u32[]{:S(2)}) collective-permute-start(f32[224,2304]{1,0:T(8,128)} %collective-permute-done.15), channel_id=1, source_target_pairs={{0,8},{8,16},{16,24},{24,28},{28,20},{20,12},{12,4},{4,0},{1,9},{9... | collective-permute-start | bytes 6193160 | tf_op jit(solution)/shard_map/ppermute | solution.py:27
  212.8 2.2 collective-permute-start.22
  216.3 12.5 %collective-permute-start.23 = (f32[224,448]{1,0:T(8,128)S(1)}, f32[224,448]{1,0:T(8,128)S(1)}, u32[]{:S(2)}, u32[]{:S(2)}) collective-permute-start(f32[224,448]{1,0:T(8,128)S(1)} %select_add_fusion.3), channel_id=1, source_target_pairs={{0,2},{1,3},{2,0},{3,1},{4,6},{5,7},{6,4},{7,5},{8,10},{9,11},{10,... | collective-permute-start | bytes 1204232 | tf_op jit(solution)/shard_map/ppermute | solution.py:32
  228.8 3.3 collective-permute-start.24
  252.2 41.8 %collective-permute-start.26 = (f32[224,2304]{1,0:T(8,128)S(1)}, f32[224,2304]{1,0:T(8,128)}, u32[]{:S(2)}, u32[]{:S(2)}) collective-permute-start(f32[224,2304]{1,0:T(8,128)S(1)} %collective-permute-done.21), channel_id=1, source_target_pairs={{0,4},{8,0},{16,8},{24,16},{28,24},{20,28},{12,20},{4,12},{1,5},{9... | collective-permute-start | bytes 6193160 | tf_op jit(solution)/shard_map/ppermute | solution.py:27
  253.5 40.5 %collective-permute-start.25 = (f32[224,2304]{1,0:T(8,128)}, f32[224,2304]{1,0:T(8,128)}, u32[]{:S(2)}, u32[]{:S(2)}) collective-permute-start(f32[224,2304]{1,0:T(8,128)} %collective-permute-done.20), channel_id=1, source_target_pairs={{0,8},{8,16},{16,24},{24,28},{28,20},{20,12},{12,4},{4,0},{1,9},{9... | collective-permute-start | bytes 6193160 | tf_op jit(solution)/shard_map/ppermute | solution.py:27
  258.9 7.2 %collective-permute-start.27 = (f32[224,448]{1,0:T(8,128)}, f32[224,448]{1,0:T(8,128)}, u32[]{:S(2)}, u32[]{:S(2)}) collective-permute-start(f32[224,448]{1,0:T(8,128)} %get-tuple-element.171), channel_id=1, source_target_pairs={{0,1},{1,0},{2,3},{3,2},{4,5},{5,4},{6,7},{7,6},{8,9},{9,8},{10,11... | collective-permute-start | bytes 1204232 | tf_op jit(solution)/shard_map/ppermute | solution.py:32
  268.4 13.0 %collective-permute-start.28 = (f32[224,448]{1,0:T(8,128)S(1)}, f32[224,448]{1,0:T(8,128)S(1)}, u32[]{:S(2)}, u32[]{:S(2)}) collective-permute-start(f32[224,448]{1,0:T(8,128)S(1)} %select_add_fusion.2), channel_id=1, source_target_pairs={{0,2},{1,3},{2,0},{3,1},{4,6},{5,7},{6,4},{7,5},{8,10},{9,11},{10,... | collective-permute-start | bytes 1204232 | tf_op jit(solution)/shard_map/ppermute | solution.py:32
  297.7 40.8 %collective-permute-start.31 = (f32[224,2304]{1,0:T(8,128)}, f32[224,2304]{1,0:T(8,128)S(1)}, u32[]{:S(2)}, u32[]{:S(2)}) collective-permute-start(f32[224,2304]{1,0:T(8,128)} %collective-permute-done.26), channel_id=1, source_target_pairs={{0,4},{8,0},{16,8},{24,16},{28,24},{20,28},{12,20},{4,12},{1,5},{9... | collective-permute-start | bytes 6193160 | tf_op jit(solution)/shard_map/ppermute | solution.py:27
  298.8 39.8 %collective-permute-start.30 = (f32[224,2304]{1,0:T(8,128)}, f32[224,2304]{1,0:T(8,128)S(1)}, u32[]{:S(2)}, u32[]{:S(2)}) collective-permute-start(f32[224,2304]{1,0:T(8,128)} %collective-permute-done.25), channel_id=1, source_target_pairs={{0,8},{8,16},{16,24},{24,28},{28,20},{20,12},{12,4},{4,0},{1,9},{9... | collective-permute-start | bytes 6193160 | tf_op jit(solution)/shard_map/ppermute | solution.py:27
  305.8 12.6 %collective-permute-start.33 = (f32[224,448]{1,0:T(8,128)S(1)}, f32[224,448]{1,0:T(8,128)S(1)}, u32[]{:S(2)}, u32[]{:S(2)}) collective-permute-start(f32[224,448]{1,0:T(8,128)S(1)} %select_add_fusion.1), channel_id=1, source_target_pairs={{0,2},{1,3},{2,0},{3,1},{4,6},{5,7},{6,4},{7,5},{8,10},{9,11},{10,... | collective-permute-start | bytes 1204232 | tf_op jit(solution)/shard_map/ppermute | solution.py:32
  318.4 3.2 collective-permute-start.34
  344.9 12.6 %collective-permute-start.36 = (f32[224,448]{1,0:T(8,128)S(1)}, f32[224,448]{1,0:T(8,128)S(1)}, u32[]{:S(2)}, u32[]{:S(2)}) collective-permute-start(f32[224,448]{1,0:T(8,128)S(1)} %select_add_fusion), channel_id=1, source_target_pairs={{0,2},{1,3},{2,0},{3,1},{4,6},{5,7},{6,4},{7,5},{8,10},{9,11},{10,... | collective-permute-start | bytes 1204232 | tf_op jit(solution)/shard_map/ppermute | solution.py:32
  364.5 20.3 %collective-permute-start.38 = (f32[224,896]{1,0:T(8,128)}, f32[224,896]{1,0:T(8,128)}, u32[]{:S(2)}, u32[]{:S(2)}) collective-permute-start(f32[224,896]{1,0:T(8,128)} %copy.19), channel_id=1, source_target_pairs={{0,8},{8,16},{16,24},{24,28},{28,20},{20,12},{12,4},{4,0},{1,9},{9... | collective-permute-start | bytes 2408456 | tf_op jit(solution)/shard_map/ppermute | solution.py:27
  367.5 19.9 %collective-permute-start.39 = (f32[224,896]{1,0:T(8,128)}, f32[224,896]{1,0:T(8,128)S(1)}, u32[]{:S(2)}, u32[]{:S(2)}) collective-permute-start(f32[224,896]{1,0:T(8,128)} %copy.20), channel_id=1, source_target_pairs={{0,4},{8,0},{16,8},{24,16},{28,24},{20,28},{12,20},{4,12},{1,5},{9... | collective-permute-start | bytes 2408456 | tf_op jit(solution)/shard_map/ppermute | solution.py:27
  387.3 19.0 %collective-permute-start.40 = (f32[224,896]{1,0:T(8,128)}, f32[224,896]{1,0:T(8,128)S(1)}, u32[]{:S(2)}, u32[]{:S(2)}) collective-permute-start(f32[224,896]{1,0:T(8,128)} %collective-permute-done.38), channel_id=1, source_target_pairs={{0,8},{8,16},{16,24},{24,28},{28,20},{20,12},{12,4},{4,0},{1,9},{9... | collective-permute-start | bytes 2408456 | tf_op jit(solution)/shard_map/ppermute | solution.py:27
  388.4 18.7 %collective-permute-start.41 = (f32[224,896]{1,0:T(8,128)S(1)}, f32[224,896]{1,0:T(8,128)S(1)}, u32[]{:S(2)}, u32[]{:S(2)}) collective-permute-start(f32[224,896]{1,0:T(8,128)S(1)} %collective-permute-done.39), channel_id=1, source_target_pairs={{0,4},{8,0},{16,8},{24,16},{28,24},{20,28},{12,20},{4,12},{1,5},{9... | collective-permute-start | bytes 2408456 | tf_op jit(solution)/shard_map/ppermute | solution.py:27
  407.1 17.9 %collective-permute-start.42 = (f32[224,896]{1,0:T(8,128)S(1)}, f32[224,896]{1,0:T(8,128)S(1)}, u32[]{:S(2)}, u32[]{:S(2)}) collective-permute-start(f32[224,896]{1,0:T(8,128)S(1)} %collective-permute-done.40), channel_id=1, source_target_pairs={{0,8},{8,16},{16,24},{24,28},{28,20},{20,12},{12,4},{4,0},{1,9},{9... | collective-permute-start | bytes 2408456 | tf_op jit(solution)/shard_map/ppermute | solution.py:27
  407.8 17.7 %collective-permute-start.43 = (f32[224,896]{1,0:T(8,128)S(1)}, f32[224,896]{1,0:T(8,128)S(1)}, u32[]{:S(2)}, u32[]{:S(2)}) collective-permute-start(f32[224,896]{1,0:T(8,128)S(1)} %collective-permute-done.41), channel_id=1, source_target_pairs={{0,4},{8,0},{16,8},{24,16},{28,24},{20,28},{12,20},{4,12},{1,5},{9... | collective-permute-start | bytes 2408456 | tf_op jit(solution)/shard_map/ppermute | solution.py:27
  425.5 17.4 %collective-permute-start.44 = (f32[224,896]{1,0:T(8,128)S(1)}, f32[224,896]{1,0:T(8,128)S(1)}, u32[]{:S(2)}, u32[]{:S(2)}) collective-permute-start(f32[224,896]{1,0:T(8,128)S(1)} %collective-permute-done.42), channel_id=1, source_target_pairs={{0,8},{8,16},{16,24},{24,28},{28,20},{20,12},{12,4},{4,0},{1,9},{9... | collective-permute-start | bytes 2408456 | tf_op jit(solution)/shard_map/ppermute | solution.py:27
  425.8 17.8 %collective-permute-start.45 = (f32[224,896]{1,0:T(8,128)S(1)}, f32[224,896]{1,0:T(8,128)S(1)}, u32[]{:S(2)}, u32[]{:S(2)}) collective-permute-start(f32[224,896]{1,0:T(8,128)S(1)} %collective-permute-done.43), channel_id=1, source_target_pairs={{0,4},{8,0},{16,8},{24,16},{28,24},{20,28},{12,20},{4,12},{1,5},{9... | collective-permute-start | bytes 2408456 | tf_op jit(solution)/shard_map/ppermute | solution.py:27
  443.6 17.8 %collective-permute-start.46 = (f32[224,896]{1,0:T(8,128)S(1)}, f32[224,896]{1,0:T(8,128)S(1)}, u32[]{:S(2)}, u32[]{:S(2)}) collective-permute-start(f32[224,896]{1,0:T(8,128)S(1)} %collective-permute-done.44), channel_id=1, source_target_pairs={{0,8},{8,16},{16,24},{24,28},{28,20},{20,12},{12,4},{4,0},{1,9},{9... | collective-permute-start | bytes 2408456 | tf_op jit(solution)/shard_map/ppermute | solution.py:27
  444.2 17.4 %collective-permute-start.47 = (f32[224,896]{1,0:T(8,128)S(1)}, f32[224,896]{1,0:T(8,128)S(1)}, u32[]{:S(2)}, u32[]{:S(2)}) collective-permute-start(f32[224,896]{1,0:T(8,128)S(1)} %collective-permute-done.45), channel_id=1, source_target_pairs={{0,4},{8,0},{16,8},{24,16},{28,24},{20,28},{12,20},{4,12},{1,5},{9... | collective-permute-start | bytes 2408456 | tf_op jit(solution)/shard_map/ppermute | solution.py:27
  461.6 18.1 %collective-permute-start.48 = (f32[224,896]{1,0:T(8,128)S(1)}, f32[224,896]{1,0:T(8,128)S(1)}, u32[]{:S(2)}, u32[]{:S(2)}) collective-permute-start(f32[224,896]{1,0:T(8,128)S(1)} %collective-permute-done.46), channel_id=1, source_target_pairs={{0,8},{8,16},{16,24},{24,28},{28,20},{20,12},{12,4},{4,0},{1,9},{9... | collective-permute-start | bytes 2408456 | tf_op jit(solution)/shard_map/ppermute | solution.py:27
  462.3 17.8 %collective-permute-start.49 = (f32[224,896]{1,0:T(8,128)S(1)}, f32[224,896]{1,0:T(8,128)S(1)}, u32[]{:S(2)}, u32[]{:S(2)}) collective-permute-start(f32[224,896]{1,0:T(8,128)S(1)} %collective-permute-done.47), channel_id=1, source_target_pairs={{0,4},{8,0},{16,8},{24,16},{28,24},{20,28},{12,20},{4,12},{1,5},{9... | collective-permute-start | bytes 2408456 | tf_op jit(solution)/shard_map/ppermute | solution.py:27
  480.1 13.4 %collective-permute-start.50 = (f32[224,896]{1,0:T(8,128)S(1)}, f32[224,896]{1,0:T(8,128)S(1)}, u32[]{:S(2)}, u32[]{:S(2)}) collective-permute-start(f32[224,896]{1,0:T(8,128)S(1)} %collective-permute-done.48), channel_id=1, source_target_pairs={{0,8},{8,16},{16,24},{24,28},{28,20},{20,12},{12,4},{4,0},{1,9},{9... | collective-permute-start | bytes 2408456 | tf_op jit(solution)/shard_map/ppermute | solution.py:27
  480.7 13.2 %collective-permute-start.51 = (f32[224,896]{1,0:T(8,128)S(1)}, f32[224,896]{1,0:T(8,128)S(1)}, u32[]{:S(2)}, u32[]{:S(2)}) collective-permute-start(f32[224,896]{1,0:T(8,128)S(1)} %collective-permute-done.49), channel_id=1, source_target_pairs={{0,4},{8,0},{16,8},{24,16},{28,24},{20,28},{12,20},{4,12},{1,5},{9... | collective-permute-start | bytes 2408456 | tf_op jit(solution)/shard_map/ppermute | solution.py:27
  499.1 3.8 collective-permute-start.53
  499.1 37.7 %collective-permute-start.52 = (f32[448,896]{1,0:T(8,128)}, f32[448,896]{1,0:T(8,128)S(1)}, u32[]{:S(2)}, u32[]{:S(2)}) collective-permute-start(f32[448,896]{1,0:T(8,128)} %copy.37), channel_id=1, source_target_pairs={{0,2},{1,3},{2,0},{3,1},{4,6},{5,7},{6,4},{7,5},{8,10},{9,11},{10,... | collective-permute-start | bytes 4816904 | tf_op jit(solution)/shard_map/ppermute | solution.py:32
  536.8 3.6 collective-permute-start.54
  (59 other events, 571.3 us)
